TPU v7x, 128 devices: a whole 4x4x4 slice. The times are simulated.
128 devices in a mesh: sec: 4 (over x), tile: 32 (over y, z, core).
Axes of the slice: x: 4, y: 4, z: 4, core: 2. Of those that a mesh axis runs over, the one named last changes fastest.
Arguments:
- strips: bfloat16 [4, 512, 256, 256], P('sec', 'tile'), may hold values from -6 to 6
- partner_tile: int32 [4, 512], P('sec'), may hold values from 0 to 31, as said below
- partner_strip: int32 [4, 512], P('sec'), may hold values from 0 to 15
- adjacency: int32 [6, 4, 512], P(None, 'sec', 'tile'), may hold values from 0 to 511
- start_positions: float32 [2, 4, 512], P(None, 'sec', 'tile'), may hold values from -6 to 6
Outputs:
- plane_flow: float32 [2, 4, 512], P(None, 'sec', 'tile')
- depth_flow: float32 [2, 4, 512], P(None, 'sec', 'tile')
- node_positions: float32 [2, 4, 512], P(None, 'sec', 'tile')
Inputs may be any that keep to these rules, and one draw needn't show every extreme that they name: `partner_tile`: within a section, the 16 strips of any one tile name any one tile at most 2 times, and some tile is named exactly 2 times by the strips of every tile.
All inputs are finite; a program needn't handle non-finite values.
Results may differ from a plain program's by a relative error of at most 0.024.
Values may be sent and summed in bfloat16 or wider, within the bound.
No kernel may reach another device: no remote copies, remote signals or barrier semaphores. Data moves between devices by JAX's collectives and lax.ppermute only.
A program may use at most 192 MiB of HBM per device.

v0:
```python
import math

import jax
import jax.numpy as jnp
from jax import lax
from jax.sharding import PartitionSpec as P

STEPS = 2


epsilon = 1e-06
relax_rate = 0.1


def shifted(x, axis, by):
    devices = lax.axis_size(axis)
    return lax.ppermute(x, axis, [(i, (i + by) % devices) for i in range(devices)])


def dft_tables(length):
    indices = jnp.arange(length, dtype=jnp.int32)
    phases = indices[:, None] * indices[None, :] % length
    angles = phases.astype(jnp.float32) * (2.0 * math.pi / length)
    return (jnp.cos(angles).astype(jnp.bfloat16), jnp.sin(angles).astype(jnp.bfloat16))


def forward_spectra(pixels, cosine, sine):
    right_cos = jnp.einsum(
        "mjk,kl->mjl", pixels, cosine, preferred_element_type=jnp.float32
    ).astype(jnp.bfloat16)
    right_sin = jnp.einsum("mjk,kl->mjl", pixels, sine, preferred_element_type=jnp.float32).astype(
        jnp.bfloat16
    )
    real_part = jnp.einsum(
        "jk,mkl->mjl", cosine, right_cos, preferred_element_type=jnp.float32
    ) - jnp.einsum("jk,mkl->mjl", sine, right_sin, preferred_element_type=jnp.float32)
    imag_part = -(
        jnp.einsum("jk,mkl->mjl", cosine, right_sin, preferred_element_type=jnp.float32)
        + jnp.einsum("jk,mkl->mjl", sine, right_cos, preferred_element_type=jnp.float32)
    )
    return jnp.stack([real_part, imag_part], 1).astype(jnp.bfloat16)


def pair_flows(firsts, seconds, cosine, sine):
    length = firsts.shape[-1]
    first_re = firsts[:, 0].astype(jnp.float32)
    first_im = firsts[:, 1].astype(jnp.float32)
    second_re = seconds[:, 0].astype(jnp.float32)
    second_im = seconds[:, 1].astype(jnp.float32)
    cross_re = (first_re * second_re + first_im * second_im).astype(jnp.bfloat16)
    cross_im = (first_re * second_im - first_im * second_re).astype(jnp.bfloat16)
    upper_re = (
        jnp.einsum("jk,mkl->mjl", cosine, cross_re, preferred_element_type=jnp.float32)
        - jnp.einsum("jk,mkl->mjl", sine, cross_im, preferred_element_type=jnp.float32)
    ).astype(jnp.bfloat16)
    upper_im = (
        jnp.einsum("jk,mkl->mjl", cosine, cross_im, preferred_element_type=jnp.float32)
        + jnp.einsum("jk,mkl->mjl", sine, cross_re, preferred_element_type=jnp.float32)
    ).astype(jnp.bfloat16)
    surface = jnp.einsum(
        "mjk,kl->mjl", upper_re, cosine, preferred_element_type=jnp.float32
    ) - jnp.einsum("mjk,kl->mjl", upper_im, sine, preferred_element_type=jnp.float32)
    weights = surface * surface
    offsets = ((jnp.arange(length, dtype=jnp.int32) + length // 2) % length - length // 2).astype(
        jnp.float32
    )
    total = jnp.mean(weights, axis=(1, 2)) + epsilon
    along_rows = jnp.mean(weights * offsets[None, :, None], axis=(1, 2)) / total
    along_cols = jnp.mean(weights * offsets[None, None, :], axis=(1, 2)) / total
    return jnp.stack([along_rows, along_cols], 1)


def flows_in_blocks(firsts, seconds, cosine, sine):
    count = firsts.shape[0]
    block = math.gcd(count, 8)

    def shaped(values):
        return values.reshape((count // block, block) + values.shape[1:])

    def per_block(operands):
        return pair_flows(operands[0], operands[1], cosine, sine)

    results = lax.map(per_block, (shaped(firsts), shaped(seconds)))
    return results.reshape(count, 2)


def strip_ranks(dest_tiles):
    width = dest_tiles.shape[1]
    same_target = dest_tiles[:, :, None] == dest_tiles[:, None, :]
    positions = jnp.arange(width, dtype=jnp.int32)
    earlier = positions[None, :] < positions[:, None]
    return jnp.sum(same_target & earlier[None], axis=2)


def slot_table(dest_row, rank_row, target, values, capacity):
    slots = jnp.arange(capacity, dtype=jnp.int32)
    matched = (dest_row[None, :] == target) & (rank_row[None, :] == slots[:, None])
    return jnp.sum(jnp.where(matched, values[None, :], 0), axis=1)


def per_device(strips, partner_tile, partner_strip, adjacency, start_positions):
    tiles = lax.axis_size("tile")
    tile_index = lax.axis_index("tile")
    per_tile = strips.shape[1]
    length = strips.shape[2]
    capacity = max(2, 3 * per_tile // tiles)
    cosine, sine = dft_tables(length)
    own_spectra = forward_spectra(strips[0], cosine, sine)
    near_pixels = shifted(strips, "sec", -1)[0]
    near_spectra = forward_spectra(near_pixels, cosine, sine)
    depth_pairs = flows_in_blocks(near_spectra, own_spectra, cosine, sine)
    dest_tiles = partner_tile[0].reshape(tiles, per_tile)
    dest_strips = partner_strip[0].reshape(tiles, per_tile)
    ranks = strip_ranks(dest_tiles)
    my_dest = lax.dynamic_index_in_dim(dest_tiles, tile_index, 0, keepdims=False)
    my_rank = lax.dynamic_index_in_dim(ranks, tile_index, 0, keepdims=False)
    my_strip = lax.dynamic_index_in_dim(dest_strips, tile_index, 0, keepdims=False)
    asked = jax.vmap(
        lambda dest_row, rank_row, wanted: slot_table(
            dest_row, rank_row, tile_index, wanted, capacity
        )
    )(dest_tiles, ranks, dest_strips)
    pick_slot = my_dest * capacity + my_rank
    item_shape = own_spectra.shape[1:]
    strip_numbers = jnp.arange(per_tile, dtype=jnp.int32)
    targets = jnp.arange(tiles, dtype=jnp.int32)
    outgoing_index = jax.vmap(
        lambda target: slot_table(my_dest, my_rank, target, strip_numbers, capacity)
    )(targets)
    outgoing = jnp.take(own_spectra, outgoing_index.reshape(-1), axis=0).reshape(
        (tiles, capacity) + item_shape
    )
    incoming = lax.all_to_all(outgoing, "tile", split_axis=0, concat_axis=0, tiled=True)
    seconds = incoming.reshape((tiles * capacity,) + item_shape)
    firsts = jnp.take(own_spectra, asked.reshape(-1), axis=0)
    slot_flows = flows_in_blocks(firsts, seconds, cosine, sine)
    returned = lax.all_to_all(
        slot_flows.reshape(tiles, capacity, 2), "tile", split_axis=0, concat_axis=0, tiled=True
    )
    plane_pairs = jnp.take(returned.reshape(tiles * capacity, 2), pick_slot, axis=0)
    plane_out = plane_pairs.T
    depth_out = depth_pairs.T
    partner_global = my_dest * per_tile + my_strip
    links = adjacency[:, 0, :]
    neighbours = links.shape[0]
    current = start_positions[:, 0, :]
    for iteration in range(STEPS):
        whole = lax.all_gather(current[:, None, :], "tile", axis=2, tiled=True)[:, 0, :]
        near_nodes = shifted(current, "sec", -1)
        springs = jnp.sum(whole[:, links], axis=1) - neighbours * current
        force = (
            springs
            + (whole[:, partner_global] + plane_out - current)
            + (near_nodes + depth_out - current)
        )
        current = current + relax_rate * force
    return (plane_out[:, None, :], depth_out[:, None, :], current[:, None, :])


def solution(mesh):
    return jax.shard_map(
        per_device,
        mesh=mesh,
        in_specs=(
            P("sec", "tile", None, None),
            P("sec", None),
            P("sec", None),
            P(None, "sec", "tile"),
            P(None, "sec", "tile"),
        ),
        out_specs=(P(None, "sec", "tile"), P(None, "sec", "tile"), P(None, "sec", "tile")),
        check_vma=False,
    )
```

profile of v0, /device:TPU:1, one launch (start us, length us, event | category | flops | bytes accessed | tf_op | source)
XLA Modules:
  0.0 650.0 jit_solution(5297564235064521092)
XLA Ops:
  20.7 9.5 %gather_fusion.6 = bf16[64,2,256,256]{2,3,1,0:T(8,128)(2,1)} fusion(bf16[16,2,256,256]{2,3,0,1:T(8,128)(2,1)} %pad_maximum_fusion.2, s32[1024]{0:T(1024)S(1)} %pad_clamp_fusion.3), kind=kCustom, calls=%fused_computation.1.clone | custom fusion | bytes 33554688 | tf_op jit(solution)/shard_map/jit(_take)/gather | solution.py:130
  30.2 14.2 %broadcast_select_fusion = bf16[64,2,256,256]{2,3,1,0:T(8,128)(2,1)} fusion(bf16[64,2,256,256]{2,3,1,0:T(8,128)(2,1)} %gather_fusion.6, pred[64]{0:T(512)(128)(4,1)S(1)} %get-tuple-element.348), kind=kLoop, calls=%fused_computation.138 | loop fusion | flops 8388608 | bytes 33554496 | tf_op jit(solution)/shard_map/jit(_take)/select_n | solution.py:130
  44.4 22.5 %copy.267 = bf16[32,2,2,256,256]{4,3,2,1,0:T(8,128)(2,1)} copy(bf16[32,2,2,256,256]{3,4,2,1,0:T(8,128)(2,1)} %bitcast.321) | data formatting | bytes 33554432 | tf_op jit(solution)/shard_map/reshape | solution.py:130
  67.0 10.3 %all-to-all-start = ((bf16[32,2,2,256,256]{4,3,2,1,0:T(8,128)(2,1)}), bf16[32,2,2,256,256]{4,3,2,1,0:T(8,128)(2,1)}, u32[]{:S(2)}, u32[]{:S(2)}) async-start(bf16[32,2,2,256,256]{4,3,2,1,0:T(8,128)(2,1)} %copy.267), calls=%async_computation | async-start | bytes 33554432 | tf_op jit(solution)/shard_map/all_to_all | solution.py:133
  80.6 281.3 %all_gather.6 = f32[2,1,512]{0,2,1:T(8,128)S(1)} all-gather(f32[2,1,16]{0,2,1:T(8,128)S(1)} %copy.282), channel_id=1, replica_groups=mesh['sec'=4,'tile'=32] {'tile'}, dimensions={2}, use_global_device_ids=true | all-gather | bytes 4224 | tf_op jit(solution)/shard_map/all_gather | solution.py:148
  363.3 9.4 %gather_fusion.5 = bf16[64,2,256,256]{2,3,1,0:T(8,128)(2,1)} fusion(bf16[16,2,256,256]{2,3,0,1:T(8,128)(2,1)} %pad_maximum_fusion.2, s32[1024]{0:T(1024)S(1)} %pad_clamp_fusion.4), kind=kCustom, calls=%fused_computation.clone | custom fusion | bytes 33554688 | tf_op jit(solution)/shard_map/jit(_take)/gather | solution.py:135
  372.7 14.2 %broadcast_select_fusion.1 = bf16[64,2,256,256]{2,3,1,0:T(8,128)(2,1)} fusion(bf16[64,2,256,256]{2,3,1,0:T(8,128)(2,1)} %gather_fusion.5, pred[64]{0:T(512)(128)(4,1)S(1)} %get-tuple-element.349), kind=kLoop, calls=%fused_computation.139 | loop fusion | flops 8388608 | bytes 33554496 | tf_op jit(solution)/shard_map/jit(_take)/select_n | solution.py:135
  400.2 3.7 pad_maximum_fusion.3
  403.9 173.6 %while.28 = (s32[]{:T(128)}, f32[8,8,2]{1,0,2:T(8,128)S(1)}, bf16[8,8,2,256,256]{3,4,2,1,0:T(8,128)(2,1)}, bf16[8,8,2,256,256]{4,3,2,1,0:T(8,128)(2,1)}, s32[]{:T(128)}, /*index=5*/s32[]{:T(128)}) while((s32[]{:T(128)}, f32[8,8,2]{1,0,2:T(8,128)S(1)}, bf16[8,8,2,256,256]{3,4,2,1,0:T(8,128)(2,1)}, ...), condition=%wide.region_7.9_spmd.clone.clone, body=%wide.region_3.8_spmd.clone.clone.sunk | while | flops 1628573184 | bytes 44042896 | solution.py:83
  414.9 3.5 fusion.288
  421.1 4.5 multiply_reduce_fusion.6
  436.6 3.5 fusion.288
  442.8 4.5 multiply_reduce_fusion.6
  458.3 3.5 fusion.288
  464.5 4.5 multiply_reduce_fusion.6
  480.0 3.5 fusion.288
  486.1 4.5 multiply_reduce_fusion.6
  501.6 3.5 fusion.288
  507.8 4.5 multiply_reduce_fusion.6
  523.3 3.5 fusion.288
  529.5 4.5 multiply_reduce_fusion.6
  545.0 3.5 fusion.288
  551.2 4.5 multiply_reduce_fusion.6
  566.7 3.5 fusion.288
  572.8 4.5 multiply_reduce_fusion.6
  578.1 7.8 %all-to-all-start.1 = ((f32[32,2,2]{1,2,0:T(2,128)}), f32[32,2,2]{1,2,0:T(2,128)S(1)}, u32[]{:S(2)}, u32[]{:S(2)}) async-start(f32[32,2,2]{1,2,0:T(2,128)} %copy.271), calls=%async_computation.1 | async-start | bytes 65536 | tf_op jit(solution)/shard_map/all_to_all | solution.py:137
  585.9 33.2 %while.29 = (s32[]{:T(128)}, f32[2,8,2]{1,0,2:T(2,128)S(1)}, bf16[2,8,2,256,256]{3,4,1,2,0:T(8,128)(2,1)}, bf16[2,8,2,256,256]{3,4,1,2,0:T(8,128)(2,1)}, s32[]{:T(128)}, /*index=5*/s32[]{:T(128)}) while((s32[]{:T(128)}, f32[2,8,2]{1,0,2:T(2,128)S(1)}, bf16[2,8,2,256,256]{3,4,1,2,0:T(8,128)(2,1)}, ...), condition=%wide.region_12.14_spmd.clone.clone, body=%wide.region_8.13_spmd.clone.clone.sunk | while | flops 1628573184 | bytes 39848588 | solution.py:83
  591.8 3.5 fusion.303
  598.0 4.5 multiply_reduce_fusion.7
  608.4 3.5 fusion.303
  614.6 4.5 multiply_reduce_fusion.7
  622.8 24.8 %all-gather.1 = f32[32,16,2]{1,2,0:T(2,128)S(1)} all-gather(f32[1,16,2]{1,2,0:T(2,128)S(1)} %bitcast.339), channel_id=2, replica_groups=mesh['sec'=4,'tile'=32] {'tile'}, dimensions={0}, use_global_device_ids=true | all-gather | bytes 4224 | tf_op jit(solution)/shard_map/all_gather | solution.py:148
  (225 shorter events, 170.6 us)
Async XLA Ops:
  5.2 3.5 copy-start.6
  17.0 1.3 copy-start.4
  66.9 12.9 %copy-start.8 = (f32[2,1,16]{2,1,0:T(1,128)S(1)}, f32[2,1,16]{2,1,0:T(1,128)}, u32[]{:S(2)}) copy-start(f32[2,1,16]{2,1,0:T(1,128)} %param.15) | copy-start | bytes 388
  66.9 13.6 %copy-start.10 = (s32[6,1,16]{2,1,0:T(1,128)S(1)}, s32[6,1,16]{2,1,0:T(1,128)}, u32[]{:S(2)}) copy-start(s32[6,1,16]{2,1,0:T(1,128)} %param.14) | copy-start | bytes 1156
  67.0 336.9 %all-to-all-start = ((bf16[32,2,2,256,256]{4,3,2,1,0:T(8,128)(2,1)}), bf16[32,2,2,256,256]{4,3,2,1,0:T(8,128)(2,1)}, u32[]{:S(2)}, u32[]{:S(2)}) async-start(bf16[32,2,2,256,256]{4,3,2,1,0:T(8,128)(2,1)} %copy.267), calls=%async_computation | async-start | bytes 33554432 | tf_op jit(solution)/shard_map/all_to_all | solution.py:133
  77.2 309.7 %collective-permute-start = (bf16[1,16,256,256]{3,2,1,0:T(8,128)(2,1)}, bf16[1,16,256,256]{3,2,1,0:T(8,128)(2,1)}, u32[]{:S(2)}, u32[]{:S(2)}) collective-permute-start(bf16[1,16,256,256]{3,2,1,0:T(8,128)(2,1)} %param.11), channel_id=1, source_target_pairs={{0,96},{32,0},{64,32},{96,64},{1,97},{33,1},{65,33},{97,65},{2,98}... | collective-permute-start | bytes 6291464 | tf_op jit(solution)/shard_map/ppermute | solution.py:17
  79.8 540.4 %collective-permute-start.1 = (f32[2,16]{1,0:T(2,128)S(1)}, f32[2,16]{1,0:T(2,128)S(1)}, u32[]{:S(2)}, u32[]{:S(2)}) collective-permute-start(f32[2,16]{1,0:T(2,128)S(1)} %bitcast.340), channel_id=1, source_target_pairs={{0,96},{32,0},{64,32},{96,64},{1,97},{33,1},{65,33},{97,65},{2,98}... | collective-permute-start | bytes 392 | tf_op jit(solution)/shard_map/ppermute | solution.py:17
  398.5 1.7 copy-start.5
  412.6 1.0 copy-start
  418.4 2.7 copy-start.1
  434.3 1.0 copy-start
  440.1 2.7 copy-start.1
  455.9 1.0 copy-start
  461.8 2.7 copy-start.1
  477.6 1.0 copy-start
  483.5 2.7 copy-start.1
  499.3 1.0 copy-start
  505.1 2.7 copy-start.1
  521.0 1.0 copy-start
  526.8 2.7 copy-start.1
  542.7 1.0 copy-start
  548.5 2.7 copy-start.1
  564.3 1.0 copy-start
  570.2 2.7 copy-start.1
  578.1 41.1 %all-to-all-start.1 = ((f32[32,2,2]{1,2,0:T(2,128)}), f32[32,2,2]{1,2,0:T(2,128)S(1)}, u32[]{:S(2)}, u32[]{:S(2)}) async-start(f32[32,2,2]{1,2,0:T(2,128)} %copy.271), calls=%async_computation.1 | async-start | bytes 65536 | tf_op jit(solution)/shard_map/all_to_all | solution.py:137
  589.4 1.0 copy-start.2
  595.3 2.7 copy-start.3
  606.0 1.0 copy-start.2
  611.9 2.7 copy-start.3
  619.2 30.6 %copy-start.7 = (f32[16,2]{0,1:T(2,128)}, f32[16,2]{0,1:T(2,128)S(1)}, u32[]{:S(2)}) copy-start(f32[16,2]{0,1:T(2,128)S(1)} %reshape.401) | copy-start | bytes 388
  620.2 29.6 %copy-start.9 = (f32[16,2]{0,1:T(2,128)}, f32[16,2]{0,1:T(2,128)S(1)}, u32[]{:S(2)}) copy-start(f32[16,2]{0,1:T(2,128)S(1)} %get-tuple-element.335) | copy-start | bytes 388
  620.2 29.0 %collective-permute-start.2 = (f32[2,16]{1,0:T(2,128)S(1)}, f32[2,16]{1,0:T(2,128)S(1)}, u32[]{:S(2)}, u32[]{:S(2)}) collective-permute-start(f32[2,16]{1,0:T(2,128)S(1)} %get-tuple-element.334), channel_id=1, source_target_pairs={{0,96},{32,0},{64,32},{96,64},{1,97},{33,1},{65,33},{97,65},{2,98}... | collective-permute-start | bytes 392 | tf_op jit(solution)/shard_map/ppermute | solution.py:17
where the time goes:
time: 661 us; the launch traced here: 650 us
  blocking collectives  306 us (46%)
  matrix products  145 us (22%)
  local copies, waits for them, and re-layouts  126 us (19%)
  other arithmetic  46.6 us (7%)
  starting transfers between devices  23.9 us (4%)
    all_gather x2, blocking collectives, per_device(): lax.all_gather(current[:, None, :], 'tile', axis=2, tiled=True)[:, 0, :]  306 us
    dynamic_slice x16, local copies, waits for them, and re-layouts, flows_in_blocks(): results = lax.map(per_block, (shaped(firsts), shaped(seconds)))  47.8 us
    dot_general x10, matrix products, pair_flows(): jnp.einsum('mjk,kl->mjl', upper_im, sine, preferred_element_type=jnp.floa...  45.1 us
    dot_general x10, matrix products, pair_flows(): jnp.einsum('mjk,kl->mjl', upper_re, cosine, preferred_element_type=jnp.fl...  35 us
    dot_general x10, matrix products, pair_flows(): jnp.einsum('jk,mkl->mjl', cosine, cross_im, preferred_element_type=jnp.fl...  26.7 us
    reshape x1, local copies, waits for them, and re-layouts, per_device(): jnp.take(own_spectra, outgoing_index.reshape(-1), axis=0)  22.5 us
    squeeze x10, local copies, waits for them, and re-layouts, flows_in_blocks(): results = lax.map(per_block, (shaped(firsts), shaped(seconds)))  19.5 us
    select_n x2, other arithmetic, per_device(): jnp.take(own_spectra, outgoing_index.reshape(-1), axis=0)  14.2 us
  transfers between devices with their start and end apart: 5, of which 0 were waited for; matrix products, arithmetic and copies ran while one was open for 37% of the time, Pallas kernels for 0%

commit v1 on v0

v1 whole, which is shorter than its diff:
```python
import functools
import math

import jax
import jax.numpy as jnp
import numpy as np
from jax import lax
from jax.experimental import pallas as pl
from jax.experimental.pallas import tpu as pltpu
from jax.sharding import PartitionSpec as P

STEPS = 2


epsilon = 1e-06
relax_rate = 0.1


def shifted(x, axis, by):
    devices = lax.axis_size(axis)
    return lax.ppermute(x, axis, [(i, (i + by) % devices) for i in range(devices)])


def offsets_of(length):
    return ((np.arange(length) + length // 2) % length - length // 2).astype(np.float32)


def angles_of(length):
    indices = np.arange(length)
    return (indices[:, None] * indices[None, :] % length) * (2.0 * math.pi / length)


def half_tables(length):
    half = length // 2
    cosine, sine = np.cos(angles_of(length)), np.sin(angles_of(length))
    to_half = np.concatenate([cosine[:, :half], -sine[:, :half]], 1)
    to_half[:, half] = cosine[:, half]
    from_half = np.concatenate([2.0 * cosine[:half], -2.0 * sine[:half]], 0)
    from_half[0] = 1.0
    from_half[half] = cosine[half]
    both = np.concatenate([cosine, sine], 0)
    return tuple(jnp.asarray(table, jnp.bfloat16) for table in (to_half, both, from_half))


def dot(left, right):
    return jnp.dot(left, right, preferred_element_type=jnp.float32)


def spectrum_fields(image, to_half, both):
    length = image.shape[0]
    half = length // 2
    rows = dot(image, to_half).astype(jnp.bfloat16)
    mixed = dot(both, rows)
    cos_re, cos_im = mixed[:length, :half], mixed[:length, half:]
    sin_re, sin_im = mixed[length:, :half], mixed[length:, half:]
    first = lax.broadcasted_iota(jnp.int32, cos_re.shape, 1) == 0
    fields = (
        jnp.where(first, cos_re, cos_re + sin_im),
        jnp.where(first, sin_re, sin_re - cos_im),
        jnp.where(first, cos_im, 0.0),
        jnp.where(first, sin_im, 0.0),
    )
    return tuple(field.astype(jnp.bfloat16).astype(jnp.float32) for field in fields)


def cross_of(a, b):
    real = a[0] * b[0] + a[1] * b[1] + a[2] * b[3] - a[3] * b[2]
    imag = a[1] * b[0] - a[0] * b[1] + a[2] * b[2] + a[3] * b[3]
    return real.astype(jnp.bfloat16), imag.astype(jnp.bfloat16)


def pair_kernel(first_ref, second_ref, to_half_ref, both_ref, from_half_ref, offsets_ref, out_ref):
    length = first_ref.shape[-1]
    half = length // 2
    to_half, both = to_half_ref[...], both_ref[...]
    first = spectrum_fields(first_ref[0], to_half, both)
    second = spectrum_fields(second_ref[0], to_half, both)
    cross = jnp.concatenate(cross_of(first, second), 1)
    mixed = dot(both, cross)
    real = mixed[:length, :half] - mixed[length:, half:]
    imag = mixed[length:, :half] + mixed[:length, half:]
    upper = jnp.concatenate([real.astype(jnp.bfloat16), imag.astype(jnp.bfloat16)], 1)
    surface = dot(upper, from_half_ref[...])
    weights = surface * surface
    out_ref[0, 0:1, :] = jnp.sum(weights, axis=0, keepdims=True)
    out_ref[0, 1:2, :] = jnp.sum(weights * offsets_ref[...], axis=0, keepdims=True)


def pair_flows(firsts, seconds, tables):
    count, length = firsts.shape[0], firsts.shape[-1]
    to_half, both, from_half = tables
    offsets = offsets_of(length)
    whole = lambda table: pl.BlockSpec(table.shape, lambda i: (0, 0))
    image = pl.BlockSpec((1, length, length), lambda i: (i, 0, 0))
    spread = jnp.broadcast_to(jnp.asarray(offsets)[:, None], (length, length))
    sums = pl.pallas_call(
        pair_kernel,
        grid=(count,),
        in_specs=[image, image, whole(to_half), whole(both), whole(from_half), whole(spread)],
        out_specs=pl.BlockSpec((1, 8, length), lambda i: (i, 0, 0)),
        out_shape=jax.ShapeDtypeStruct((count, 8, length), jnp.float32),
        compiler_params=pltpu.CompilerParams(vmem_limit_bytes=32 * 1024 * 1024),
        cost_estimate=pl.CostEstimate(
            flops=count * 18 * length**3, bytes_accessed=count * 4 * length**2, transcendentals=0
        ),
        name="pair_flows",
    )(firsts, seconds, to_half, both, from_half, spread)
    cells = float(length * length)
    total = jnp.sum(sums[:, 0], axis=1) / cells + epsilon
    along_rows = jnp.sum(sums[:, 1], axis=1) / cells / total
    along_cols = jnp.sum(sums[:, 0] * offsets, axis=1) / cells / total
    return jnp.stack([along_rows, along_cols], 0)


def exchange(x):
    return lax.all_to_all(x, "tile", split_axis=0, concat_axis=0, tiled=True)


def gathered(values):
    tiles = lax.axis_size("tile")
    return exchange(jnp.broadcast_to(values[None], (tiles,) + values.shape))


def per_device(strips, partner_tile, partner_strip, adjacency, start_positions):
    tiles = lax.axis_size("tile")
    tile_index = lax.axis_index("tile")
    own = strips[0]
    per_tile, length = own.shape[0], own.shape[1]
    half_strips = per_tile // 2
    tables = half_tables(length)
    partner = partner_tile[0] * per_tile + partner_strip[0]

    near_low = shifted(own[:half_strips], "sec", -1)
    back_high = shifted(own[half_strips:], "sec", 1)

    slices = own.reshape(per_tile, tiles, length // tiles, length).transpose(1, 0, 2, 3)
    spread = exchange(slices).reshape(tiles * per_tile, length // tiles, length)
    picked = jnp.take(spread, partner, axis=0).reshape(slices.shape)
    partners = exchange(picked).transpose(1, 0, 2, 3).reshape(own.shape)

    firsts = jnp.concatenate([near_low, own[half_strips:]], 0)
    seconds = jnp.concatenate([own[:half_strips], back_high], 0)
    depth_pairs = pair_flows(firsts, seconds, tables)
    depth_out = jnp.concatenate(
        [depth_pairs[:, :half_strips], shifted(depth_pairs[:, half_strips:], "sec", -1)], 1
    )
    plane_out = pair_flows(partners, own, tables)

    my_partner = lax.dynamic_slice_in_dim(partner, tile_index * per_tile, per_tile, 0)
    links = adjacency[:, 0, :]
    neighbours = links.shape[0]
    current = start_positions[:, 0, :]
    for iteration in range(STEPS):
        whole = gathered(current).transpose(1, 0, 2).reshape(2, tiles * per_tile)
        near_nodes = shifted(current, "sec", -1)
        springs = jnp.sum(whole[:, links], axis=1) - neighbours * current
        force = (
            springs
            + (whole[:, my_partner] + plane_out - current)
            + (near_nodes + depth_out - current)
        )
        current = current + relax_rate * force
    return (plane_out[:, None, :], depth_out[:, None, :], current[:, None, :])


def solution(mesh):
    return jax.shard_map(
        per_device,
        mesh=mesh,
        in_specs=(
            P("sec", "tile", None, None),
            P("sec", None),
            P("sec", None),
            P(None, "sec", "tile"),
            P(None, "sec", "tile"),
        ),
        out_specs=(P(None, "sec", "tile"), P(None, "sec", "tile"), P(None, "sec", "tile")),
        check_vma=False,
    )
```

time: 661 us -> 147 us (0.22); the launches traced: 650 us -> 146 us
  blocking collectives: 306 us -> 0 us
  matrix products: 145 us -> 0 us
  local copies, waits for them, and re-layouts: 126 us -> 14.2 us
  waiting for transfers between devices: 0.01 us -> 54.6 us
  other arithmetic: 46.6 us -> 8.28 us
  Pallas kernels: 0 us -> 31.3 us
  starting transfers between devices: 23.9 us -> 37.1 us
    all_gather x2 -> x0, blocking collectives: 306 us -> none  [per_device(): lax.all_gather(current[:, None, :], 'tile', axis=2, tiled=True)[:, 0, :]]
    dot_general x52 -> x0, matrix products: 145 us -> none  [the longest x10 45.1 us: pair_flows(): jnp.einsum('mjk,kl->mjl', upper_im, sine, preferred_element_type=jnp.floa...]
    dynamic_slice x16 -> x0, local copies, waits for them, and re-layouts: 47.8 us -> none  [flows_in_blocks(): results = lax.map(per_block, (shaped(firsts), shaped(seconds)))]
    all_to_all x2 -> x4, waiting for transfers between devices: 0.01 us -> 33.4 us  [exchange(): return lax.all_to_all(x, 'tile', split_axis=0, concat_axis=0, tiled=True)]
    pallas_call x0 -> x2, Pallas kernels: none -> 31.3 us  [pair_flows(): pl.pallas_call(pair_kernel, grid=(count,), in_specs=[image, image, whole(...]
    select_n x5 -> x3, other arithmetic: 28.4 us -> 3.01 us  [the longest x2 2.94 us: per_device(): picked = jnp.take(spread, partner, axis=0).reshape(slices.shape)]
    reshape x5 -> x1, local copies, waits for them, and re-layouts: 23.1 us -> 1.79 us  [per_device(): partners = exchange(picked).transpose(1, 0, 2, 3).reshape(own.shape)]
    ppermute x3 -> x5, waiting for transfers between devices: 0.01 us -> 21.1 us  [shifted(): lax.ppermute(x, axis, [(i, (i + by) % devices) for i in range(devices)])]
  transfers between devices with their start and end apart: 5 -> 9, of which waited for: 0 -> 5; matrix products, arithmetic and copies ran while one was open for 37% -> 12% of each run, Pallas kernels for 0% -> 21%
where the time goes in v1:
time: 147 us; the launch traced here: 146 us
  waiting for transfers between devices  54.6 us (37%)
  starting transfers between devices  37.1 us (25%)
  Pallas kernels  31.3 us (21%)
  local copies, waits for them, and re-layouts  14.2 us (10%)
  other arithmetic  8.28 us (6%)
    all_to_all x4, waiting for transfers between devices, exchange(): return lax.all_to_all(x, 'tile', split_axis=0, concat_axis=0, tiled=True)  33.4 us
    pallas_call x2, Pallas kernels, pair_flows(): pl.pallas_call(pair_kernel, grid=(count,), in_specs=[image, image, whole(...  31.3 us
    all_to_all x4, starting transfers between devices, exchange(): return lax.all_to_all(x, 'tile', split_axis=0, concat_axis=0, tiled=True)  29.3 us
    ppermute x5, waiting for transfers between devices, shifted(): lax.ppermute(x, axis, [(i, (i + by) % devices) for i in range(devices)])  21.1 us
    ppermute x5, starting transfers between devices, shifted(): lax.ppermute(x, axis, [(i, (i + by) % devices) for i in range(devices)])  7.77 us
    transpose x1, local copies, waits for them, and re-layouts, per_device(): own.reshape(per_tile, tiles, length // tiles, length).transpose(1, 0, 2, 3)  3.18 us
    select_n x2, other arithmetic, per_device(): picked = jnp.take(spread, partner, axis=0).reshape(slices.shape)  2.94 us
  transfers between devices with their start and end apart: 9, of which 5 were waited for; matrix products, arithmetic and copies ran while one was open for 12% of the time, Pallas kernels for 21%

profile of v1, /device:TPU:1, one launch (start us, length us, event | category | flops | bytes accessed | tf_op | source)
XLA Modules:
  0.0 146.3 jit_solution(245492213933201070)
XLA Ops:
  0.6 3.2 %copy.97 = bf16[32,16,8,256]{3,2,1,0:T(8,128)(2,1)} copy(bf16[32,16,8,256]{3,2,0,1:T(8,128)(2,1)} %bitcast.88) | data formatting | bytes 4194304 | tf_op jit(solution)/shard_map/transpose | solution.py:136
  3.8 9.7 %all-to-all-start = ((bf16[32,16,8,256]{3,2,1,0:T(8,128)(2,1)}), bf16[32,16,8,256]{3,2,1,0:T(8,128)(2,1)S(1)}, u32[]{:S(2)}, u32[]{:S(2)}) async-start(bf16[32,16,8,256]{3,2,1,0:T(8,128)(2,1)} %copy.97), calls=%async_computation | async-start | bytes 4194304 | tf_op jit(solution)/shard_map/all_to_all | solution.py:116
  13.6 0.5 broadcast.237
  14.1 0.7 fusion.18
  14.9 27.0 %all-to-all-done = bf16[32,16,8,256]{3,2,1,0:T(8,128)(2,1)S(1)} async-done(((bf16[32,16,8,256]{3,2,1,0:T(8,128)(2,1)}), bf16[32,16,8,256]{3,2,1,0:T(8,128)(2,1)S(1)}, u32[]{:S(2)}, u32[]{:S(2)}) %all-to-all-start) | async-done | bytes 2097184 | tf_op jit(solution)/shard_map/all_to_all | solution.py:116
  41.9 0.6 broadcast_in_dim.56
  42.5 4.4 %all-to-all-start.2 = ((f32[32,2,16]{2,1,0:T(2,128)}), f32[32,2,16]{2,1,0:T(2,128)S(1)}, u32[]{:S(2)}, u32[]{:S(2)}) async-start(f32[32,2,16]{2,1,0:T(2,128)} %broadcast_in_dim.56), calls=%async_computation.2 | async-start | bytes 65536 | tf_op jit(solution)/shard_map/all_to_all | solution.py:116
  46.8 2.7 %gather_fusion = bf16[512,8,256]{2,1,0:T(8,128)(2,1)} fusion(bf16[512,8,256]{2,1,0:T(8,128)(2,1)S(1)} %bitcast.90, s32[1024]{0:T(1024)S(1)} %pad_clamp_fusion.2), kind=kCustom, calls=%fused_computation | custom fusion | bytes 4196352 | tf_op jit(solution)/shard_map/jit(_take)/gather | solution.py:138
  49.5 2.9 %broadcast_select_fusion = bf16[32,16,8,256]{3,2,1,0:T(8,128)(2,1)} fusion(bf16[32,16,8,256]{3,2,1,0:T(8,128)(2,1)} %bitcast.91, pred[32,16]{1,0:T(8,128)(4,1)S(1)} %compare_and_fusion), kind=kLoop, calls=%fused_computation.8 | loop fusion | flops 1048576 | bytes 4194816 | tf_op jit(solution)/shard_map/jit(_take)/select_n | solution.py:138
  52.5 1.7 %all-to-all-done.2 = f32[32,2,16]{2,1,0:T(2,128)S(1)} async-done(((f32[32,2,16]{2,1,0:T(2,128)}), f32[32,2,16]{2,1,0:T(2,128)S(1)}, u32[]{:S(2)}, u32[]{:S(2)}) %all-to-all-start.2) | async-done | bytes 4128 | tf_op jit(solution)/shard_map/all_to_all | solution.py:116
  54.2 6.0 %all-to-all-start.1 = ((bf16[32,16,8,256]{3,2,1,0:T(8,128)(2,1)}), bf16[32,16,8,256]{3,2,1,0:T(8,128)(2,1)}, u32[]{:S(2)}, u32[]{:S(2)}) async-start(bf16[32,16,8,256]{3,2,1,0:T(8,128)(2,1)} %broadcast_select_fusion), calls=%async_computation.1 | async-start | bytes 4194304 | tf_op jit(solution)/shard_map/all_to_all | solution.py:116
  60.2 1.1 slice_bitcast_fusion.1
  61.3 1.2 collective-permute-start.1
  62.6 1.5 %collective-permute-start = (bf16[8,256,256]{2,1,0:T(8,128)(2,1)}, bf16[8,256,256]{2,1,0:T(8,128)(2,1)}, u32[]{:S(2)}, u32[]{:S(2)}) collective-permute-start(bf16[8,256,256]{2,1,0:T(8,128)(2,1)} %get-tuple-element.31), channel_id=1, source_target_pairs={{0,96},{32,0},{64,32},{96,64},{1,97},{33,1},{65,33},{97,65},{2,98}... | collective-permute-start | bytes 3145736 | tf_op jit(solution)/shard_map/ppermute | solution.py:21
  64.0 1.3 collective-permute-start.3
  65.8 0.6 gather_fusion.2
  66.4 0.6 gather_fusion.1
  67.1 20.0 %collective-permute-done.1 = bf16[8,256,256]{2,1,0:T(8,128)(2,1)} collective-permute-done((bf16[8,256,256]{2,1,0:T(8,128)(2,1)S(1)}, bf16[8,256,256]{2,1,0:T(8,128)(2,1)}, u32[]{:S(2)}, u32[]{:S(2)}) %collective-permute-start.1) | collective-permute-done | bytes 1048608 | tf_op jit(solution)/shard_map/ppermute | solution.py:21
  87.1 1.7 %pad_maximum_fusion.1.second_ref = bf16[16,256,256]{2,1,0:T(8,128)(2,1)S(1)} fusion(bf16[8,256,256]{2,1,0:T(8,128)(2,1)} %collective-permute-done.1, bf16[8,256,256]{2,1,0:T(8,128)(2,1)} %get-tuple-element.31), kind=kLoop, calls=%fused_computation.6 | loop fusion | flops 1048576 | bytes 4194304 | tf_op jit(solution)/shard_map/concatenate | solution.py:142
  88.9 1.8 %pad_maximum_fusion.first_ref = bf16[16,256,256]{2,1,0:T(8,128)(2,1)S(1)} fusion(bf16[8,256,256]{2,1,0:T(8,128)(2,1)} %copy-done.4, bf16[8,256,256]{2,1,0:T(8,128)(2,1)} %collective-permute-done), kind=kLoop, calls=%fused_computation.5 | loop fusion | flops 1048576 | bytes 4194304 | tf_op jit(solution)/shard_map/concatenate | solution.py:141
  90.8 15.7 %pair_flows.3 = f32[16,8,256]{2,1,0:T(8,128)S(1)} custom-call(bf16[16,256,256]{2,1,0:T(8,128)(2,1)S(1)} %pad_maximum_fusion.first_ref, bf16[16,256,256]{2,1,0:T(8,128)(2,1)S(1)} %pad_maximum_fusion.1.second_ref, bf16[256,256]{1,0:T(8,128)(2,1)S(1)} %copy-done.2, bf16[512,256]{1,0:T(8,128)(2,1)S(1)} %copy-done.1, bf16[256,256]{1,0:T(8,128)(2,1)S(1)} %copy-done.3, ...), custom_call_target="tpu_custom_call" | custom-call | flops 4831838208 | bytes 4194304 | tf_op jit(solution)/shard_map/pair_flows/pallas_call | solution.py:96
  106.5 1.8 %copy_bitcast_fusion.first_ref = bf16[16,256,256]{2,1,0:T(8,128)(2,1)S(1)} fusion(bf16[32,16,8,256]{3,2,1,0:T(8,128)(2,1)} %all-to-all-done.1), kind=kLoop, calls=%fused_computation.7 | loop fusion | bytes 4194304 | tf_op jit(solution)/shard_map/reshape | solution.py:139
  108.3 15.7 %pair_flows.2 = f32[16,8,256]{2,1,0:T(8,128)S(1)} custom-call(bf16[16,256,256]{2,1,0:T(8,128)(2,1)S(1)} %copy_bitcast_fusion.first_ref, bf16[16,256,256]{2,1,0:T(8,128)(2,1)S(1)} %bitcast.89, bf16[256,256]{1,0:T(8,128)(2,1)S(1)} %copy-done.2, bf16[512,256]{1,0:T(8,128)(2,1)S(1)} %copy-done.1, bf16[256,256]{1,0:T(8,128)(2,1)S(1)} %copy-done.3, ...), custom_call_target="tpu_custom_call" | custom-call | flops 4831838208 | bytes 4194304 | tf_op jit(solution)/shard_map/pair_flows/pallas_call | solution.py:96
  124.4 1.3 collective-permute-start.2
  125.7 1.1 collective-permute-done.2
  126.9 0.6 broadcast_in_dim.58
  127.5 9.3 %all-to-all-start.3 = ((f32[32,2,16]{2,1,0:T(2,128)}), f32[32,2,16]{2,1,0:T(2,128)S(1)}, u32[]{:S(2)}, u32[]{:S(2)}) async-start(f32[32,2,16]{2,1,0:T(2,128)} %broadcast_in_dim.58), calls=%async_computation.3 | async-start | bytes 65536 | tf_op jit(solution)/shard_map/all_to_all | solution.py:116
  136.8 2.6 %collective-permute-start.4 = (f32[2,16]{1,0:T(2,128)S(1)}, f32[2,16]{1,0:T(2,128)S(1)}, u32[]{:S(2)}, u32[]{:S(2)}) collective-permute-start(f32[2,16]{1,0:T(2,128)S(1)} %get-tuple-element.27), channel_id=1, source_target_pairs={{0,96},{32,0},{64,32},{96,64},{1,97},{33,1},{65,33},{97,65},{2,98}... | collective-permute-start | bytes 392 | tf_op jit(solution)/shard_map/ppermute | solution.py:21
  139.4 4.7 %all-to-all-done.3 = f32[32,2,16]{2,1,0:T(2,128)S(1)} async-done(((f32[32,2,16]{2,1,0:T(2,128)}), f32[32,2,16]{2,1,0:T(2,128)S(1)}, u32[]{:S(2)}, u32[]{:S(2)}) %all-to-all-start.3) | async-done | bytes 4128 | tf_op jit(solution)/shard_map/all_to_all | solution.py:116
  144.4 0.6 gather_fusion.3
  145.0 0.6 gather_fusion.4
  145.7 0.6 fusion.8
  (51 shorter events, 1.8 us)
Async XLA Ops:
  3.8 10.3 %copy-start.9 = (s32[1,512]{1,0:T(1,128)S(1)}, s32[1,512]{1,0:T(1,128)}, u32[]{:S(2)}) copy-start(s32[1,512]{1,0:T(1,128)} %param.12) | copy-start | bytes 6148
  3.8 10.3 %copy-start.10 = (s32[1,512]{1,0:T(1,128)S(1)}, s32[1,512]{1,0:T(1,128)}, u32[]{:S(2)}) copy-start(s32[1,512]{1,0:T(1,128)} %param.11) | copy-start | bytes 6148
  3.8 38.0 %copy-start.6 = (f32[2,1,16]{2,1,0:T(1,128)S(1)}, f32[2,1,16]{2,1,0:T(1,128)}, u32[]{:S(2)}) copy-start(f32[2,1,16]{2,1,0:T(1,128)} %param.14) | copy-start | bytes 388
  3.8 38.0 %all-to-all-start = ((bf16[32,16,8,256]{3,2,1,0:T(8,128)(2,1)}), bf16[32,16,8,256]{3,2,1,0:T(8,128)(2,1)S(1)}, u32[]{:S(2)}, u32[]{:S(2)}) async-start(bf16[32,16,8,256]{3,2,1,0:T(8,128)(2,1)} %copy.97), calls=%async_computation | async-start | bytes 4194304 | tf_op jit(solution)/shard_map/all_to_all | solution.py:116
  42.5 11.7 %all-to-all-start.2 = ((f32[32,2,16]{2,1,0:T(2,128)}), f32[32,2,16]{2,1,0:T(2,128)S(1)}, u32[]{:S(2)}, u32[]{:S(2)}) async-start(f32[32,2,16]{2,1,0:T(2,128)} %broadcast_in_dim.56), calls=%async_computation.2 | async-start | bytes 65536 | tf_op jit(solution)/shard_map/all_to_all | solution.py:116
  52.5 7.7 %copy-start = (bf16[1,16,256,256]{3,2,1,0:T(8,128)(2,1)S(1)}, bf16[1,16,256,256]{3,2,1,0:T(8,128)(2,1)}, u32[]{:S(2)}) copy-start(bf16[1,16,256,256]{3,2,1,0:T(8,128)(2,1)} %param.10) | copy-start | bytes 6291460
  54.2 52.3 %all-to-all-start.1 = ((bf16[32,16,8,256]{3,2,1,0:T(8,128)(2,1)}), bf16[32,16,8,256]{3,2,1,0:T(8,128)(2,1)}, u32[]{:S(2)}, u32[]{:S(2)}) async-start(bf16[32,16,8,256]{3,2,1,0:T(8,128)(2,1)} %broadcast_select_fusion), calls=%async_computation.1 | async-start | bytes 4194304 | tf_op jit(solution)/shard_map/all_to_all | solution.py:116
  60.2 5.1 %copy-start.8 = (s32[6,1,16]{2,1,0:T(1,128)S(1)}, s32[6,1,16]{2,1,0:T(1,128)}, u32[]{:S(2)}) copy-start(s32[6,1,16]{2,1,0:T(1,128)} %param.13) | copy-start | bytes 1156
  61.3 25.8 %copy-start.4 = (bf16[8,256,256]{2,1,0:T(8,128)(2,1)}, bf16[8,256,256]{2,1,0:T(8,128)(2,1)S(1)}, u32[]{:S(2)}) copy-start(bf16[8,256,256]{2,1,0:T(8,128)(2,1)S(1)} %get-tuple-element.32) | copy-start | bytes 3145732
  61.3 25.8 %collective-permute-start.1 = (bf16[8,256,256]{2,1,0:T(8,128)(2,1)S(1)}, bf16[8,256,256]{2,1,0:T(8,128)(2,1)}, u32[]{:S(2)}, u32[]{:S(2)}) collective-permute-start(bf16[8,256,256]{2,1,0:T(8,128)(2,1)S(1)} %get-tuple-element.32), channel_id=1, source_target_pairs={{0,32},{32,64},{64,96},{96,0},{1,33},{33,65},{65,97},{97,1},{2,34}... | collective-permute-start | bytes 3145736 | tf_op jit(solution)/shard_map/ppermute | solution.py:21
  62.6 26.3 %collective-permute-start = (bf16[8,256,256]{2,1,0:T(8,128)(2,1)}, bf16[8,256,256]{2,1,0:T(8,128)(2,1)}, u32[]{:S(2)}, u32[]{:S(2)}) collective-permute-start(bf16[8,256,256]{2,1,0:T(8,128)(2,1)} %get-tuple-element.31), channel_id=1, source_target_pairs={{0,96},{32,0},{64,32},{96,64},{1,97},{33,1},{65,33},{97,65},{2,98}... | collective-permute-start | bytes 3145736 | tf_op jit(solution)/shard_map/ppermute | solution.py:21
  64.0 61.7 %collective-permute-start.3 = (f32[2,16]{1,0:T(2,128)S(1)}, f32[2,16]{1,0:T(2,128)S(1)}, u32[]{:S(2)}, u32[]{:S(2)}) collective-permute-start(f32[2,16]{1,0:T(2,128)S(1)} %bitcast.102), channel_id=1, source_target_pairs={{0,96},{32,0},{64,32},{96,64},{1,97},{33,1},{65,33},{97,65},{2,98}... | collective-permute-start | bytes 392 | tf_op jit(solution)/shard_map/ppermute | solution.py:21
  88.8 1.8 %copy-start.5 = (f32[256]{0:T(256)S(1)}, f32[256]{0:T(256)}, u32[]{:S(2)}) copy-start(f32[256]{0:T(256)} %constant.57.clone) | copy-start | bytes 3076
  88.8 1.9 %copy-start.1 = (bf16[512,256]{1,0:T(8,128)(2,1)S(1)}, bf16[512,256]{1,0:T(8,128)(2,1)}, u32[]{:S(2)}) copy-start(bf16[512,256]{1,0:T(8,128)(2,1)} %constant.55.clone.both_ref) | copy-start | bytes 786436
  88.9 1.9 %copy-start.2 = (bf16[256,256]{1,0:T(8,128)(2,1)S(1)}, bf16[256,256]{1,0:T(8,128)(2,1)}, u32[]{:S(2)}) copy-start(bf16[256,256]{1,0:T(8,128)(2,1)} %constant.54.clone.to_half_ref) | copy-start | bytes 393220
  88.9 1.9 %copy-start.3 = (bf16[256,256]{1,0:T(8,128)(2,1)S(1)}, bf16[256,256]{1,0:T(8,128)(2,1)}, u32[]{:S(2)}) copy-start(bf16[256,256]{1,0:T(8,128)(2,1)} %constant.56.clone.from_half_ref) | copy-start | bytes 393220
  124.4 2.4 %collective-permute-start.2 = (f32[2,8]{1,0:T(2,128)S(1)}, f32[2,8]{1,0:T(2,128)S(1)}, u32[]{:S(2)}, u32[]{:S(2)}) collective-permute-start(f32[2,8]{1,0:T(2,128)S(1)} %get-tuple-element.38), channel_id=1, source_target_pairs={{0,96},{32,0},{64,32},{96,64},{1,97},{33,1},{65,33},{97,65},{2,98}... | collective-permute-start | bytes 200 | tf_op jit(solution)/shard_map/ppermute | solution.py:21
  126.9 19.4 %copy-start.7 = (f32[2,16]{1,0:T(2,128)}, f32[2,16]{1,0:T(2,128)S(1)}, u32[]{:S(2)}) copy-start(f32[2,16]{1,0:T(2,128)S(1)} %get-tuple-element.28) | copy-start | bytes 388
  127.5 16.6 %all-to-all-start.3 = ((f32[32,2,16]{2,1,0:T(2,128)}), f32[32,2,16]{2,1,0:T(2,128)S(1)}, u32[]{:S(2)}, u32[]{:S(2)}) async-start(f32[32,2,16]{2,1,0:T(2,128)} %broadcast_in_dim.58), calls=%async_computation.3 | async-start | bytes 65536 | tf_op jit(solution)/shard_map/all_to_all | solution.py:116
  136.8 8.9 %collective-permute-start.4 = (f32[2,16]{1,0:T(2,128)S(1)}, f32[2,16]{1,0:T(2,128)S(1)}, u32[]{:S(2)}, u32[]{:S(2)}) collective-permute-start(f32[2,16]{1,0:T(2,128)S(1)} %get-tuple-element.27), channel_id=1, source_target_pairs={{0,96},{32,0},{64,32},{96,64},{1,97},{33,1},{65,33},{97,65},{2,98}... | collective-permute-start | bytes 392 | tf_op jit(solution)/shard_map/ppermute | solution.py:21

commit v2 on v1

v2 whole, which is shorter than its diff:
```python
import functools
import math

import jax
import jax.numpy as jnp
import numpy as np
from jax import lax
from jax.experimental import pallas as pl
from jax.experimental.pallas import tpu as pltpu
from jax.sharding import PartitionSpec as P

STEPS = 2


epsilon = 1e-06
relax_rate = 0.1


def shifted(x, axis, by):
    devices = lax.axis_size(axis)
    return lax.ppermute(x, axis, [(i, (i + by) % devices) for i in range(devices)])


def offsets_of(length):
    return ((np.arange(length) + length // 2) % length - length // 2).astype(np.float32)


def angles_of(length):
    indices = np.arange(length)
    return (indices[:, None] * indices[None, :] % length) * (2.0 * math.pi / length)


def half_tables(length):
    half = length // 2
    cosine, sine = np.cos(angles_of(length)), np.sin(angles_of(length))
    to_half = np.concatenate([cosine[:, :half], -sine[:, :half]], 1)
    to_half[:, half] = cosine[:, half]
    from_half = np.concatenate([2.0 * cosine[:half], -2.0 * sine[:half]], 0)
    from_half[0] = 1.0
    from_half[half] = cosine[half]
    both = np.concatenate([cosine, sine], 0)
    return tuple(jnp.asarray(table, jnp.bfloat16) for table in (to_half, both, from_half))


def dot(left, right):
    return jnp.dot(left, right, preferred_element_type=jnp.float32)


def mixed_by(both, halves):
    length, half = both.shape[1], both.shape[1] // 2
    mixed = dot(both, halves)
    return (
        mixed[:length, :half],
        mixed[:length, half:],
        mixed[length:, :half],
        mixed[length:, half:],
    )


def fields_of(images, to_half, both):
    rows = [dot(image, to_half).astype(jnp.bfloat16) for image in images]
    parts = [mixed_by(both, row) for row in rows]
    fields = []
    for cos_re, cos_im, sin_re, sin_im in parts:
        first = lax.broadcasted_iota(jnp.int32, cos_re.shape, 1) == 0
        fields.append(
            tuple(
                field.astype(jnp.bfloat16)
                for field in (
                    jnp.where(first, cos_re, cos_re + sin_im),
                    jnp.where(first, sin_re, sin_re - cos_im),
                    jnp.where(first, cos_im, 0.0),
                    jnp.where(first, sin_im, 0.0),
                )
            )
        )
    return fields


def cross_of(a, b):
    a = [field.astype(jnp.float32) for field in a]
    b = [field.astype(jnp.float32) for field in b]
    real = a[0] * b[0] + a[1] * b[1] + a[2] * b[3] - a[3] * b[2]
    imag = a[1] * b[0] - a[0] * b[1] + a[2] * b[2] + a[3] * b[3]
    return jnp.concatenate([real.astype(jnp.bfloat16), imag.astype(jnp.bfloat16)], 1)


def store_sums(pairs, both, from_half, offsets, out_ref):
    crosses = [cross_of(first, second) for first, second in pairs]
    parts = [mixed_by(both, cross) for cross in crosses]
    uppers = [
        jnp.concatenate(
            [(cos_re - sin_im).astype(jnp.bfloat16), (sin_re + cos_im).astype(jnp.bfloat16)], 1
        )
        for cos_re, cos_im, sin_re, sin_im in parts
    ]
    for k, upper in enumerate(uppers):
        surface = dot(upper, from_half)
        weights = surface * surface
        out_ref[k, 0:1, :] = jnp.sum(weights, axis=0, keepdims=True)
        out_ref[k, 1:2, :] = jnp.sum(weights * offsets, axis=0, keepdims=True)


def split_fields(packed):
    half = packed.shape[-1] // 2
    return packed[0, :, :half], packed[0, :, half:], packed[1, :, :half], packed[1, :, half:]


def spectra_kernel(images_ref, to_half_ref, both_ref, out_ref):
    count = images_ref.shape[0]
    images = [images_ref[k] for k in range(count)]
    for k, (a, b, c, d) in enumerate(fields_of(images, to_half_ref[...], both_ref[...])):
        out_ref[k, 0] = jnp.concatenate([a, b], 1)
        out_ref[k, 1] = jnp.concatenate([c, d], 1)


def joined(pieces, k):
    rows = pieces.shape[0] // 2
    return jnp.concatenate(
        [
            jnp.concatenate([pieces[2 * r, k], pieces[2 * r + 1, k]], 1)
            for r in range(rows)
        ],
        0,
    )


def pair_kernel(
    other_first, in_pieces, images_ref, fields_ref, to_half_ref, both_ref, from_half_ref, offsets_ref, out_ref
):
    count = fields_ref.shape[0]
    if in_pieces:
        images = [joined(images_ref, k) for k in range(count)]
    else:
        images = [images_ref[k] for k in range(count)]
    others = fields_of(images, to_half_ref[...], both_ref[...])
    owns = [split_fields(fields_ref[k]) for k in range(count)]
    pairs = [(x, y) if other_first else (y, x) for x, y in zip(others, owns)]
    store_sums(pairs, both_ref[...], from_half_ref[...], offsets_ref[...], out_ref)


def whole(table):
    return pl.BlockSpec(table.shape, lambda i: (0,) * table.ndim)


def call_params():
    return pltpu.CompilerParams(vmem_limit_bytes=60 * 1024 * 1024)


def spectra_of(images, tables, batch=4):
    count, length = images.shape[0], images.shape[-1]
    to_half, both, _ = tables
    return pl.pallas_call(
        spectra_kernel,
        grid=(count // batch,),
        in_specs=[
            pl.BlockSpec((batch, length, length), lambda i: (i, 0, 0)),
            whole(to_half),
            whole(both),
        ],
        out_specs=pl.BlockSpec((batch, 2, length, length), lambda i: (i, 0, 0, 0)),
        out_shape=jax.ShapeDtypeStruct((count, 2, length, length), jnp.bfloat16),
        compiler_params=call_params(),
        cost_estimate=pl.CostEstimate(
            flops=count * 6 * length**3, bytes_accessed=count * 6 * length**2, transcendentals=0
        ),
        name="spectra",
    )(images, to_half, both)


def pair_sums(images, fields, start, other_first, tables, batch=4):
    in_pieces = images.ndim == 4
    count = images.shape[1] if in_pieces else images.shape[0]
    length = fields.shape[-1]
    to_half, both, from_half = tables
    spread = jnp.broadcast_to(jnp.asarray(offsets_of(length))[:, None], (length, length))
    if in_pieces:
        image_block = pl.BlockSpec(
            (images.shape[0], batch) + images.shape[2:], lambda i: (0, i, 0, 0)
        )
    else:
        image_block = pl.BlockSpec((batch, length, length), lambda i: (i, 0, 0))
    return pl.pallas_call(
        functools.partial(pair_kernel, other_first, in_pieces),
        grid=(count // batch,),
        in_specs=[
            image_block,
            pl.BlockSpec((batch, 2, length, length), lambda i: (i + start // batch, 0, 0, 0)),
            whole(to_half),
            whole(both),
            whole(from_half),
            whole(spread),
        ],
        out_specs=pl.BlockSpec((batch, 8, length), lambda i: (i, 0, 0)),
        out_shape=jax.ShapeDtypeStruct((count, 8, length), jnp.float32),
        compiler_params=call_params(),
        cost_estimate=pl.CostEstimate(
            flops=count * 12 * length**3, bytes_accessed=count * 6 * length**2, transcendentals=0
        ),
        name="pair_sums",
    )(images, fields, to_half, both, from_half, spread)


def flows_of(sums):
    length = sums.shape[-1]
    cells = float(length * length)
    total = jnp.sum(sums[:, 0], axis=1) / cells + epsilon
    along_rows = jnp.sum(sums[:, 1], axis=1) / cells / total
    along_cols = jnp.sum(sums[:, 0] * offsets_of(length), axis=1) / cells / total
    return jnp.stack([along_rows, along_cols], 0)


def cut_kernel(images_ref, note_ref, out_ref, held, read_sems, write_sem):
    pieces, slots, rows, columns = out_ref.shape
    count = slots - 1
    across = images_ref.shape[2] // columns
    chunks = read_sems.shape[0]
    batch = count // chunks

    def read(chunk):
        strips = pl.ds(chunk * batch, batch)
        return pltpu.make_async_copy(images_ref.at[strips], held.at[strips], read_sems.at[chunk])

    for chunk in range(chunks):
        read(chunk).start()
    writes = []
    for piece in range(pieces):
        write = pltpu.make_async_copy(
            note_ref, out_ref.at[piece, count], write_sem.at[len(writes)]
        )
        write.start()
        writes.append(write)
    for chunk in range(chunks):
        read(chunk).wait()
        strips = pl.ds(chunk * batch, batch)
        for piece in range(pieces):
            r, c = piece // across, piece % across
            write = pltpu.make_async_copy(
                held.at[strips, pl.ds(r * rows, rows), pl.ds(c * columns, columns)],
                out_ref.at[piece, strips],
                write_sem.at[len(writes)],
            )
            write.start()
            writes.append(write)
    for write in writes:
        write.wait()


def cut(images, note, pieces, chunks=4):
    count, length = images.shape[0], images.shape[-1]
    shape = (pieces, count + 1, 2 * length // pieces, length // 2)
    return pl.pallas_call(
        cut_kernel,
        in_specs=[
            pl.BlockSpec(memory_space=pl.ANY),
            pl.BlockSpec(memory_space=pltpu.VMEM),
        ],
        out_specs=pl.BlockSpec(memory_space=pl.ANY),
        out_shape=jax.ShapeDtypeStruct(shape, images.dtype),
        scratch_shapes=[
            pltpu.VMEM(images.shape, images.dtype),
            pltpu.SemaphoreType.DMA((chunks,)),
            pltpu.SemaphoreType.DMA(((chunks + 1) * pieces,)),
        ],
        compiler_params=pltpu.CompilerParams(vmem_limit_bytes=60 * 1024 * 1024),
        name="cut",
    )(images, note)


def exchange(x):
    return lax.all_to_all(x, "tile", split_axis=0, concat_axis=0, tiled=True)


def gathered(values):
    tiles = lax.axis_size("tile")
    spread = exchange(jnp.broadcast_to(values[None], (tiles,) + values.shape))
    return spread.transpose(1, 0, 2).reshape(values.shape[0], -1)


def in_parts(values, rows, columns):
    parts = []
    rest = values
    for _ in range(3):
        part = lax.reduce_precision(rest, 8, 7)
        parts.append(part.astype(jnp.bfloat16))
        rest = rest - part
    stacked = jnp.concatenate(parts, 0)
    return jnp.pad(stacked, ((0, rows - stacked.shape[0]), (0, columns - stacked.shape[1])))


def from_parts(tiles, height, width):
    parts = tiles[:, : 3 * height, :width].astype(jnp.float32)
    parts = parts.reshape(tiles.shape[0], 3, height, width)
    values = (parts[:, 2] + parts[:, 1]) + parts[:, 0]
    return values.transpose(1, 0, 2).reshape(height, -1)


def per_device(strips, partner_tile, partner_strip, adjacency, start_positions):
    tiles = lax.axis_size("tile")
    tile_index = lax.axis_index("tile")
    own = strips[0]
    per_tile, length = own.shape[0], own.shape[1]
    half_strips = per_tile // 2
    tables = half_tables(length)
    partner = partner_tile[0] * per_tile + partner_strip[0]
    my_partner = lax.dynamic_slice_in_dim(partner, tile_index * per_tile, per_tile, 0)
    links = adjacency[:, 0, :]
    neighbours = links.shape[0]
    start = start_positions[:, 0, :]

    def pull(whole_positions, current, near):
        springs = jnp.sum(whole_positions[:, links], axis=1) - neighbours * current
        return springs + (whole_positions[:, my_partner] - current) + (near - current)

    partner_rows = partner_tile[0] * (per_tile + 1) + partner_strip[0]

    near_low = shifted(own[:half_strips], "sec", -1)
    back_high = shifted(own[half_strips:], "sec", 1)

    rows, columns = 2 * length // tiles, length // 2
    pieces = cut(own, in_parts(start, rows, columns), tiles)
    spread = exchange(pieces)
    fields = spectra_of(own, tables)
    spread, fields, partner_rows = lax.optimization_barrier((spread, fields, partner_rows))
    picked = spread.reshape((-1, rows, columns)).at[partner_rows].get(mode="promise_in_bounds")
    partners = exchange(picked.reshape(tiles, per_tile, rows, columns))

    whole_start = from_parts(spread[:, per_tile], *start.shape)
    first_pull = pull(whole_start, start, shifted(start, "sec", -1))
    low = flows_of(pair_sums(near_low, fields, 0, True, tables))
    high = flows_of(pair_sums(back_high, fields, half_strips, False, tables))
    depth_out = jnp.concatenate([low, shifted(high, "sec", -1)], 1)
    partners, depth_out, first_pull = lax.optimization_barrier((partners, depth_out, first_pull))

    plane_out = flows_of(pair_sums(partners, fields, 0, True, tables))
    current = start + relax_rate * (first_pull + plane_out + depth_out)
    for iteration in range(1, STEPS):
        force = pull(gathered(current), current, shifted(current, "sec", -1))
        current = current + relax_rate * (force + plane_out + depth_out)
    return (plane_out[:, None, :], depth_out[:, None, :], current[:, None, :])


def solution(mesh):
    return jax.shard_map(
        per_device,
        mesh=mesh,
        in_specs=(
            P("sec", "tile", None, None),
            P("sec", None),
            P("sec", None),
            P(None, "sec", "tile"),
            P(None, "sec", "tile"),
        ),
        out_specs=(P(None, "sec", "tile"), P(None, "sec", "tile"), P(None, "sec", "tile")),
        check_vma=False,
    )
```

time: 147 us -> 110 us (0.75)
  waiting for transfers between devices: 54.6 us -> 32.9 us
  starting transfers between devices: 37.1 us -> 29.1 us
  other arithmetic: 8.28 us -> 4.15 us
  Pallas kernels: 31.3 us -> 29.3 us
    ppermute x5, waiting for transfers between devices: 21.1 us -> 0.01 us  [shifted(): lax.ppermute(x, axis, [(i, (i + by) % devices) for i in range(devices)])]
    all_to_all x4 -> x3, starting transfers between devices: 29.3 us -> 18.8 us  [exchange(): return lax.all_to_all(x, 'tile', split_axis=0, concat_axis=0, tiled=True)]
    transpose x3 -> x2, local copies, waits for them, and re-layouts: 3.71 us -> 0.47 us  [the longest x1 0.26 us: gathered(): return spread.transpose(1, 0, 2).reshape(values.shape[0], -1)]
    select_n x4 -> x3, other arithmetic: 3.03 us -> 0.1 us  [the longest x1 0.08 us: pull(): whole_positions[:, my_partner] - current]
    concatenate x2, other arithmetic: 3.5 us -> 0.68 us  [the longest x1 0.6 us: in_parts(): stacked = jnp.concatenate(parts, 0)]
    ppermute x5, starting transfers between devices: 7.77 us -> 10.3 us  [shifted(): lax.ppermute(x, axis, [(i, (i + by) % devices) for i in range(devices)])]
    reduce_sum x4 -> x6, other arithmetic: 0.37 us -> 2.55 us  [the longest x2 2.27 us: flows_of(): along_rows = jnp.sum(sums[:, 1], axis=1) / cells / total]
    pallas_call x2 -> x5, Pallas kernels: 31.3 us -> 29.3 us  [the longest x3 19.1 us: pair_sums(): pl.pallas_call(functools.partial(pair_kernel, other_first, in_pieces), gr...]
  transfers between devices with their start and end apart: 9 -> 8, of which waited for: 5 -> 3; matrix products, arithmetic and copies ran while one was open for 12% -> 11% of each run, Pallas kernels for 21% -> 15%
where the time goes in v2:
time: 110 us; the launch traced here: 109 us
  waiting for transfers between devices  32.9 us (30%)
  Pallas kernels  29.3 us (27%)
  starting transfers between devices  29.1 us (26%)
  local copies, waits for them, and re-layouts  12.9 us (12%)
  other arithmetic  4.15 us (4%)
    all_to_all x3, waiting for transfers between devices, exchange(): return lax.all_to_all(x, 'tile', split_axis=0, concat_axis=0, tiled=True)  32.9 us
    pallas_call x3, Pallas kernels, pair_sums(): pl.pallas_call(functools.partial(pair_kernel, other_first, in_pieces), gr...  19.1 us
    all_to_all x3, starting transfers between devices, exchange(): return lax.all_to_all(x, 'tile', split_axis=0, concat_axis=0, tiled=True)  18.8 us
    ppermute x5, starting transfers between devices, shifted(): lax.ppermute(x, axis, [(i, (i + by) % devices) for i in range(devices)])  10.3 us
    pallas_call x1, Pallas kernels, spectra_of(): pl.pallas_call(spectra_kernel, grid=(count // batch,), in_specs=[pl.Block...  5.58 us
    pallas_call x1, Pallas kernels, cut(): pl.pallas_call(cut_kernel, in_specs=[pl.BlockSpec(memory_space=pl.ANY), p...  4.59 us
    gather x1, local copies, waits for them, and re-layouts, per_device(): spread.reshape((-1, rows, columns)).at[partner_rows]  4.04 us
    reduce_sum x2, other arithmetic, flows_of(): along_rows = jnp.sum(sums[:, 1], axis=1) / cells / total  2.27 us
  transfers between devices with their start and end apart: 8, of which 3 were waited for; matrix products, arithmetic and copies ran while one was open for 11% of the time, Pallas kernels for 15%

profile of v2, /device:TPU:1, one launch (start us, length us, event | category | flops | bytes accessed | tf_op | source)
XLA Modules:
  0.0 109.2 jit_solution(3486290956095661652)
XLA Ops:
  0.6 0.7 reduce-precision_convert_fusion.1
  1.3 0.6 fusion.22.note_ref
  1.9 4.6 %cut.1 = bf16[32,17,16,128]{3,2,1,0:T(8,128)(2,1)} custom-call(bf16[16,256,256]{2,1,0:T(8,128)(2,1)} %bitcast.91, bf16[16,128]{1,0:T(8,128)(2,1)} %fusion.22.note_ref), custom_call_target="tpu_custom_call" | custom-call | tf_op jit(solution)/shard_map/cut/pallas_call | solution.py:252
  6.5 9.8 %all-to-all-start = ((bf16[32,17,16,128]{3,2,1,0:T(8,128)(2,1)}), bf16[32,17,16,128]{3,2,1,0:T(8,128)(2,1)}, u32[]{:S(2)}, u32[]{:S(2)}) async-start(bf16[32,17,16,128]{3,2,1,0:T(8,128)(2,1)} %cut.1), calls=%async_computation | async-start | bytes 4456448 | tf_op jit(solution)/shard_map/all_to_all | solution.py:271
  16.4 2.5 %collective-permute-start.3 = (f32[2,16]{0,1:T(8,128)S(1)}, f32[2,16]{0,1:T(8,128)S(1)}, u32[]{:S(2)}, u32[]{:S(2)}) collective-permute-start(f32[2,16]{0,1:T(8,128)S(1)} %copy.77), channel_id=1, source_target_pairs={{0,96},{32,0},{64,32},{96,64},{1,97},{33,1},{65,33},{97,65},{2,98}... | collective-permute-start | bytes 392 | tf_op jit(solution)/shard_map/ppermute | solution.py:21
  19.0 1.1 %slice_bitcast_fusion = (bf16[8,256,256]{2,1,0:T(8,128)(2,1)}, bf16[8,256,256]{2,1,0:T(8,128)(2,1)S(1)}) fusion(bf16[1,16,256,256]{3,2,1,0:T(8,128)(2,1)S(1)} %copy-done), kind=kLoop, calls=%fused_computation.5 | loop fusion | bytes 4194304 | tf_op jit(solution)/shard_map/slice | solution.py:318
  20.1 2.7 %collective-permute-start = (bf16[8,256,256]{2,1,0:T(8,128)(2,1)S(1)}, bf16[8,256,256]{2,1,0:T(8,128)(2,1)}, u32[]{:S(2)}, u32[]{:S(2)}) collective-permute-start(bf16[8,256,256]{2,1,0:T(8,128)(2,1)S(1)} %get-tuple-element.36), channel_id=1, source_target_pairs={{0,96},{32,0},{64,32},{96,64},{1,97},{33,1},{65,33},{97,65},{2,98}... | collective-permute-start | bytes 3145736 | tf_op jit(solution)/shard_map/ppermute | solution.py:21
  23.0 5.6 %spectra.1.fields_ref = bf16[16,2,256,256]{3,2,1,0:T(8,128)(2,1)} custom-call(bf16[16,256,256]{2,1,0:T(8,128)(2,1)} %bitcast.92, bf16[256,256]{1,0:T(8,128)(2,1)} %constant.52.clone.to_half_ref, bf16[512,256]{1,0:T(8,128)(2,1)} %constant.53.clone.both_ref), custom_call_target="tpu_custom_call" | custom-call | flops 1610612736 | bytes 6291456 | tf_op jit(solution)/shard_map/spectra/pallas_call | solution.py:153
  28.6 17.5 %all-to-all-done = bf16[32,17,16,128]{3,2,1,0:T(8,128)(2,1)} async-done(((bf16[32,17,16,128]{3,2,1,0:T(8,128)(2,1)}), bf16[32,17,16,128]{3,2,1,0:T(8,128)(2,1)}, u32[]{:S(2)}, u32[]{:S(2)}) %all-to-all-start) | async-done | bytes 2228256 | tf_op jit(solution)/shard_map/all_to_all | solution.py:271
  46.1 4.0 %gather_fusion = bf16[512,16,128]{2,1,0:T(8,128)(2,1)} fusion(bf16[544,16,128]{2,1,0:T(8,128)(2,1)} %bitcast.3, s32[1024]{0:T(1024)S(1)} %pad_clamp_fusion.2), kind=kCustom, calls=%fused_computation | custom fusion | bytes 4196352 | tf_op jit(solution)/shard_map/gather | solution.py:325
  50.2 4.7 %all-to-all-start.1 = ((bf16[32,16,16,128]{3,2,1,0:T(8,128)(2,1)}), bf16[32,16,16,128]{3,2,1,0:T(8,128)(2,1)S(1)}, u32[]{:S(2)}, u32[]{:S(2)}) async-start(bf16[32,16,16,128]{3,2,1,0:T(8,128)(2,1)} %bitcast.4), calls=%async_computation.1 | async-start | bytes 4194304 | tf_op jit(solution)/shard_map/all_to_all | solution.py:271
  54.9 0.8 broadcast_in_dim.19.offsets_ref
  55.7 5.3 %pair_sums.4 = f32[8,8,256]{2,1,0:T(8,128)} custom-call(bf16[8,256,256]{2,1,0:T(8,128)(2,1)} %collective-permute-done.1.images_ref, bf16[16,2,256,256]{3,2,1,0:T(8,128)(2,1)} %spectra.1.fields_ref, bf16[256,256]{1,0:T(8,128)(2,1)} %constant.52.clone.to_half_ref, bf16[512,256]{1,0:T(8,128)(2,1)} %constant.53.clone.both_ref, ...), custom_call_target="tpu_custom_call" | custom-call | flops 1610612736 | bytes 3145728 | tf_op jit(solution)/shard_map/pair_sums/pallas_call | solution.py:183
  61.0 5.3 %pair_sums.3 = f32[8,8,256]{2,1,0:T(8,128)} custom-call(bf16[8,256,256]{2,1,0:T(8,128)(2,1)} %collective-permute-done.images_ref, bf16[16,2,256,256]{3,2,1,0:T(8,128)(2,1)} %spectra.1.fields_ref, bf16[256,256]{1,0:T(8,128)(2,1)} %constant.52.clone.to_half_ref, bf16[512,256]{1,0:T(8,128)(2,1)} %constant.53.clone.both_ref, ...), custom_call_target="tpu_custom_call" | custom-call | flops 1610612736 | bytes 3145728 | tf_op jit(solution)/shard_map/pair_sums/pallas_call | solution.py:183
  66.4 1.1 slice_reduce_fusion.1
  67.6 2.5 %collective-permute-start.2 = (f32[2,8]{1,0:T(2,128)S(1)}, f32[2,8]{1,0:T(2,128)S(1)}, u32[]{:S(2)}, u32[]{:S(2)}) collective-permute-start(f32[2,8]{1,0:T(2,128)S(1)} %pad_maximum_fusion), channel_id=1, source_target_pairs={{0,96},{32,0},{64,32},{96,64},{1,97},{33,1},{65,33},{97,65},{2,98}... | collective-permute-start | bytes 200 | tf_op jit(solution)/shard_map/ppermute | solution.py:21
  70.2 0.9 slice_bitcast_fusion.2
  71.2 0.2 copy.76
  71.4 0.6 gather_fusion.2
  72.0 0.6 gather_fusion.1
  72.8 10.5 %all-to-all-done.1.images_ref = bf16[32,16,16,128]{3,2,1,0:T(8,128)(2,1)S(1)} async-done(((bf16[32,16,16,128]{3,2,1,0:T(8,128)(2,1)}), bf16[32,16,16,128]{3,2,1,0:T(8,128)(2,1)S(1)}, u32[]{:S(2)}, u32[]{:S(2)}) %all-to-all-start.1) | async-done | bytes 2097184 | tf_op jit(solution)/shard_map/all_to_all | solution.py:271
  83.2 1.3 %copy-done.1 = bf16[32,16,16,128]{3,2,1,0:T(8,128)(2,1)} copy-done((bf16[32,16,16,128]{3,2,1,0:T(8,128)(2,1)}, bf16[32,16,16,128]{3,2,1,0:T(8,128)(2,1)S(1)}, u32[]{:S(2)}) %copy-start.1) | copy-done | bytes 2097176
  84.6 8.5 %pair_sums.5 = f32[16,8,256]{2,1,0:T(8,128)} custom-call(bf16[32,16,16,128]{3,2,1,0:T(8,128)(2,1)} %copy-done.1, bf16[16,2,256,256]{3,2,1,0:T(8,128)(2,1)} %spectra.1.fields_ref, bf16[256,256]{1,0:T(8,128)(2,1)} %constant.52.clone.to_half_ref, bf16[512,256]{1,0:T(8,128)(2,1)} %constant.53.clone.both_ref, bf16[256,256]{1,0:T(8,128)(2,1)} %constant.54.clone.from_half_ref, ...), custom_call_target="tpu_custom_call" | custom-call | flops 3221225472 | bytes 6291456 | tf_op jit(solution)/shard_map/pair_sums/pallas_call | solution.py:183
  93.1 1.2 %slice_reduce_fusion = (f32[16]{0:T(128)S(1)}, f32[16]{0:T(128)S(1)}, f32[16,1,256]{2,1,0:T(1,128)S(1)}) fusion(f32[16,8,256]{2,1,0:T(8,128)} %pair_sums.5), kind=kLoop, calls=%fused_computation.10 | loop fusion | flops 8160 | bytes 49280 | tf_op jit(solution)/shard_map/reduce_sum | solution.py:208
  94.7 0.6 broadcast_in_dim.25
  95.3 4.4 %all-to-all-start.2 = ((f32[32,2,16]{2,1,0:T(2,128)}), f32[32,2,16]{2,1,0:T(2,128)S(1)}, u32[]{:S(2)}, u32[]{:S(2)}) async-start(f32[32,2,16]{2,1,0:T(2,128)} %broadcast_in_dim.25), calls=%async_computation.2 | async-start | bytes 65536 | tf_op jit(solution)/shard_map/all_to_all | solution.py:271
  99.6 2.5 %collective-permute-start.4 = (f32[2,16]{0,1:T(8,128)S(1)}, f32[2,16]{0,1:T(8,128)S(1)}, u32[]{:S(2)}, u32[]{:S(2)}) collective-permute-start(f32[2,16]{0,1:T(8,128)S(1)} %multiply_add_fusion), channel_id=1, source_target_pairs={{0,96},{32,0},{64,32},{96,64},{1,97},{33,1},{65,33},{97,65},{2,98}... | collective-permute-start | bytes 392 | tf_op jit(solution)/shard_map/ppermute | solution.py:21
  102.2 4.8 %all-to-all-done.2 = f32[32,2,16]{2,1,0:T(2,128)S(1)} async-done(((f32[32,2,16]{2,1,0:T(2,128)}), f32[32,2,16]{2,1,0:T(2,128)S(1)}, u32[]{:S(2)}, u32[]{:S(2)}) %all-to-all-start.2) | async-done | bytes 4128 | tf_op jit(solution)/shard_map/all_to_all | solution.py:271
  107.0 0.3 copy.85
  107.3 0.6 gather_fusion.4
  107.8 0.6 gather_fusion.3
  108.5 0.6 copy.91
  (51 shorter events, 1.1 us)
Async XLA Ops:
  6.5 9.8 %copy-start.4 = (f32[2,1,16]{2,1,0:T(1,128)S(1)}, f32[2,1,16]{2,1,0:T(1,128)}, u32[]{:S(2)}) copy-start(f32[2,1,16]{2,1,0:T(1,128)} %param.18) | copy-start | bytes 388
  6.5 12.4 %copy-start = (bf16[1,16,256,256]{3,2,1,0:T(8,128)(2,1)S(1)}, bf16[1,16,256,256]{3,2,1,0:T(8,128)(2,1)}, u32[]{:S(2)}) copy-start(bf16[1,16,256,256]{3,2,1,0:T(8,128)(2,1)} %param.14) | copy-start | bytes 6291460
  6.5 39.6 %all-to-all-start = ((bf16[32,17,16,128]{3,2,1,0:T(8,128)(2,1)}), bf16[32,17,16,128]{3,2,1,0:T(8,128)(2,1)}, u32[]{:S(2)}, u32[]{:S(2)}) async-start(bf16[32,17,16,128]{3,2,1,0:T(8,128)(2,1)} %cut.1), calls=%async_computation | async-start | bytes 4456448 | tf_op jit(solution)/shard_map/all_to_all | solution.py:271
  16.4 6.3 %copy-start.8 = (s32[6,1,16]{2,1,0:T(1,128)S(1)}, s32[6,1,16]{2,1,0:T(1,128)}, u32[]{:S(2)}) copy-start(s32[6,1,16]{2,1,0:T(1,128)} %param.17) | copy-start | bytes 1156
  16.4 6.4 %copy-start.6 = (s32[1,512]{1,0:T(1,128)S(1)}, s32[1,512]{1,0:T(1,128)}, u32[]{:S(2)}) copy-start(s32[1,512]{1,0:T(1,128)} %param.16) | copy-start | bytes 6148
  16.4 6.4 %copy-start.7 = (s32[1,512]{1,0:T(1,128)S(1)}, s32[1,512]{1,0:T(1,128)}, u32[]{:S(2)}) copy-start(s32[1,512]{1,0:T(1,128)} %param.15) | copy-start | bytes 6148
  16.4 56.2 %collective-permute-start.3 = (f32[2,16]{0,1:T(8,128)S(1)}, f32[2,16]{0,1:T(8,128)S(1)}, u32[]{:S(2)}, u32[]{:S(2)}) collective-permute-start(f32[2,16]{0,1:T(8,128)S(1)} %copy.77), channel_id=1, source_target_pairs={{0,96},{32,0},{64,32},{96,64},{1,97},{33,1},{65,33},{97,65},{2,98}... | collective-permute-start | bytes 392 | tf_op jit(solution)/shard_map/ppermute | solution.py:21
  20.1 34.8 %collective-permute-start.1 = (bf16[8,256,256]{2,1,0:T(8,128)(2,1)}, bf16[8,256,256]{2,1,0:T(8,128)(2,1)}, u32[]{:S(2)}, u32[]{:S(2)}) collective-permute-start(bf16[8,256,256]{2,1,0:T(8,128)(2,1)} %get-tuple-element.35), channel_id=1, source_target_pairs={{0,32},{32,64},{64,96},{96,0},{1,33},{33,65},{65,97},{97,1},{2,34}... | collective-permute-start | bytes 3145736 | tf_op jit(solution)/shard_map/ppermute | solution.py:21
  20.1 40.9 %collective-permute-start = (bf16[8,256,256]{2,1,0:T(8,128)(2,1)S(1)}, bf16[8,256,256]{2,1,0:T(8,128)(2,1)}, u32[]{:S(2)}, u32[]{:S(2)}) collective-permute-start(bf16[8,256,256]{2,1,0:T(8,128)(2,1)S(1)} %get-tuple-element.36), channel_id=1, source_target_pairs={{0,96},{32,0},{64,32},{96,64},{1,97},{33,1},{65,33},{97,65},{2,98}... | collective-permute-start | bytes 3145736 | tf_op jit(solution)/shard_map/ppermute | solution.py:21
  50.2 4.7 %copy-start.2 = (f32[256]{0:T(256)S(1)}, f32[256]{0:T(256)}, u32[]{:S(2)}) copy-start(f32[256]{0:T(256)} %constant.55.clone) | copy-start | bytes 3076
  50.2 33.1 %all-to-all-start.1 = ((bf16[32,16,16,128]{3,2,1,0:T(8,128)(2,1)}), bf16[32,16,16,128]{3,2,1,0:T(8,128)(2,1)S(1)}, u32[]{:S(2)}, u32[]{:S(2)}) async-start(bf16[32,16,16,128]{3,2,1,0:T(8,128)(2,1)} %bitcast.4), calls=%async_computation.1 | async-start | bytes 4194304 | tf_op jit(solution)/shard_map/all_to_all | solution.py:271
  67.6 5.1 %collective-permute-start.2 = (f32[2,8]{1,0:T(2,128)S(1)}, f32[2,8]{1,0:T(2,128)S(1)}, u32[]{:S(2)}, u32[]{:S(2)}) collective-permute-start(f32[2,8]{1,0:T(2,128)S(1)} %pad_maximum_fusion), channel_id=1, source_target_pairs={{0,96},{32,0},{64,32},{96,64},{1,97},{33,1},{65,33},{97,65},{2,98}... | collective-permute-start | bytes 200 | tf_op jit(solution)/shard_map/ppermute | solution.py:21
  72.7 35.7 %copy-start.3 = (f32[2,16]{1,0:T(2,128)}, f32[2,16]{1,0:T(2,128)S(1)}, u32[]{:S(2)}) copy-start(f32[2,16]{1,0:T(2,128)S(1)} %pad_maximum_fusion.1) | copy-start | bytes 388
  83.2 1.3 %copy-start.1 = (bf16[32,16,16,128]{3,2,1,0:T(8,128)(2,1)}, bf16[32,16,16,128]{3,2,1,0:T(8,128)(2,1)S(1)}, u32[]{:S(2)}) copy-start(bf16[32,16,16,128]{3,2,1,0:T(8,128)(2,1)S(1)} %all-to-all-done.1.images_ref) | copy-start | bytes 6291460
  94.4 14.8 %copy-start.5 = (f32[2,16]{1,0:T(2,128)}, f32[2,16]{1,0:T(2,128)S(1)}, u32[]{:S(2)}) copy-start(f32[2,16]{1,0:T(2,128)S(1)} %pad_maximum_fusion.2) | copy-start | bytes 388
  95.3 11.8 %all-to-all-start.2 = ((f32[32,2,16]{2,1,0:T(2,128)}), f32[32,2,16]{2,1,0:T(2,128)S(1)}, u32[]{:S(2)}, u32[]{:S(2)}) async-start(f32[32,2,16]{2,1,0:T(2,128)} %broadcast_in_dim.25), calls=%async_computation.2 | async-start | bytes 65536 | tf_op jit(solution)/shard_map/all_to_all | solution.py:271
  99.6 8.9 %collective-permute-start.4 = (f32[2,16]{0,1:T(8,128)S(1)}, f32[2,16]{0,1:T(8,128)S(1)}, u32[]{:S(2)}, u32[]{:S(2)}) collective-permute-start(f32[2,16]{0,1:T(8,128)S(1)} %multiply_add_fusion), channel_id=1, source_target_pairs={{0,96},{32,0},{64,32},{96,64},{1,97},{33,1},{65,33},{97,65},{2,98}... | collective-permute-start | bytes 392 | tf_op jit(solution)/shard_map/ppermute | solution.py:21

commit v3 on v2

--- a/solution.py
+++ b/solution.py
@@ -114,25 +114,11 @@
         out_ref[k, 1] = jnp.concatenate([c, d], 1)
 
 
-def joined(pieces, k):
-    rows = pieces.shape[0] // 2
-    return jnp.concatenate(
-        [
-            jnp.concatenate([pieces[2 * r, k], pieces[2 * r + 1, k]], 1)
-            for r in range(rows)
-        ],
-        0,
-    )
-
-
 def pair_kernel(
-    other_first, in_pieces, images_ref, fields_ref, to_half_ref, both_ref, from_half_ref, offsets_ref, out_ref
+    other_first, images_ref, fields_ref, to_half_ref, both_ref, from_half_ref, offsets_ref, out_ref
 ):
     count = fields_ref.shape[0]
-    if in_pieces:
-        images = [joined(images_ref, k) for k in range(count)]
-    else:
-        images = [images_ref[k] for k in range(count)]
+    images = [images_ref[k] for k in range(count)]
     others = fields_of(images, to_half_ref[...], both_ref[...])
     owns = [split_fields(fields_ref[k]) for k in range(count)]
     pairs = [(x, y) if other_first else (y, x) for x, y in zip(others, owns)]
@@ -169,22 +155,14 @@
 
 
 def pair_sums(images, fields, start, other_first, tables, batch=4):
-    in_pieces = images.ndim == 4
-    count = images.shape[1] if in_pieces else images.shape[0]
-    length = fields.shape[-1]
+    count, length = images.shape[0], images.shape[-1]
     to_half, both, from_half = tables
     spread = jnp.broadcast_to(jnp.asarray(offsets_of(length))[:, None], (length, length))
-    if in_pieces:
-        image_block = pl.BlockSpec(
-            (images.shape[0], batch) + images.shape[2:], lambda i: (0, i, 0, 0)
-        )
-    else:
-        image_block = pl.BlockSpec((batch, length, length), lambda i: (i, 0, 0))
     return pl.pallas_call(
-        functools.partial(pair_kernel, other_first, in_pieces),
+        functools.partial(pair_kernel, other_first),
         grid=(count // batch,),
         in_specs=[
-            image_block,
+            pl.BlockSpec((batch, length, length), lambda i: (i, 0, 0)),
             pl.BlockSpec((batch, 2, length, length), lambda i: (i + start // batch, 0, 0, 0)),
             whole(to_half),
             whole(both),
@@ -210,10 +188,9 @@
     return jnp.stack([along_rows, along_cols], 0)
 
 
-def cut_kernel(images_ref, note_ref, out_ref, held, read_sems, write_sem):
-    pieces, slots, rows, columns = out_ref.shape
+def lines_kernel(images_ref, note_ref, table_ref, out_ref, held, lines, read_sems, write_sems):
+    devices, slots, rows, _ = out_ref.shape
     count = slots - 1
-    across = images_ref.shape[2] // columns
     chunks = read_sems.shape[0]
     batch = count // chunks
 
@@ -224,75 +201,232 @@
     for chunk in range(chunks):
         read(chunk).start()
     writes = []
-    for piece in range(pieces):
-        write = pltpu.make_async_copy(
-            note_ref, out_ref.at[piece, count], write_sem.at[len(writes)]
-        )
-        write.start()
-        writes.append(write)
+
+    def write(source, target):
+        copy = pltpu.make_async_copy(source, target, write_sems.at[len(writes)])
+        copy.start()
+        writes.append(copy)
+
+    for device in range(devices):
+        write(note_ref, out_ref.at[device, count])
+    table = table_ref[...]
     for chunk in range(chunks):
         read(chunk).wait()
+        for strip in range(chunk * batch, (chunk + 1) * batch):
+            image = held[strip]
+            across = lax.dot_general(
+                table, image, (((1,), (1,)), ((), ())), preferred_element_type=jnp.float32
+            )
+            down = dot(table, image)
+            for core, values in enumerate((across, down)):
+                values = values.astype(jnp.bfloat16)
+                for chip in range(devices // 2):
+                    lines[2 * chip + core, strip] = values[chip * rows : (chip + 1) * rows]
         strips = pl.ds(chunk * batch, batch)
-        for piece in range(pieces):
-            r, c = piece // across, piece % across
-            write = pltpu.make_async_copy(
-                held.at[strips, pl.ds(r * rows, rows), pl.ds(c * columns, columns)],
-                out_ref.at[piece, strips],
-                write_sem.at[len(writes)],
-            )
-            write.start()
-            writes.append(write)
-    for write in writes:
-        write.wait()
-
-
-def cut(images, note, pieces, chunks=4):
+        for device in range(devices):
+            write(lines.at[device, strips], out_ref.at[device, strips])
+    for copy in writes:
+        copy.wait()
+
+
+def lines_of(images, note, table, devices, chunks=4):
     count, length = images.shape[0], images.shape[-1]
-    shape = (pieces, count + 1, 2 * length // pieces, length // 2)
+    rows = 2 * length // devices
     return pl.pallas_call(
-        cut_kernel,
+        lines_kernel,
         in_specs=[
             pl.BlockSpec(memory_space=pl.ANY),
             pl.BlockSpec(memory_space=pltpu.VMEM),
+            pl.BlockSpec(memory_space=pltpu.VMEM),
         ],
         out_specs=pl.BlockSpec(memory_space=pl.ANY),
-        out_shape=jax.ShapeDtypeStruct(shape, images.dtype),
+        out_shape=jax.ShapeDtypeStruct((devices, count + 1, rows, length), jnp.bfloat16),
         scratch_shapes=[
             pltpu.VMEM(images.shape, images.dtype),
+            pltpu.VMEM((devices, count, rows, length), jnp.bfloat16),
             pltpu.SemaphoreType.DMA((chunks,)),
-            pltpu.SemaphoreType.DMA(((chunks + 1) * pieces,)),
+            pltpu.SemaphoreType.DMA(((chunks + 1) * devices,)),
         ],
-        compiler_params=pltpu.CompilerParams(vmem_limit_bytes=60 * 1024 * 1024),
-        name="cut",
-    )(images, note)
+        compiler_params=call_params(),
+        name="lines",
+    )(images, note, table)
+
+
+def moments_kernel(
+    partner_ref, lines_ref, masks_ref, chosen_ref, both_ref, weights_ref, depth_ref, out_ref,
+    held, spectra, extra, profile, read_sems,
+):
+    tiles, slots, rows, length = lines_ref.shape
+    count = slots - 1
+    half = rows // 2
+    chunks = read_sems.shape[0]
+    batch = tiles // chunks
+
+    def read(chunk):
+        part = pl.ds(chunk * batch, batch)
+        return pltpu.make_async_copy(lines_ref.at[part], held.at[part], read_sems.at[chunk])
+
+    for chunk in range(chunks):
+        read(chunk).start()
+    both = both_ref[...]
+    plain, scale = masks_ref[0:half], masks_ref[half:rows]
+
+    def transform(tile):
+        mixed = dot(held[tile, :count].reshape(count * rows, length), both)
+        mixed = mixed.reshape(count, rows, 2 * length)
+        cos_re, sin_re = mixed[:, :half, :length], mixed[:, :half, length:]
+        cos_im, sin_im = mixed[:, half:, :length], mixed[:, half:, length:]
+        fields = jnp.concatenate([cos_re + sin_im * plain, sin_re - cos_im * plain], 1)
+        at = pl.multiple_of(tile * count, count)
+        spectra[pl.ds(at, count)] = fields.astype(jnp.bfloat16)
+        extra[pl.ds(at, count), :] = mixed[:, half, :].astype(jnp.bfloat16)
+
+    for chunk in range(chunks):
+        read(chunk).wait()
+
+        @pl.loop(0, batch // 2)
+        def _(pair):
+            transform(chunk * batch + 2 * pair)
+            transform(chunk * batch + 2 * pair + 1)
+
+    def surfaces(tile):
+        at = pl.multiple_of(tile * count, count)
+        first = jnp.stack([spectra[partner_ref[at + k]] for k in range(count)], 0)
+        first = first.astype(jnp.float32)
+        second = spectra[pl.ds(at, count)].astype(jnp.float32)
+        a, b = first[:, :half], first[:, half:]
+        c, d = second[:, :half], second[:, half:]
+        cross = jnp.concatenate([a * c + b * d, b * c - a * d], 1).astype(jnp.bfloat16)
+        mixed = dot(cross.reshape(count * rows, length), both).reshape(count, rows, 2 * length)
+        real = mixed[:, :half, :length] - mixed[:, half:, length:]
+        imag = mixed[:, :half, length:] + mixed[:, half:, :length]
+        profile[pl.ds(at, count), :] = jnp.sum((real * real + imag * imag) * scale, axis=1)
+
+    @pl.loop(0, tiles // 2)
+    def _(pair):
+        surfaces(2 * pair)
+        surfaces(2 * pair + 1)
+
+    second = extra[...]
+    first = dot(chosen_ref[...], second)
+    second = second.astype(jnp.float32)
+    a, b = first[:, :length], first[:, length:]
+    c, d = second[:, :length], second[:, length:]
+    real = dot((a * c + b * d).astype(jnp.bfloat16), both[:, :length])
+    imag = dot((b * c - a * d).astype(jnp.bfloat16), both[:, length:])
+    last = real - imag
+    profile[...] += last * last * masks_ref[rows : rows + 1]
+    sums = lax.dot_general(
+        weights_ref[...],
+        profile[...],
+        (((1,), (1,)), ((), ())),
+        precision=lax.Precision.HIGHEST,
+        preferred_element_type=jnp.float32,
+    )
+    sums = jnp.concatenate([sums[0:2], depth_ref[...]], 0)
+    for tile in range(tiles):
+        out_ref[tile] = sums
+
+
+def moments_of(lines, partner, first_chip, depth, both, chunks=8):
+    tiles, slots, rows, length = lines.shape
+    count = slots - 1
+    nodes = tiles * count
+    half = rows // 2
+    special = first_chip & (jnp.arange(half) == 0)
+    masks = jnp.concatenate(
+        [jnp.where(special, 0.0, 1.0), jnp.where(special, 1.0, 2.0), jnp.where(first_chip, 1.0, 0.0)[None]]
+    )
+    masks = jnp.broadcast_to(jnp.pad(masks, (0, half - 1))[:, None], (3 * half, length))
+    chosen = (partner[:, None] == jnp.arange(nodes)).astype(jnp.bfloat16)
+    weights = np.zeros((8, length), np.float32)
+    weights[0] = 1.0
+    weights[1] = offsets_of(length)
+    vmem = pl.BlockSpec(memory_space=pltpu.VMEM)
+    return pl.pallas_call(
+        moments_kernel,
+        in_specs=[
+            pl.BlockSpec(memory_space=pltpu.SMEM),
+            pl.BlockSpec(memory_space=pl.ANY),
+            vmem,
+            vmem,
+            vmem,
+            vmem,
+            vmem,
+        ],
+        out_specs=vmem,
+        out_shape=jax.ShapeDtypeStruct((tiles, 4, nodes), jnp.float32),
+        scratch_shapes=[
+            pltpu.VMEM(lines.shape, lines.dtype),
+            pltpu.VMEM((nodes, rows, length), jnp.bfloat16),
+            pltpu.VMEM((nodes, 2 * length), jnp.bfloat16),
+            pltpu.VMEM((nodes, length), jnp.float32),
+            pltpu.SemaphoreType.DMA((chunks,)),
+        ],
+        compiler_params=call_params(),
+        cost_estimate=pl.CostEstimate(
+            flops=nodes * rows * 4 * 2 * length**2, bytes_accessed=2 * lines.size, transcendentals=0
+        ),
+        name="moments",
+    )(partner, lines, masks, chosen, both, jnp.asarray(weights), depth)
+
+
+def pull_kernel(parts_ref, links_ref, own_ref, near_ref, out_ref):
+    nodes = own_ref.shape[1]
+    links = links_ref.shape[0]
+    sources = lax.broadcasted_iota(jnp.int32, (nodes, nodes), 0)
+    table = jnp.zeros((nodes, nodes), jnp.float32)
+    for k in range(links):
+        table += jnp.where(sources == links_ref[k : k + 1, :], 1.0, 0.0)
+    sums = dot(parts_ref[...], table.astype(jnp.bfloat16))
+    linked = (sums[4:6] + sums[2:4]) + sums[0:2]
+    out_ref[...] = (linked - links * own_ref[...]) + (near_ref[...] - own_ref[...])
+
+
+def pull_all(parts, links, own, near):
+    return pl.pallas_call(
+        pull_kernel,
+        out_shape=jax.ShapeDtypeStruct(own.shape, jnp.float32),
+        compiler_params=pltpu.CompilerParams(vmem_limit_bytes=32 * 1024 * 1024),
+        name="pull",
+    )(parts, links, own, near)
 
 
 def exchange(x):
     return lax.all_to_all(x, "tile", split_axis=0, concat_axis=0, tiled=True)
 
 
-def gathered(values):
-    tiles = lax.axis_size("tile")
-    spread = exchange(jnp.broadcast_to(values[None], (tiles,) + values.shape))
-    return spread.transpose(1, 0, 2).reshape(values.shape[0], -1)
-
-
-def in_parts(values, rows, columns):
+def in_parts(values):
     parts = []
     rest = values
     for _ in range(3):
         part = lax.reduce_precision(rest, 8, 7)
         parts.append(part.astype(jnp.bfloat16))
         rest = rest - part
-    stacked = jnp.concatenate(parts, 0)
-    return jnp.pad(stacked, ((0, rows - stacked.shape[0]), (0, columns - stacked.shape[1])))
-
-
-def from_parts(tiles, height, width):
-    parts = tiles[:, : 3 * height, :width].astype(jnp.float32)
-    parts = parts.reshape(tiles.shape[0], 3, height, width)
-    values = (parts[:, 2] + parts[:, 1]) + parts[:, 0]
-    return values.transpose(1, 0, 2).reshape(height, -1)
+    return jnp.concatenate(parts, 0)
+
+
+def note_of(start, links, rows, length):
+    first = jnp.concatenate([in_parts(start), (links // 2).astype(jnp.bfloat16)], 0)
+    second = (links % 2).astype(jnp.bfloat16)
+    half = length // 2
+
+    def padded(values):
+        return jnp.pad(values, ((0, rows - values.shape[0]), (0, half - values.shape[1])))
+
+    return jnp.concatenate([padded(first), padded(second)], 1)
+
+
+def read_notes(notes, components, links, count):
+    half = notes.shape[2] // 2
+    first = notes[:, :, :count].transpose(1, 0, 2).reshape(notes.shape[1], -1)
+    second = notes[:, :links, half : half + count].transpose(1, 0, 2).reshape(links, -1)
+    height = 3 * components
+    parts = first[:height]
+    values = parts.astype(jnp.float32)
+    start = (values[2 * components :] + values[components : 2 * components]) + values[:components]
+    linked = 2 * first[height : height + links].astype(jnp.int32) + second.astype(jnp.int32)
+    return parts, start, linked
 
 
 def per_device(strips, partner_tile, partner_strip, adjacency, start_positions):
@@ -302,42 +436,52 @@
     per_tile, length = own.shape[0], own.shape[1]
     half_strips = per_tile // 2
     tables = half_tables(length)
+    both = jnp.concatenate([tables[1][:length], tables[1][length:]], 1)
     partner = partner_tile[0] * per_tile + partner_strip[0]
-    my_partner = lax.dynamic_slice_in_dim(partner, tile_index * per_tile, per_tile, 0)
+    place = tile_index * per_tile
     links = adjacency[:, 0, :]
-    neighbours = links.shape[0]
     start = start_positions[:, 0, :]
 
-    def pull(whole_positions, current, near):
-        springs = jnp.sum(whole_positions[:, links], axis=1) - neighbours * current
-        return springs + (whole_positions[:, my_partner] - current) + (near - current)
-
-    partner_rows = partner_tile[0] * (per_tile + 1) + partner_strip[0]
+    rows = 2 * length // tiles
+    order = np.arange(length).reshape(2, tiles // 2, rows // 2).transpose(1, 0, 2).reshape(-1)
+    line_table = tables[0].T[order]
+    lines = exchange(lines_of(own, note_of(start, links, rows, length), line_table, tiles))
 
     near_low = shifted(own[:half_strips], "sec", -1)
     back_high = shifted(own[half_strips:], "sec", 1)
-
-    rows, columns = 2 * length // tiles, length // 2
-    pieces = cut(own, in_parts(start, rows, columns), tiles)
-    spread = exchange(pieces)
     fields = spectra_of(own, tables)
-    spread, fields, partner_rows = lax.optimization_barrier((spread, fields, partner_rows))
-    picked = spread.reshape((-1, rows, columns)).at[partner_rows].get(mode="promise_in_bounds")
-    partners = exchange(picked.reshape(tiles, per_tile, rows, columns))
-
-    whole_start = from_parts(spread[:, per_tile], *start.shape)
-    first_pull = pull(whole_start, start, shifted(start, "sec", -1))
     low = flows_of(pair_sums(near_low, fields, 0, True, tables))
     high = flows_of(pair_sums(back_high, fields, half_strips, False, tables))
     depth_out = jnp.concatenate([low, shifted(high, "sec", -1)], 1)
-    partners, depth_out, first_pull = lax.optimization_barrier((partners, depth_out, first_pull))
-
-    plane_out = flows_of(pair_sums(partners, fields, 0, True, tables))
-    current = start + relax_rate * (first_pull + plane_out + depth_out)
+    depth_row = lax.dynamic_update_slice(
+        jnp.zeros((2, tiles * per_tile), jnp.float32), depth_out, (0, place)
+    )
+
+    shares = moments_of(lines, partner, tile_index < 2, depth_row, both)
+    parts, whole_start, whole_links = read_notes(
+        lines[:, per_tile], start.shape[0], links.shape[0], per_tile
+    )
+    whole_links = jnp.concatenate([whole_links, partner[None]], 0)
+    first_pull = pull_all(parts, whole_links, whole_start, shifted(whole_start, "sec", -1))
+
+    received = exchange(shares).reshape(tiles // 2, 2, 4, tiles * per_tile)
+    summed = jnp.sum(received, axis=0)
+    plane_all = summed[:, 1] / length / (summed[:, 0] / length + epsilon)
+    depth_all = summed[0, 2:] + summed[1, 2:]
+    flow_all = plane_all + depth_all
+    current = whole_start + relax_rate * (first_pull + flow_all)
+
+    def mine(values):
+        return lax.dynamic_slice_in_dim(values, place, per_tile, 1)
+
+    my_links = jnp.concatenate([links, mine(partner[None])], 0)
     for iteration in range(1, STEPS):
-        force = pull(gathered(current), current, shifted(current, "sec", -1))
-        current = current + relax_rate * (force + plane_out + depth_out)
-    return (plane_out[:, None, :], depth_out[:, None, :], current[:, None, :])
+        here = mine(current)
+        linked = jnp.sum(current[:, my_links], axis=1)
+        near = shifted(here, "sec", -1)
+        force = (linked - my_links.shape[0] * here) + (near - here) + mine(flow_all)
+        here = here + relax_rate * force
+    return (mine(plane_all)[:, None, :], depth_out[:, None, :], here[:, None, :])
 
 
 def solution(mesh):

time: 110 us -> 112 us (1.018)
  Pallas kernels: 29.3 us -> 37.8 us
  local copies, waits for them, and re-layouts: 12.9 us -> 7.19 us
    all_to_all x3 -> x2, waiting for transfers between devices: 32.9 us -> 15.1 us  [exchange(): return lax.all_to_all(x, 'tile', split_axis=0, concat_axis=0, tiled=True)]
    ppermute x5, waiting for transfers between devices: 0.01 us -> 17.2 us  [shifted(): lax.ppermute(x, axis, [(i, (i + by) % devices) for i in range(devices)])]
    pallas_call x4 -> x5, Pallas kernels: 23.7 us -> 32.2 us  [the longest x1 14.2 us: moments_of(): pl.pallas_call(moments_kernel, in_specs=[pl.BlockSpec(memory_space=pltpu....]
    gather x5 -> x1, local copies, waits for them, and re-layouts: 6.4 us -> 0.63 us  [per_device(): linked = jnp.sum(current[:, my_links], axis=1)]
    all_to_all x3 -> x2, starting transfers between devices: 18.8 us -> 17.1 us  [exchange(): return lax.all_to_all(x, 'tile', split_axis=0, concat_axis=0, tiled=True)]
    convert_element_type x0 -> x3, other arithmetic: none -> 1.64 us  [the longest x1 0.93 us: moments_of(): chosen = (partner[:, None] == jnp.arange(nodes)).astype(jnp.bfloat16)]
    reduce_sum x2 -> x1, other arithmetic: 2.27 us -> 1.08 us  [flows_of(): along_rows = jnp.sum(sums[:, 1], axis=1) / cells / total]
  transfers between devices with their start and end apart: 8 -> 7, of which waited for: 3 -> 5; matrix products, arithmetic and copies ran while one was open for 11% -> 5% of each run, Pallas kernels for 15% -> 15%
where the time goes in v3:
time: 112 us; the launch traced here: 111 us
  Pallas kernels  37.8 us (34%)
  waiting for transfers between devices  32.3 us (29%)
  starting transfers between devices  28.2 us (25%)
  local copies, waits for them, and re-layouts  7.19 us (6%)
  other arithmetic  5.21 us (5%)
    ppermute x5, waiting for transfers between devices, shifted(): lax.ppermute(x, axis, [(i, (i + by) % devices) for i in range(devices)])  17.2 us
    all_to_all x2, starting transfers between devices, exchange(): return lax.all_to_all(x, 'tile', split_axis=0, concat_axis=0, tiled=True)  17.1 us
    all_to_all x2, waiting for transfers between devices, exchange(): return lax.all_to_all(x, 'tile', split_axis=0, concat_axis=0, tiled=True)  15.1 us
    pallas_call x1, Pallas kernels, moments_of(): pl.pallas_call(moments_kernel, in_specs=[pl.BlockSpec(memory_space=pltpu....  14.2 us
    ppermute x5, starting transfers between devices, shifted(): lax.ppermute(x, axis, [(i, (i + by) % devices) for i in range(devices)])  11.1 us
    pallas_call x2, Pallas kernels, pair_sums(): pl.pallas_call(functools.partial(pair_kernel, other_first), grid=(count /...  10.6 us
    pallas_call x1, Pallas kernels, lines_of(): pl.pallas_call(lines_kernel, in_specs=[pl.BlockSpec(memory_space=pl.ANY),...  6.53 us
    pallas_call x1, Pallas kernels, spectra_of(): pl.pallas_call(spectra_kernel, grid=(count // batch,), in_specs=[pl.Block...  5.59 us
  transfers between devices with their start and end apart: 7, of which 5 were waited for; matrix products, arithmetic and copies ran while one was open for 5% of the time, Pallas kernels for 15%

profile of v3, /device:TPU:1, one launch (start us, length us, event | category | flops | bytes accessed | tf_op | source)
XLA Modules:
  0.0 111.5 jit_solution(2986432373387661447)
XLA Ops:
  0.6 0.7 reduce-precision_convert_fusion.1
  1.3 0.7 fusion.11
  2.0 0.6 fusion.2.note_ref
  2.6 6.5 %lines.1 = bf16[32,17,16,256]{3,2,1,0:T(8,128)(2,1)} custom-call(bf16[16,256,256]{2,1,0:T(8,128)(2,1)} %bitcast.87, bf16[16,256]{1,0:T(8,128)(2,1)} %fusion.2.note_ref, bf16[256,256]{1,0:T(8,128)(2,1)} %constant.108.table_ref), custom_call_target="tpu_custom_call" | custom-call | tf_op jit(solution)/shard_map/lines/pallas_call | solution.py:235
  9.2 9.8 %all-to-all-start = ((bf16[32,17,16,256]{3,2,1,0:T(8,128)(2,1)}), bf16[32,17,16,256]{3,2,1,0:T(8,128)(2,1)}, u32[]{:S(2)}, u32[]{:S(2)}) async-start(bf16[32,17,16,256]{3,2,1,0:T(8,128)(2,1)} %lines.1), calls=%async_computation | async-start | bytes 8912896 | tf_op jit(solution)/shard_map/all_to_all | solution.py:396
  19.0 1.2 %slice_bitcast_fusion = (bf16[8,256,256]{2,1,0:T(8,128)(2,1)S(1)}, bf16[8,256,256]{2,1,0:T(8,128)(2,1)}) fusion(bf16[1,16,256,256]{3,2,1,0:T(8,128)(2,1)S(1)} %copy-done), kind=kLoop, calls=%fused_computation.1 | loop fusion | bytes 4194304 | tf_op jit(solution)/shard_map/slice | solution.py:451
  20.2 2.5 %collective-permute-start = (bf16[8,256,256]{2,1,0:T(8,128)(2,1)}, bf16[8,256,256]{2,1,0:T(8,128)(2,1)S(1)}, u32[]{:S(2)}, u32[]{:S(2)}) collective-permute-start(bf16[8,256,256]{2,1,0:T(8,128)(2,1)} %get-tuple-element.24), channel_id=1, source_target_pairs={{0,96},{32,0},{64,32},{96,64},{1,97},{33,1},{65,33},{97,65},{2,98}... | collective-permute-start | bytes 3145736 | tf_op jit(solution)/shard_map/ppermute | solution.py:21
  23.0 5.6 %spectra.1.fields_ref = bf16[16,2,256,256]{3,2,1,0:T(8,128)(2,1)} custom-call(bf16[16,256,256]{2,1,0:T(8,128)(2,1)} %bitcast.88, bf16[256,256]{1,0:T(8,128)(2,1)} %constant.88.clone.to_half_ref, bf16[512,256]{1,0:T(8,128)(2,1)} %constant.89.clone.both_ref), custom_call_target="tpu_custom_call" | custom-call | flops 1610612736 | bytes 6291456 | tf_op jit(solution)/shard_map/spectra/pallas_call | solution.py:139
  28.6 0.9 fusion.chosen_ref
  29.5 15.7 %collective-permute-done.images_ref = bf16[8,256,256]{2,1,0:T(8,128)(2,1)S(1)} collective-permute-done((bf16[8,256,256]{2,1,0:T(8,128)(2,1)}, bf16[8,256,256]{2,1,0:T(8,128)(2,1)S(1)}, u32[]{:S(2)}, u32[]{:S(2)}) %collective-permute-start) | collective-permute-done | bytes 1048608 | tf_op jit(solution)/shard_map/ppermute | solution.py:21
  45.3 0.9 broadcast_in_dim.60.offsets_ref
  46.2 0.1 copy-done.2
  46.4 5.3 %pair_sums.2 = f32[8,8,256]{2,1,0:T(8,128)} custom-call(bf16[8,256,256]{2,1,0:T(8,128)(2,1)} %copy-done.2, bf16[16,2,256,256]{3,2,1,0:T(8,128)(2,1)} %spectra.1.fields_ref, bf16[256,256]{1,0:T(8,128)(2,1)} %constant.88.clone.to_half_ref, bf16[512,256]{1,0:T(8,128)(2,1)} %constant.89.clone.both_ref, bf16[256,256]{1,0:T(8,128)(2,1)} %constant.90.clone.from_half_ref, ...), custom_call_target="tpu_custom_call" | custom-call | flops 1610612736 | bytes 3145728 | tf_op jit(solution)/shard_map/pair_sums/pallas_call | solution.py:161
  51.7 1.0 copy-done.1
  52.7 5.3 %pair_sums.3 = f32[8,8,256]{2,1,0:T(8,128)} custom-call(bf16[8,256,256]{2,1,0:T(8,128)(2,1)} %copy-done.1, bf16[16,2,256,256]{3,2,1,0:T(8,128)(2,1)} %spectra.1.fields_ref, bf16[256,256]{1,0:T(8,128)(2,1)} %constant.88.clone.to_half_ref, bf16[512,256]{1,0:T(8,128)(2,1)} %constant.89.clone.both_ref, bf16[256,256]{1,0:T(8,128)(2,1)} %constant.90.clone.from_half_ref, ...), custom_call_target="tpu_custom_call" | custom-call | flops 1610612736 | bytes 3145728 | tf_op jit(solution)/shard_map/pair_sums/pallas_call | solution.py:161
  58.0 1.1 slice_reduce_fusion
  59.3 3.5 %collective-permute-start.2 = (f32[2,8]{1,0:T(2,128)S(1)}, f32[2,8]{1,0:T(2,128)S(1)}, u32[]{:S(2)}, u32[]{:S(2)}) collective-permute-start(f32[2,8]{1,0:T(2,128)S(1)} %pad_maximum_fusion), channel_id=1, source_target_pairs={{0,96},{32,0},{64,32},{96,64},{1,97},{33,1},{65,33},{97,65},{2,98}... | collective-permute-start | bytes 200 | tf_op jit(solution)/shard_map/ppermute | solution.py:21
  62.8 0.7 collective-permute-done.2
  63.6 0.2 dynamic_update_slice.3.depth_ref
  63.8 10.6 %all-to-all-done.lines_ref = bf16[32,17,16,256]{3,2,1,0:T(8,128)(2,1)} async-done(((bf16[32,17,16,256]{3,2,1,0:T(8,128)(2,1)}), bf16[32,17,16,256]{3,2,1,0:T(8,128)(2,1)}, u32[]{:S(2)}, u32[]{:S(2)}) %all-to-all-start) | async-done | bytes 4456480 | tf_op jit(solution)/shard_map/all_to_all | solution.py:396
  74.4 1.0 slice_bitcast_fusion.2
  75.4 0.7 broadcast_in_dim.58.masks_ref
  76.1 14.2 %moments.1 = f32[32,4,512]{2,1,0:T(4,128)} custom-call(s32[512]{0:T(512)} %bitcast.92, bf16[32,17,16,256]{3,2,1,0:T(8,128)(2,1)} %all-to-all-done.lines_ref, f32[24,256]{1,0:T(8,128)} %broadcast_in_dim.58.masks_ref, bf16[512,512]{1,0:T(8,128)(2,1)} %fusion.chosen_ref, bf16[256,512]{1,0:T(8,128)(2,1)} %constant.111.both_ref, ...), custom_call_target="tpu_custom_call" | custom-call | flops 4294967296 | bytes 4456448 | tf_op jit(solution)/shard_map/moments/pallas_call | solution.py:346
  90.3 7.3 %all-to-all-start.1 = ((f32[32,4,512]{2,1,0:T(4,128)}), f32[32,4,512]{2,1,0:T(4,128)S(1)}, u32[]{:S(2)}, u32[]{:S(2)}) async-start(f32[32,4,512]{2,1,0:T(4,128)} %moments.1), calls=%async_computation.1 | async-start | bytes 524288 | tf_op jit(solution)/shard_map/all_to_all | solution.py:396
  97.9 2.6 %collective-permute-start.3 = (f32[2,512]{1,0:T(2,128)S(1)}, f32[2,512]{1,0:T(2,128)S(1)}, u32[]{:S(2)}, u32[]{:S(2)}) collective-permute-start(f32[2,512]{1,0:T(2,128)S(1)} %slice_add_fusion.1.own_ref), channel_id=1, source_target_pairs={{0,96},{32,0},{64,32},{96,64},{1,97},{33,1},{65,33},{97,65},{2,98}... | collective-permute-start | bytes 12296 | tf_op jit(solution)/shard_map/ppermute | solution.py:21
  100.5 0.7 collective-permute-done.3.near_ref
  101.3 0.8 pull.1
  102.1 4.5 %all-to-all-done.1 = f32[32,4,512]{2,1,0:T(4,128)S(1)} async-done(((f32[32,4,512]{2,1,0:T(4,128)}), f32[32,4,512]{2,1,0:T(4,128)S(1)}, u32[]{:S(2)}, u32[]{:S(2)}) %all-to-all-start.1) | async-done | bytes 262176 | tf_op jit(solution)/shard_map/all_to_all | solution.py:396
  107.0 0.6 constant_dynamic-slice_fusion.2
  107.6 2.5 %collective-permute-start.4 = (f32[2,16]{1,0:T(2,128)S(1)}, f32[2,16]{1,0:T(2,128)S(1)}, u32[]{:S(2)}, u32[]{:S(2)}) collective-permute-start(f32[2,16]{1,0:T(2,128)S(1)} %constant_dynamic-slice_fusion.1), channel_id=1, source_target_pairs={{0,96},{32,0},{64,32},{96,64},{1,97},{33,1},{65,33},{97,65},{2,98}... | collective-permute-start | bytes 392 | tf_op jit(solution)/shard_map/ppermute | solution.py:21
  110.1 0.6 gather_fusion
  110.8 0.6 fusion.33
  (54 shorter events, 1.4 us)
Async XLA Ops:
  9.2 9.8 %copy-start = (bf16[1,16,256,256]{3,2,1,0:T(8,128)(2,1)S(1)}, bf16[1,16,256,256]{3,2,1,0:T(8,128)(2,1)}, u32[]{:S(2)}) copy-start(bf16[1,16,256,256]{3,2,1,0:T(8,128)(2,1)} %param.15) | copy-start | bytes 6291460
  9.2 13.5 %copy-start.9 = (s32[1,512]{1,0:T(1,128)S(1)}, s32[1,512]{1,0:T(1,128)}, u32[]{:S(2)}) copy-start(s32[1,512]{1,0:T(1,128)} %param.17) | copy-start | bytes 6148
  9.2 13.5 %copy-start.10 = (s32[1,512]{1,0:T(1,128)S(1)}, s32[1,512]{1,0:T(1,128)}, u32[]{:S(2)}) copy-start(s32[1,512]{1,0:T(1,128)} %param.16) | copy-start | bytes 6148
  9.2 13.6 %copy-start.5 = (s32[6,1,16]{2,1,0:T(1,128)S(1)}, s32[6,1,16]{2,1,0:T(1,128)}, u32[]{:S(2)}) copy-start(s32[6,1,16]{2,1,0:T(1,128)} %param.18) | copy-start | bytes 1156
  9.2 65.1 %all-to-all-start = ((bf16[32,17,16,256]{3,2,1,0:T(8,128)(2,1)}), bf16[32,17,16,256]{3,2,1,0:T(8,128)(2,1)}, u32[]{:S(2)}, u32[]{:S(2)}) async-start(bf16[32,17,16,256]{3,2,1,0:T(8,128)(2,1)} %lines.1), calls=%async_computation | async-start | bytes 8912896 | tf_op jit(solution)/shard_map/all_to_all | solution.py:396
  20.2 25.1 %copy-start.6 = (f32[256]{0:T(256)S(1)}, f32[256]{0:T(256)}, u32[]{:S(2)}) copy-start(f32[256]{0:T(256)} %constant.93.clone) | copy-start | bytes 3076
  20.2 25.1 %collective-permute-start = (bf16[8,256,256]{2,1,0:T(8,128)(2,1)}, bf16[8,256,256]{2,1,0:T(8,128)(2,1)S(1)}, u32[]{:S(2)}, u32[]{:S(2)}) collective-permute-start(bf16[8,256,256]{2,1,0:T(8,128)(2,1)} %get-tuple-element.24), channel_id=1, source_target_pairs={{0,96},{32,0},{64,32},{96,64},{1,97},{33,1},{65,33},{97,65},{2,98}... | collective-permute-start | bytes 3145736 | tf_op jit(solution)/shard_map/ppermute | solution.py:21
  22.7 29.0 %collective-permute-start.1 = (bf16[8,256,256]{2,1,0:T(8,128)(2,1)S(1)}, bf16[8,256,256]{2,1,0:T(8,128)(2,1)S(1)}, u32[]{:S(2)}, u32[]{:S(2)}) collective-permute-start(bf16[8,256,256]{2,1,0:T(8,128)(2,1)S(1)} %get-tuple-element.23), channel_id=1, source_target_pairs={{0,32},{32,64},{64,96},{96,0},{1,33},{33,65},{65,97},{97,1},{2,34}... | collective-permute-start | bytes 3145736 | tf_op jit(solution)/shard_map/ppermute | solution.py:21
  22.7 29.0 %copy-start.3 = (s32[1,512]{1,0:T(1,128)}, s32[1,512]{1,0:T(1,128)S(1)}, u32[]{:S(2)}) copy-start(s32[1,512]{1,0:T(1,128)S(1)} %multiply_add_fusion.1) | copy-start | bytes 6148
  45.3 1.1 copy-start.2
  51.7 1.0 copy-start.1
  59.3 4.2 %collective-permute-start.2 = (f32[2,8]{1,0:T(2,128)S(1)}, f32[2,8]{1,0:T(2,128)S(1)}, u32[]{:S(2)}, u32[]{:S(2)}) collective-permute-start(f32[2,8]{1,0:T(2,128)S(1)} %pad_maximum_fusion), channel_id=1, source_target_pairs={{0,96},{32,0},{64,32},{96,64},{1,97},{33,1},{65,33},{97,65},{2,98}... | collective-permute-start | bytes 200 | tf_op jit(solution)/shard_map/ppermute | solution.py:21
  63.6 26.7 %copy-start.7 = (f32[2,16]{1,0:T(2,128)}, f32[2,16]{1,0:T(2,128)S(1)}, u32[]{:S(2)}) copy-start(f32[2,16]{1,0:T(2,128)S(1)} %pad_maximum_fusion.1) | copy-start | bytes 388
  63.8 12.3 %copy-start.8 = (f32[2,512]{1,0:T(2,128)}, f32[2,512]{1,0:T(2,128)S(1)}, u32[]{:S(2)}) copy-start(f32[2,512]{1,0:T(2,128)S(1)} %dynamic_update_slice.3.depth_ref) | copy-start | bytes 12292
  76.1 24.4 %copy-start.4 = (s32[1,512]{1,0:T(1,128)S(1)}, s32[1,512]{1,0:T(1,128)}, u32[]{:S(2)}) copy-start(s32[1,512]{1,0:T(1,128)} %copy-done.3) | copy-start | bytes 6148
  90.3 16.3 %all-to-all-start.1 = ((f32[32,4,512]{2,1,0:T(4,128)}), f32[32,4,512]{2,1,0:T(4,128)S(1)}, u32[]{:S(2)}, u32[]{:S(2)}) async-start(f32[32,4,512]{2,1,0:T(4,128)} %moments.1), calls=%async_computation.1 | async-start | bytes 524288 | tf_op jit(solution)/shard_map/all_to_all | solution.py:396
  97.9 3.3 %collective-permute-start.3 = (f32[2,512]{1,0:T(2,128)S(1)}, f32[2,512]{1,0:T(2,128)S(1)}, u32[]{:S(2)}, u32[]{:S(2)}) collective-permute-start(f32[2,512]{1,0:T(2,128)S(1)} %slice_add_fusion.1.own_ref), channel_id=1, source_target_pairs={{0,96},{32,0},{64,32},{96,64},{1,97},{33,1},{65,33},{97,65},{2,98}... | collective-permute-start | bytes 12296 | tf_op jit(solution)/shard_map/ppermute | solution.py:21
  107.6 3.2 %collective-permute-start.4 = (f32[2,16]{1,0:T(2,128)S(1)}, f32[2,16]{1,0:T(2,128)S(1)}, u32[]{:S(2)}, u32[]{:S(2)}) collective-permute-start(f32[2,16]{1,0:T(2,128)S(1)} %constant_dynamic-slice_fusion.1), channel_id=1, source_target_pairs={{0,96},{32,0},{64,32},{96,64},{1,97},{33,1},{65,33},{97,65},{2,98}... | collective-permute-start | bytes 392 | tf_op jit(solution)/shard_map/ppermute | solution.py:21

commit v4 on v3

--- a/solution.py
+++ b/solution.py
@@ -8,9 +8,6 @@
 from jax.experimental import pallas as pl
 from jax.experimental.pallas import tpu as pltpu
 from jax.sharding import PartitionSpec as P
-
-STEPS = 2
-
 
 epsilon = 1e-06
 relax_rate = 0.1
@@ -129,8 +126,8 @@
     return pl.BlockSpec(table.shape, lambda i: (0,) * table.ndim)
 
 
-def call_params():
-    return pltpu.CompilerParams(vmem_limit_bytes=60 * 1024 * 1024)
+def call_params(megabytes=32):
+    return pltpu.CompilerParams(vmem_limit_bytes=megabytes * 1024 * 1024)
 
 
 def spectra_of(images, tables, batch=4):
@@ -188,9 +185,11 @@
     return jnp.stack([along_rows, along_cols], 0)
 
 
-def lines_kernel(images_ref, note_ref, table_ref, out_ref, held, lines, read_sems, write_sems):
-    devices, slots, rows, _ = out_ref.shape
-    count = slots - 1
+def lines_kernel(
+    images_ref, start_ref, table_ref, out_ref, held, lines, note, read_sems, write_sems
+):
+    devices, slots, rows, columns = out_ref.shape
+    count = slots // 2
     chunks = read_sems.shape[0]
     batch = count // chunks
 
@@ -200,15 +199,29 @@
 
     for chunk in range(chunks):
         read(chunk).start()
+
+    height, nodes = start_ref.shape
+    note[...] = jnp.zeros_like(note)
+    rest = start_ref[...]
+    for part in range(3):
+        rounded = rest.astype(jnp.bfloat16).astype(jnp.float32)
+        note[part * height : (part + 1) * height, :nodes] = rounded
+        rest = rest - rounded
+    packed = note[...].astype(jnp.bfloat16)
+    for device in range(devices):
+        lines[device, 2 * count] = packed
+
     writes = []
 
-    def write(source, target):
-        copy = pltpu.make_async_copy(source, target, write_sems.at[len(writes)])
+    def write(first, number):
+        part = pl.ds(first, number)
+        copy = pltpu.make_async_copy(
+            lines.at[:, part], out_ref.at[:, part], write_sems.at[len(writes)]
+        )
         copy.start()
         writes.append(copy)
 
-    for device in range(devices):
-        write(note_ref, out_ref.at[device, count])
+    write(2 * count, 1)
     table = table_ref[...]
     for chunk in range(chunks):
         read(chunk).wait()
@@ -221,58 +234,60 @@
             for core, values in enumerate((across, down)):
                 values = values.astype(jnp.bfloat16)
                 for chip in range(devices // 2):
-                    lines[2 * chip + core, strip] = values[chip * rows : (chip + 1) * rows]
-        strips = pl.ds(chunk * batch, batch)
-        for device in range(devices):
-            write(lines.at[device, strips], out_ref.at[device, strips])
+                    piece = values[chip * rows : (chip + 1) * rows]
+                    lines[2 * chip + core, strip] = piece[:, :columns]
+                    lines[2 * chip + core, count + strip] = piece[:, columns:]
+        write(chunk * batch, batch)
+        write(count + chunk * batch, batch)
     for copy in writes:
         copy.wait()
 
 
-def lines_of(images, note, table, devices, chunks=4):
+def lines_of(images, start, table, devices, chunks=4):
     count, length = images.shape[0], images.shape[-1]
     rows = 2 * length // devices
+    shape = (devices, 2 * count + 1, rows, length // 2)
+    vmem = pl.BlockSpec(memory_space=pltpu.VMEM)
     return pl.pallas_call(
         lines_kernel,
-        in_specs=[
-            pl.BlockSpec(memory_space=pl.ANY),
-            pl.BlockSpec(memory_space=pltpu.VMEM),
-            pl.BlockSpec(memory_space=pltpu.VMEM),
-        ],
+        in_specs=[pl.BlockSpec(memory_space=pl.ANY), vmem, vmem],
         out_specs=pl.BlockSpec(memory_space=pl.ANY),
-        out_shape=jax.ShapeDtypeStruct((devices, count + 1, rows, length), jnp.bfloat16),
+        out_shape=jax.ShapeDtypeStruct(shape, jnp.bfloat16),
         scratch_shapes=[
             pltpu.VMEM(images.shape, images.dtype),
-            pltpu.VMEM((devices, count, rows, length), jnp.bfloat16),
+            pltpu.VMEM(shape, jnp.bfloat16),
+            pltpu.VMEM((rows, length // 2), jnp.float32),
             pltpu.SemaphoreType.DMA((chunks,)),
-            pltpu.SemaphoreType.DMA(((chunks + 1) * devices,)),
+            pltpu.SemaphoreType.DMA((2 * chunks + 1,)),
         ],
-        compiler_params=call_params(),
+        compiler_params=call_params(60),
+        cost_estimate=pl.CostEstimate(
+            flops=count * 4 * length**3, bytes_accessed=count * 6 * length**2, transcendentals=0
+        ),
         name="lines",
-    )(images, note, table)
+    )(images, start, table)
 
 
 def moments_kernel(
-    partner_ref, lines_ref, masks_ref, chosen_ref, both_ref, weights_ref, depth_ref, out_ref,
-    held, spectra, extra, profile, read_sems,
+    partner_ref, place_ref, lines_ref, chosen_ref, both_ref, weights_ref, counts_ref, rest_ref, out_ref,
+    spectra, extra, profile,
 ):
-    tiles, slots, rows, length = lines_ref.shape
-    count = slots - 1
+    tiles, slots, rows, columns = lines_ref.shape
+    count, length = slots // 2, 2 * columns
     half = rows // 2
-    chunks = read_sems.shape[0]
-    batch = tiles // chunks
-
-    def read(chunk):
-        part = pl.ds(chunk * batch, batch)
-        return pltpu.make_async_copy(lines_ref.at[part], held.at[part], read_sems.at[chunk])
-
-    for chunk in range(chunks):
-        read(chunk).start()
+    unroll = math.gcd(tiles, 8)
     both = both_ref[...]
-    plain, scale = masks_ref[0:half], masks_ref[half:rows]
+    place = place_ref[0]
+    on_first = (place < 2 * count).astype(jnp.int32)
+    special = (lax.broadcasted_iota(jnp.int32, (half, length), 0) == 0) & (on_first == 1)
+    plain = jnp.where(special, 0.0, 1.0)
+    scale = jnp.where(special, 1.0, 2.0)
 
     def transform(tile):
-        mixed = dot(held[tile, :count].reshape(count * rows, length), both)
+        lines = jnp.concatenate(
+            [lines_ref[tile, :count], lines_ref[tile, count : 2 * count]], 2
+        )
+        mixed = dot(lines.reshape(count * rows, length), both)
         mixed = mixed.reshape(count, rows, 2 * length)
         cos_re, sin_re = mixed[:, :half, :length], mixed[:, :half, length:]
         cos_im, sin_im = mixed[:, half:, :length], mixed[:, half:, length:]
@@ -281,13 +296,10 @@
         spectra[pl.ds(at, count)] = fields.astype(jnp.bfloat16)
         extra[pl.ds(at, count), :] = mixed[:, half, :].astype(jnp.bfloat16)
 
-    for chunk in range(chunks):
-        read(chunk).wait()
-
-        @pl.loop(0, batch // 2)
-        def _(pair):
-            transform(chunk * batch + 2 * pair)
-            transform(chunk * batch + 2 * pair + 1)
+    @pl.loop(0, tiles // unroll)
+    def _(step):
+        for k in range(unroll):
+            transform(step * unroll + k)
 
     def surfaces(tile):
         at = pl.multiple_of(tile * count, count)
@@ -302,10 +314,10 @@
         imag = mixed[:, :half, length:] + mixed[:, half:, :length]
         profile[pl.ds(at, count), :] = jnp.sum((real * real + imag * imag) * scale, axis=1)
 
-    @pl.loop(0, tiles // 2)
-    def _(pair):
-        surfaces(2 * pair)
-        surfaces(2 * pair + 1)
+    @pl.loop(0, tiles // unroll)
+    def _(step):
+        for k in range(unroll):
+            surfaces(step * unroll + k)
 
     second = extra[...]
     first = dot(chosen_ref[...], second)
@@ -315,7 +327,7 @@
     real = dot((a * c + b * d).astype(jnp.bfloat16), both[:, :length])
     imag = dot((b * c - a * d).astype(jnp.bfloat16), both[:, length:])
     last = real - imag
-    profile[...] += last * last * masks_ref[rows : rows + 1]
+    profile[...] += last * last * on_first.astype(jnp.float32)
     sums = lax.dot_general(
         weights_ref[...],
         profile[...],
@@ -323,110 +335,53 @@
         precision=lax.Precision.HIGHEST,
         preferred_element_type=jnp.float32,
     )
-    sums = jnp.concatenate([sums[0:2], depth_ref[...]], 0)
+    linked = jnp.zeros((rows, columns), jnp.float32)
+    for tile in range(tiles):
+        linked += dot(lines_ref[tile, 2 * count], counts_ref[tile])
+    linked = (linked[4:6] + linked[2:4]) + linked[0:2]
+    base = jnp.concatenate([rest_ref[0:2] + relax_rate * linked, rest_ref[2:8]], 0)
+    base = jnp.concatenate([base, jnp.zeros((8, tiles * count - columns), jnp.float32)], 1)
+    base = pltpu.roll(base, place, 1)
+    sums = jnp.concatenate([sums[0:2], base[0:2]], 0)
     for tile in range(tiles):
         out_ref[tile] = sums
 
 
-def moments_of(lines, partner, first_chip, depth, both, chunks=8):
-    tiles, slots, rows, length = lines.shape
-    count = slots - 1
+def moments_of(lines, partner, place, links, rest, both):
+    tiles, slots, rows, columns = lines.shape
+    count, length = slots // 2, 2 * columns
     nodes = tiles * count
-    half = rows // 2
-    special = first_chip & (jnp.arange(half) == 0)
-    masks = jnp.concatenate(
-        [jnp.where(special, 0.0, 1.0), jnp.where(special, 1.0, 2.0), jnp.where(first_chip, 1.0, 0.0)[None]]
-    )
-    masks = jnp.broadcast_to(jnp.pad(masks, (0, half - 1))[:, None], (3 * half, length))
     chosen = (partner[:, None] == jnp.arange(nodes)).astype(jnp.bfloat16)
     weights = np.zeros((8, length), np.float32)
     weights[0] = 1.0
     weights[1] = offsets_of(length)
+    lanes = np.arange(columns)
+    sources = jnp.asarray(np.where(lanes < count, np.arange(tiles)[:, None] * count + lanes, -1))
+    links = jnp.pad(links, ((0, 0), (0, columns - count)), constant_values=nodes)
+    counts = sum(sources[:, :, None] == links[k] for k in range(links.shape[0])).astype(jnp.bfloat16)
+    rest = jnp.pad(rest, ((0, 8 - rest.shape[0]), (0, columns - count)))
     vmem = pl.BlockSpec(memory_space=pltpu.VMEM)
+    smem = pl.BlockSpec(memory_space=pltpu.SMEM)
     return pl.pallas_call(
         moments_kernel,
-        in_specs=[
-            pl.BlockSpec(memory_space=pltpu.SMEM),
-            pl.BlockSpec(memory_space=pl.ANY),
-            vmem,
-            vmem,
-            vmem,
-            vmem,
-            vmem,
-        ],
+        in_specs=[smem, smem, vmem, vmem, vmem, vmem, vmem, vmem],
         out_specs=vmem,
         out_shape=jax.ShapeDtypeStruct((tiles, 4, nodes), jnp.float32),
         scratch_shapes=[
-            pltpu.VMEM(lines.shape, lines.dtype),
             pltpu.VMEM((nodes, rows, length), jnp.bfloat16),
             pltpu.VMEM((nodes, 2 * length), jnp.bfloat16),
             pltpu.VMEM((nodes, length), jnp.float32),
-            pltpu.SemaphoreType.DMA((chunks,)),
         ],
         compiler_params=call_params(),
         cost_estimate=pl.CostEstimate(
             flops=nodes * rows * 4 * 2 * length**2, bytes_accessed=2 * lines.size, transcendentals=0
         ),
         name="moments",
-    )(partner, lines, masks, chosen, both, jnp.asarray(weights), depth)
-
-
-def pull_kernel(parts_ref, links_ref, own_ref, near_ref, out_ref):
-    nodes = own_ref.shape[1]
-    links = links_ref.shape[0]
-    sources = lax.broadcasted_iota(jnp.int32, (nodes, nodes), 0)
-    table = jnp.zeros((nodes, nodes), jnp.float32)
-    for k in range(links):
-        table += jnp.where(sources == links_ref[k : k + 1, :], 1.0, 0.0)
-    sums = dot(parts_ref[...], table.astype(jnp.bfloat16))
-    linked = (sums[4:6] + sums[2:4]) + sums[0:2]
-    out_ref[...] = (linked - links * own_ref[...]) + (near_ref[...] - own_ref[...])
-
-
-def pull_all(parts, links, own, near):
-    return pl.pallas_call(
-        pull_kernel,
-        out_shape=jax.ShapeDtypeStruct(own.shape, jnp.float32),
-        compiler_params=pltpu.CompilerParams(vmem_limit_bytes=32 * 1024 * 1024),
-        name="pull",
-    )(parts, links, own, near)
+    )(partner, place[None], lines, chosen, both, jnp.asarray(weights), counts, rest)
 
 
 def exchange(x):
     return lax.all_to_all(x, "tile", split_axis=0, concat_axis=0, tiled=True)
-
-
-def in_parts(values):
-    parts = []
-    rest = values
-    for _ in range(3):
-        part = lax.reduce_precision(rest, 8, 7)
-        parts.append(part.astype(jnp.bfloat16))
-        rest = rest - part
-    return jnp.concatenate(parts, 0)
-
-
-def note_of(start, links, rows, length):
-    first = jnp.concatenate([in_parts(start), (links // 2).astype(jnp.bfloat16)], 0)
-    second = (links % 2).astype(jnp.bfloat16)
-    half = length // 2
-
-    def padded(values):
-        return jnp.pad(values, ((0, rows - values.shape[0]), (0, half - values.shape[1])))
-
-    return jnp.concatenate([padded(first), padded(second)], 1)
-
-
-def read_notes(notes, components, links, count):
-    half = notes.shape[2] // 2
-    first = notes[:, :, :count].transpose(1, 0, 2).reshape(notes.shape[1], -1)
-    second = notes[:, :links, half : half + count].transpose(1, 0, 2).reshape(links, -1)
-    height = 3 * components
-    parts = first[:height]
-    values = parts.astype(jnp.float32)
-    start = (values[2 * components :] + values[components : 2 * components]) + values[:components]
-    linked = 2 * first[height : height + links].astype(jnp.int32) + second.astype(jnp.int32)
-    return parts, start, linked
 
 
 def per_device(strips, partner_tile, partner_strip, adjacency, start_positions):
@@ -445,43 +400,36 @@
     rows = 2 * length // tiles
     order = np.arange(length).reshape(2, tiles // 2, rows // 2).transpose(1, 0, 2).reshape(-1)
     line_table = tables[0].T[order]
-    lines = exchange(lines_of(own, note_of(start, links, rows, length), line_table, tiles))
+    lines = exchange(lines_of(own, start, line_table, tiles))
 
     near_low = shifted(own[:half_strips], "sec", -1)
     back_high = shifted(own[half_strips:], "sec", 1)
-    fields = spectra_of(own, tables)
+    strips_here, near_low, back_high = lax.optimization_barrier((own, near_low, back_high))
+    fields = spectra_of(strips_here, tables)
     low = flows_of(pair_sums(near_low, fields, 0, True, tables))
     high = flows_of(pair_sums(back_high, fields, half_strips, False, tables))
     depth_out = jnp.concatenate([low, shifted(high, "sec", -1)], 1)
-    depth_row = lax.dynamic_update_slice(
-        jnp.zeros((2, tiles * per_tile), jnp.float32), depth_out, (0, place)
-    )
-
-    shares = moments_of(lines, partner, tile_index < 2, depth_row, both)
-    parts, whole_start, whole_links = read_notes(
-        lines[:, per_tile], start.shape[0], links.shape[0], per_tile
-    )
-    whole_links = jnp.concatenate([whole_links, partner[None]], 0)
-    first_pull = pull_all(parts, whole_links, whole_start, shifted(whole_start, "sec", -1))
-
-    received = exchange(shares).reshape(tiles // 2, 2, 4, tiles * per_tile)
-    summed = jnp.sum(received, axis=0)
-    plane_all = summed[:, 1] / length / (summed[:, 0] / length + epsilon)
-    depth_all = summed[0, 2:] + summed[1, 2:]
-    flow_all = plane_all + depth_all
-    current = whole_start + relax_rate * (first_pull + flow_all)
 
     def mine(values):
         return lax.dynamic_slice_in_dim(values, place, per_tile, 1)
 
-    my_links = jnp.concatenate([links, mine(partner[None])], 0)
-    for iteration in range(1, STEPS):
-        here = mine(current)
-        linked = jnp.sum(current[:, my_links], axis=1)
-        near = shifted(here, "sec", -1)
-        force = (linked - my_links.shape[0] * here) + (near - here) + mine(flow_all)
-        here = here + relax_rate * force
-    return (mine(plane_all)[:, None, :], depth_out[:, None, :], here[:, None, :])
+    links = jnp.concatenate([links, mine(partner[None])], 0)
+    number = links.shape[0]
+    near = shifted(start, "sec", -1)
+    rest = start + relax_rate * ((near - start) - number * start + depth_out)
+
+    shares = exchange(moments_of(lines, partner, place, links, rest, both))
+    summed = jnp.sum(shares.reshape(tiles // 2, 2, 4, tiles * per_tile), axis=0)
+    plane_all = summed[:, 1] / length / (summed[:, 0] / length + epsilon)
+    current = summed[0, 2:] + summed[1, 2:] + relax_rate * plane_all
+
+    plane_out, here = mine(plane_all), mine(current)
+    linked = jnp.sum(current[:, links], axis=1)
+    near = shifted(here, "sec", -1)
+    here = here + relax_rate * (
+        (linked - number * here) + (near - here) + plane_out + depth_out
+    )
+    return (plane_out[:, None, :], depth_out[:, None, :], here[:, None, :])
 
 
 def solution(mesh):

time: 112 us -> 102 us (0.911)
  Pallas kernels: 37.8 us -> 27.5 us
  waiting for transfers between devices: 32.3 us -> 41 us
  local copies, waits for them, and re-layouts: 7.19 us -> 2.82 us
  starting transfers between devices: 28.2 us -> 23.9 us
    ppermute x5, waiting for transfers between devices: 17.2 us -> 23 us  [shifted(): lax.ppermute(x, axis, [(i, (i + by) % devices) for i in range(devices)])]
    ppermute x5, starting transfers between devices: 11.1 us -> 6.92 us  [shifted(): lax.ppermute(x, axis, [(i, (i + by) % devices) for i in range(devices)])]
    pallas_call x2 -> x1, Pallas kernels: 15 us -> 11.4 us  [moments_of(): pl.pallas_call(moments_kernel, in_specs=[smem, smem, vmem, vmem, vmem, vm...]
    pallas_call x1, Pallas kernels: 5.59 us -> 2.64 us  [spectra_of(): pl.pallas_call(spectra_kernel, grid=(count // batch,), in_specs=[pl.Block...]
    all_to_all x2, waiting for transfers between devices: 15.1 us -> 18 us  [exchange(): return lax.all_to_all(x, 'tile', split_axis=0, concat_axis=0, tiled=True)]
    pallas_call x2, Pallas kernels: 10.6 us -> 8.48 us  [pair_sums(): pl.pallas_call(functools.partial(pair_kernel, other_first), grid=(count /...]
    pallas_call x1, Pallas kernels: 6.53 us -> 5.04 us  [lines_of(): pl.pallas_call(lines_kernel, in_specs=[pl.BlockSpec(memory_space=pl.ANY),...]
    convert_element_type x3 -> x1, other arithmetic: 1.39 us -> 2.74 us  [moments_of(): sum((sources[:, :, None] == links[k] for k in range(links.shape[0])))]
  transfers between devices with their start and end apart: 7 -> 7, of which waited for: 5 -> 5; matrix products, arithmetic and copies ran while one was open for 5% -> 7% of each run, Pallas kernels for 15% -> 11%
where the time goes in v4:
time: 102 us; the launch traced here: 101 us
  waiting for transfers between devices  41 us (40%)
  Pallas kernels  27.5 us (27%)
  starting transfers between devices  23.9 us (23%)
  other arithmetic  4.92 us (5%)
  local copies, waits for them, and re-layouts  2.82 us (3%)
    ppermute x5, waiting for transfers between devices, shifted(): lax.ppermute(x, axis, [(i, (i + by) % devices) for i in range(devices)])  23 us
    all_to_all x2, waiting for transfers between devices, exchange(): return lax.all_to_all(x, 'tile', split_axis=0, concat_axis=0, tiled=True)  18 us
    all_to_all x2, starting transfers between devices, exchange(): return lax.all_to_all(x, 'tile', split_axis=0, concat_axis=0, tiled=True)  17 us
    pallas_call x1, Pallas kernels, moments_of(): pl.pallas_call(moments_kernel, in_specs=[smem, smem, vmem, vmem, vmem, vm...  11.4 us
    pallas_call x2, Pallas kernels, pair_sums(): pl.pallas_call(functools.partial(pair_kernel, other_first), grid=(count /...  8.48 us
    ppermute x5, starting transfers between devices, shifted(): lax.ppermute(x, axis, [(i, (i + by) % devices) for i in range(devices)])  6.92 us
    pallas_call x1, Pallas kernels, lines_of(): pl.pallas_call(lines_kernel, in_specs=[pl.BlockSpec(memory_space=pl.ANY),...  5.04 us
    convert_element_type x1, other arithmetic, moments_of(): sum((sources[:, :, None] == links[k] for k in range(links.shape[0])))  2.74 us
  transfers between devices with their start and end apart: 7, of which 5 were waited for; matrix products, arithmetic and copies ran while one was open for 7% of the time, Pallas kernels for 11%

profile of v4, /device:TPU:1, one launch (start us, length us, event | category | flops | bytes accessed | tf_op | source)
XLA Modules:
  0.0 101.1 jit_solution(6370494254977250955)
XLA Ops:
  0.6 5.0 %lines.1 = bf16[32,33,16,128]{3,2,1,0:T(8,128)(2,1)} custom-call(bf16[16,256,256]{2,1,0:T(8,128)(2,1)} %bitcast.75, f32[2,16]{1,0:T(2,128)} %bitcast.84, bf16[256,256]{1,0:T(8,128)(2,1)} %constant.75.table_ref), custom_call_target="tpu_custom_call" | custom-call | flops 1073741824 | bytes 6291456 | tf_op jit(solution)/shard_map/lines/pallas_call | solution.py:251
  5.7 9.8 %all-to-all-start = ((bf16[32,33,16,128]{3,2,1,0:T(8,128)(2,1)}), bf16[32,33,16,128]{3,2,1,0:T(8,128)(2,1)}, u32[]{:S(2)}, u32[]{:S(2)}) async-start(bf16[32,33,16,128]{3,2,1,0:T(8,128)(2,1)} %lines.1), calls=%async_computation | async-start | bytes 8650752 | tf_op jit(solution)/shard_map/all_to_all | solution.py:384
  15.6 2.5 %collective-permute-start = (f32[2,16]{1,0:T(2,128)S(1)}, f32[2,16]{1,0:T(2,128)S(1)}, u32[]{:S(2)}, u32[]{:S(2)}) collective-permute-start(f32[2,16]{1,0:T(2,128)S(1)} %bitcast.85), channel_id=1, source_target_pairs={{0,96},{32,0},{64,32},{96,64},{1,97},{33,1},{65,33},{97,65},{2,98}... | collective-permute-start | bytes 392 | tf_op jit(solution)/shard_map/ppermute | solution.py:18
  18.1 1.4 %slice_bitcast_fusion = (bf16[8,256,256]{2,1,0:T(8,128)(2,1)}, bf16[8,256,256]{2,1,0:T(8,128)(2,1)}) fusion(bf16[1,16,256,256]{3,2,1,0:T(8,128)(2,1)S(1)} %copy-done), kind=kLoop, calls=%fused_computation.2 | loop fusion | bytes 4194304 | tf_op jit(solution)/shard_map/slice | solution.py:406
  19.6 0.5 collective-permute-start.1
  20.1 0.9 collective-permute-start.2
  21.1 0.1 constant_dynamic-slice_fusion.2
  21.2 1.0 fusion.chosen_ref
  22.2 2.7 %add_convert_fusion.counts_ref = bf16[32,128,128]{2,1,0:T(8,128)(2,1)S(1)} fusion(s32[128]{0:T(128)S(1)} %get-tuple-element.39, s32[128]{0:T(128)S(1)} %get-tuple-element.38, s32[128]{0:T(128)S(1)} %get-tuple-element.37, s32[128]{0:T(128)S(1)} %get-tuple-element.36, s32[128]{0:T(128)S(1)} %get-tuple-element.35, s32[128]{0:T(128)S(1)} %get-tuple-element.34, ...), kind=kLoop, calls=%fused_computation.1 | loop fusion | flops 11010048 | bytes 1068544 | tf_op jit(solution)/shard_map/convert_element_type | solution.py:361
  24.9 19.1 %collective-permute-done.1.images_ref = bf16[8,256,256]{2,1,0:T(8,128)(2,1)} collective-permute-done((bf16[8,256,256]{2,1,0:T(8,128)(2,1)}, bf16[8,256,256]{2,1,0:T(8,128)(2,1)}, u32[]{:S(2)}, u32[]{:S(2)}) %collective-permute-start.1) | collective-permute-done | bytes 1048608 | tf_op jit(solution)/shard_map/ppermute | solution.py:18
  44.0 1.4 %collective-permute-done.2.images_ref = bf16[8,256,256]{2,1,0:T(8,128)(2,1)} collective-permute-done((bf16[8,256,256]{2,1,0:T(8,128)(2,1)}, bf16[8,256,256]{2,1,0:T(8,128)(2,1)}, u32[]{:S(2)}, u32[]{:S(2)}) %collective-permute-start.2) | collective-permute-done | bytes 1048608 | tf_op jit(solution)/shard_map/ppermute | solution.py:18
  45.5 2.6 %spectra.1.fields_ref = bf16[16,2,256,256]{3,2,1,0:T(8,128)(2,1)S(1)} custom-call(bf16[16,256,256]{2,1,0:T(8,128)(2,1)S(1)} %bitcast.76, bf16[256,256]{1,0:T(8,128)(2,1)S(1)} %copy-done.2, bf16[512,256]{1,0:T(8,128)(2,1)S(1)} %copy-done.1), custom_call_target="tpu_custom_call" | custom-call | flops 1610612736 | bytes 6291456 | tf_op jit(solution)/shard_map/spectra/pallas_call | solution.py:136
  48.1 0.1 broadcast_in_dim.14.offsets_ref
  48.2 4.2 %pair_sums.3 = f32[8,8,256]{2,1,0:T(8,128)S(1)} custom-call(bf16[8,256,256]{2,1,0:T(8,128)(2,1)} %collective-permute-done.2.images_ref, bf16[16,2,256,256]{3,2,1,0:T(8,128)(2,1)S(1)} %spectra.1.fields_ref, bf16[256,256]{1,0:T(8,128)(2,1)S(1)} %copy-done.2, bf16[512,256]{1,0:T(8,128)(2,1)S(1)} %copy-done.1, bf16[256,256]{1,0:T(8,128)(2,1)S(1)} %copy-done.3, ...), custom_call_target="tpu_custom_call" | custom-call | flops 1610612736 | bytes 3145728 | tf_op jit(solution)/shard_map/pair_sums/pallas_call | solution.py:158
  52.5 4.3 %pair_sums.2 = f32[8,8,256]{2,1,0:T(8,128)S(1)} custom-call(bf16[8,256,256]{2,1,0:T(8,128)(2,1)} %collective-permute-done.1.images_ref, bf16[16,2,256,256]{3,2,1,0:T(8,128)(2,1)S(1)} %spectra.1.fields_ref, bf16[256,256]{1,0:T(8,128)(2,1)S(1)} %copy-done.2, bf16[512,256]{1,0:T(8,128)(2,1)S(1)} %copy-done.1, bf16[256,256]{1,0:T(8,128)(2,1)S(1)} %copy-done.3, ...), custom_call_target="tpu_custom_call" | custom-call | flops 1610612736 | bytes 3145728 | tf_op jit(solution)/shard_map/pair_sums/pallas_call | solution.py:158
  56.8 0.2 slice_reduce_fusion
  56.9 0.1 fusion.2
  57.1 0.4 collective-permute-start.3
  57.5 2.5 %collective-permute-done.3 = f32[2,8]{1,0:T(2,128)S(1)} collective-permute-done((f32[2,8]{1,0:T(2,128)S(1)}, f32[2,8]{1,0:T(2,128)S(1)}, u32[]{:S(2)}, u32[]{:S(2)}) %collective-permute-start.3) | collective-permute-done | bytes 96 | tf_op jit(solution)/shard_map/ppermute | solution.py:18
  60.0 0.1 multiply_add_fusion.1
  60.1 9.2 %all-to-all-done.lines_ref = bf16[32,33,16,128]{3,2,1,0:T(8,128)(2,1)} async-done(((bf16[32,33,16,128]{3,2,1,0:T(8,128)(2,1)}), bf16[32,33,16,128]{3,2,1,0:T(8,128)(2,1)}, u32[]{:S(2)}, u32[]{:S(2)}) %all-to-all-start) | async-done | bytes 4325408 | tf_op jit(solution)/shard_map/all_to_all | solution.py:384
  69.3 11.4 %moments.1 = f32[32,4,512]{2,1,0:T(4,128)} custom-call(s32[512]{0:T(512)S(1)} %bitcast.78, s32[1]{0:T(128)} %bitcast.1.place_ref, bf16[32,33,16,128]{3,2,1,0:T(8,128)(2,1)} %all-to-all-done.lines_ref, bf16[512,512]{1,0:T(8,128)(2,1)S(1)} %copy-done.4, bf16[256,512]{1,0:T(8,128)(2,1)S(1)} %copy-done.5, f32[8,256]{1,0:T(8,128)S(1)} %copy-done.6, ...), custom_call_target="tpu_custom_call" | custom-call | flops 4294967296 | bytes 4325376 | tf_op jit(solution)/shard_map/moments/pallas_call | solution.py:365
  80.7 7.2 %all-to-all-start.1 = ((f32[32,4,512]{2,1,0:T(4,128)}), f32[32,4,512]{2,1,0:T(4,128)S(1)}, u32[]{:S(2)}, u32[]{:S(2)}) async-start(f32[32,4,512]{2,1,0:T(4,128)} %moments.1), calls=%async_computation.1 | async-start | bytes 524288 | tf_op jit(solution)/shard_map/all_to_all | solution.py:384
  87.9 0.1 fusion.26
  88.0 0.1 reshape.228
  88.1 8.8 %all-to-all-done.1 = f32[32,4,512]{2,1,0:T(4,128)S(1)} async-done(((f32[32,4,512]{2,1,0:T(4,128)}), f32[32,4,512]{2,1,0:T(4,128)S(1)}, u32[]{:S(2)}, u32[]{:S(2)}) %all-to-all-start.1) | async-done | bytes 262176 | tf_op jit(solution)/shard_map/all_to_all | solution.py:384
  97.0 0.1 copy.27
  97.1 0.1 constant_dynamic-slice_fusion
  97.2 2.5 %collective-permute-start.4 = (f32[2,16]{1,0:T(2,128)S(1)}, f32[2,16]{1,0:T(2,128)S(1)}, u32[]{:S(2)}, u32[]{:S(2)}) collective-permute-start(f32[2,16]{1,0:T(2,128)S(1)} %constant_dynamic-slice_fusion), channel_id=1, source_target_pairs={{0,96},{32,0},{64,32},{96,64},{1,97},{33,1},{65,33},{97,65},{2,98}... | collective-permute-start | bytes 392 | tf_op jit(solution)/shard_map/ppermute | solution.py:18
  99.7 0.6 gather_fusion
  100.4 0.1 copy.28
  100.5 0.6 fusion.11
  (42 shorter events, 0.3 us)
Async XLA Ops:
  5.7 9.8 %copy-start.10 = (f32[2,1,16]{2,1,0:T(1,128)S(1)}, f32[2,1,16]{2,1,0:T(1,128)}, u32[]{:S(2)}) copy-start(f32[2,1,16]{2,1,0:T(1,128)} %param.20) | copy-start | bytes 388
  5.7 12.4 %copy-start = (bf16[1,16,256,256]{3,2,1,0:T(8,128)(2,1)S(1)}, bf16[1,16,256,256]{3,2,1,0:T(8,128)(2,1)}, u32[]{:S(2)}) copy-start(bf16[1,16,256,256]{3,2,1,0:T(8,128)(2,1)} %param.16) | copy-start | bytes 6291460
  5.7 63.6 %all-to-all-start = ((bf16[32,33,16,128]{3,2,1,0:T(8,128)(2,1)}), bf16[32,33,16,128]{3,2,1,0:T(8,128)(2,1)}, u32[]{:S(2)}, u32[]{:S(2)}) async-start(bf16[32,33,16,128]{3,2,1,0:T(8,128)(2,1)} %lines.1), calls=%async_computation | async-start | bytes 8650752 | tf_op jit(solution)/shard_map/all_to_all | solution.py:384
  15.5 5.5 %copy-start.7 = (s32[6,1,16]{2,1,0:T(1,128)S(1)}, s32[6,1,16]{2,1,0:T(1,128)}, u32[]{:S(2)}) copy-start(s32[6,1,16]{2,1,0:T(1,128)} %param.19) | copy-start | bytes 1156
  15.5 5.5 %copy-start.11 = (s32[1,512]{1,0:T(1,128)S(1)}, s32[1,512]{1,0:T(1,128)}, u32[]{:S(2)}) copy-start(s32[1,512]{1,0:T(1,128)} %param.18) | copy-start | bytes 6148
  15.5 5.5 %copy-start.12 = (s32[1,512]{1,0:T(1,128)S(1)}, s32[1,512]{1,0:T(1,128)}, u32[]{:S(2)}) copy-start(s32[1,512]{1,0:T(1,128)} %param.17) | copy-start | bytes 6148
  15.5 29.9 %copy-start.1 = (bf16[512,256]{1,0:T(8,128)(2,1)S(1)}, bf16[512,256]{1,0:T(8,128)(2,1)}, u32[]{:S(2)}) copy-start(bf16[512,256]{1,0:T(8,128)(2,1)} %constant.57.clone.both_ref) | copy-start | bytes 786436
  15.6 29.9 %copy-start.2 = (bf16[256,256]{1,0:T(8,128)(2,1)S(1)}, bf16[256,256]{1,0:T(8,128)(2,1)}, u32[]{:S(2)}) copy-start(bf16[256,256]{1,0:T(8,128)(2,1)} %constant.56.clone.to_half_ref) | copy-start | bytes 393220
  15.6 41.9 %collective-permute-start = (f32[2,16]{1,0:T(2,128)S(1)}, f32[2,16]{1,0:T(2,128)S(1)}, u32[]{:S(2)}, u32[]{:S(2)}) collective-permute-start(f32[2,16]{1,0:T(2,128)S(1)} %bitcast.85), channel_id=1, source_target_pairs={{0,96},{32,0},{64,32},{96,64},{1,97},{33,1},{65,33},{97,65},{2,98}... | collective-permute-start | bytes 392 | tf_op jit(solution)/shard_map/ppermute | solution.py:18
  19.6 24.4 %collective-permute-start.1 = (bf16[8,256,256]{2,1,0:T(8,128)(2,1)}, bf16[8,256,256]{2,1,0:T(8,128)(2,1)}, u32[]{:S(2)}, u32[]{:S(2)}) collective-permute-start(bf16[8,256,256]{2,1,0:T(8,128)(2,1)} %get-tuple-element.28), channel_id=1, source_target_pairs={{0,96},{32,0},{64,32},{96,64},{1,97},{33,1},{65,33},{97,65},{2,98}... | collective-permute-start | bytes 3145736 | tf_op jit(solution)/shard_map/ppermute | solution.py:18
  20.1 25.3 %collective-permute-start.2 = (bf16[8,256,256]{2,1,0:T(8,128)(2,1)}, bf16[8,256,256]{2,1,0:T(8,128)(2,1)}, u32[]{:S(2)}, u32[]{:S(2)}) collective-permute-start(bf16[8,256,256]{2,1,0:T(8,128)(2,1)} %get-tuple-element.27), channel_id=1, source_target_pairs={{0,32},{32,64},{64,96},{96,0},{1,33},{33,65},{65,97},{97,1},{2,34}... | collective-permute-start | bytes 3145736 | tf_op jit(solution)/shard_map/ppermute | solution.py:18
  24.9 23.2 %copy-start.8 = (f32[256]{0:T(256)S(1)}, f32[256]{0:T(256)}, u32[]{:S(2)}) copy-start(f32[256]{0:T(256)} %constant.61.clone) | copy-start | bytes 3076
  24.9 23.3 %copy-start.3 = (bf16[256,256]{1,0:T(8,128)(2,1)S(1)}, bf16[256,256]{1,0:T(8,128)(2,1)}, u32[]{:S(2)}) copy-start(bf16[256,256]{1,0:T(8,128)(2,1)} %constant.58.clone.from_half_ref) | copy-start | bytes 393220
  52.5 16.8 %copy-start.4 = (bf16[512,512]{1,0:T(8,128)(2,1)S(1)}, bf16[512,512]{1,0:T(8,128)(2,1)}, u32[]{:S(2)}) copy-start(bf16[512,512]{1,0:T(8,128)(2,1)} %fusion.chosen_ref) | copy-start | bytes 1572868
  52.5 16.8 %copy-start.5 = (bf16[256,512]{1,0:T(8,128)(2,1)S(1)}, bf16[256,512]{1,0:T(8,128)(2,1)}, u32[]{:S(2)}) copy-start(bf16[256,512]{1,0:T(8,128)(2,1)} %constant.78.both_ref) | copy-start | bytes 786436
  52.5 16.8 %copy-start.6 = (f32[8,256]{1,0:T(8,128)S(1)}, f32[8,256]{1,0:T(8,128)}, u32[]{:S(2)}) copy-start(f32[8,256]{1,0:T(8,128)} %constant.63.clone.weights_ref) | copy-start | bytes 24580
  57.1 2.9 %collective-permute-start.3 = (f32[2,8]{1,0:T(2,128)S(1)}, f32[2,8]{1,0:T(2,128)S(1)}, u32[]{:S(2)}, u32[]{:S(2)}) collective-permute-start(f32[2,8]{1,0:T(2,128)S(1)} %pad_maximum_fusion), channel_id=1, source_target_pairs={{0,96},{32,0},{64,32},{96,64},{1,97},{33,1},{65,33},{97,65},{2,98}... | collective-permute-start | bytes 200 | tf_op jit(solution)/shard_map/ppermute | solution.py:18
  60.1 40.4 %copy-start.9 = (f32[2,16]{1,0:T(2,128)}, f32[2,16]{1,0:T(2,128)S(1)}, u32[]{:S(2)}) copy-start(f32[2,16]{1,0:T(2,128)S(1)} %get-tuple-element.26) | copy-start | bytes 388
  80.7 16.2 %all-to-all-start.1 = ((f32[32,4,512]{2,1,0:T(4,128)}), f32[32,4,512]{2,1,0:T(4,128)S(1)}, u32[]{:S(2)}, u32[]{:S(2)}) async-start(f32[32,4,512]{2,1,0:T(4,128)} %moments.1), calls=%async_computation.1 | async-start | bytes 524288 | tf_op jit(solution)/shard_map/all_to_all | solution.py:384
  97.2 3.2 %collective-permute-start.4 = (f32[2,16]{1,0:T(2,128)S(1)}, f32[2,16]{1,0:T(2,128)S(1)}, u32[]{:S(2)}, u32[]{:S(2)}) collective-permute-start(f32[2,16]{1,0:T(2,128)S(1)} %constant_dynamic-slice_fusion), channel_id=1, source_target_pairs={{0,96},{32,0},{64,32},{96,64},{1,97},{33,1},{65,33},{97,65},{2,98}... | collective-permute-start | bytes 392 | tf_op jit(solution)/shard_map/ppermute | solution.py:18

commit v5 on v4

--- a/solution.py
+++ b/solution.py
@@ -275,7 +275,7 @@
     tiles, slots, rows, columns = lines_ref.shape
     count, length = slots // 2, 2 * columns
     half = rows // 2
-    unroll = math.gcd(tiles, 8)
+    unroll = math.gcd(tiles, 16)
     both = both_ref[...]
     place = place_ref[0]
     on_first = (place < 2 * count).astype(jnp.int32)
@@ -339,12 +339,61 @@
     for tile in range(tiles):
         linked += dot(lines_ref[tile, 2 * count], counts_ref[tile])
     linked = (linked[4:6] + linked[2:4]) + linked[0:2]
-    base = jnp.concatenate([rest_ref[0:2] + relax_rate * linked, rest_ref[2:8]], 0)
-    base = jnp.concatenate([base, jnp.zeros((8, tiles * count - columns), jnp.float32)], 1)
-    base = pltpu.roll(base, place, 1)
-    sums = jnp.concatenate([sums[0:2], base[0:2]], 0)
+    base = rest_ref[...] + relax_rate * linked
+    width = count
+    while width < columns:
+        base += pltpu.roll(base, width, 1)
+        width *= 2
+
+    def folded(row):
+        return jnp.concatenate(
+            [sums[row : row + 1, at : at + columns] for at in range(0, tiles * count, columns)], 0
+        )
+
+    packed = jnp.concatenate([folded(0), *two_parts(folded(1)), *two_parts(base)], 0)
+    packed = packed.astype(jnp.bfloat16)
     for tile in range(tiles):
-        out_ref[tile] = sums
+        out_ref[tile] = packed
+
+
+def two_parts(values):
+    high = values.astype(jnp.bfloat16).astype(jnp.float32)
+    return high, values - high
+
+
+def finish_kernel(shares_ref, out_ref):
+    tiles, _, columns = shares_ref.shape
+    nodes = out_ref.shape[1]
+    folds = nodes // columns
+    count = nodes // tiles
+    length = 2 * columns
+    shares = [shares_ref[tile].astype(jnp.float32) for tile in range(tiles)]
+    owner = lax.broadcasted_iota(jnp.int32, (2, columns), 1) // count
+    flows = []
+    for core in range(2):
+        total = sum(shares[core + 2 :: 2], shares[core])
+        moment = total[folds : 2 * folds] + total[2 * folds : 3 * folds]
+        flows.append(moment / length / (total[:folds] / length + epsilon))
+    first = 3 * folds
+    for fold in range(folds):
+        at = pl.ds(fold * columns, columns)
+        base = jnp.zeros((2, columns), jnp.float32)
+        for k in range(columns // count):
+            share = shares[fold * (columns // count) + k]
+            position = share[first : first + 2] + share[first + 2 : first + 4]
+            base += jnp.where(owner == k, position, 0.0)
+        flow = jnp.concatenate([part[fold : fold + 1] for part in flows], 0)
+        out_ref[0:2, at] = flow
+        out_ref[2:4, at] = base + relax_rate * flow
+
+
+def finish(shares, nodes):
+    return pl.pallas_call(
+        finish_kernel,
+        out_shape=jax.ShapeDtypeStruct((4, nodes), jnp.float32),
+        compiler_params=call_params(),
+        name="finish",
+    )(shares)
 
 
 def moments_of(lines, partner, place, links, rest, both):
@@ -359,14 +408,14 @@
     sources = jnp.asarray(np.where(lanes < count, np.arange(tiles)[:, None] * count + lanes, -1))
     links = jnp.pad(links, ((0, 0), (0, columns - count)), constant_values=nodes)
     counts = sum(sources[:, :, None] == links[k] for k in range(links.shape[0])).astype(jnp.bfloat16)
-    rest = jnp.pad(rest, ((0, 8 - rest.shape[0]), (0, columns - count)))
+    rest = jnp.pad(rest, ((0, 0), (0, columns - count)))
     vmem = pl.BlockSpec(memory_space=pltpu.VMEM)
     smem = pl.BlockSpec(memory_space=pltpu.SMEM)
     return pl.pallas_call(
         moments_kernel,
         in_specs=[smem, smem, vmem, vmem, vmem, vmem, vmem, vmem],
         out_specs=vmem,
-        out_shape=jax.ShapeDtypeStruct((tiles, 4, nodes), jnp.float32),
+        out_shape=jax.ShapeDtypeStruct((tiles, 3 * nodes // columns + 4, columns), jnp.bfloat16),
         scratch_shapes=[
             pltpu.VMEM((nodes, rows, length), jnp.bfloat16),
             pltpu.VMEM((nodes, 2 * length), jnp.bfloat16),
@@ -419,9 +468,8 @@
     rest = start + relax_rate * ((near - start) - number * start + depth_out)
 
     shares = exchange(moments_of(lines, partner, place, links, rest, both))
-    summed = jnp.sum(shares.reshape(tiles // 2, 2, 4, tiles * per_tile), axis=0)
-    plane_all = summed[:, 1] / length / (summed[:, 0] / length + epsilon)
-    current = summed[0, 2:] + summed[1, 2:] + relax_rate * plane_all
+    everyone = finish(shares, tiles * per_tile)
+    plane_all, current = everyone[:2], everyone[2:]
 
     plane_out, here = mine(plane_all), mine(current)
     linked = jnp.sum(current[:, links], axis=1)

time: 102 us -> 100 us (0.980)
  waiting for transfers between devices: 41 us -> 39.5 us
    all_to_all x2, waiting for transfers between devices: 18 us -> 16.5 us  [exchange(): return lax.all_to_all(x, 'tile', split_axis=0, concat_axis=0, tiled=True)]
where the time goes in v5:
time: 100 us; the launch traced here: 99.4 us
  waiting for transfers between devices  39.5 us (40%)
  Pallas kernels  27.2 us (27%)
  starting transfers between devices  24.1 us (24%)
  other arithmetic  4.85 us (5%)
  local copies, waits for them, and re-layouts  2.82 us (3%)
    ppermute x5, waiting for transfers between devices, shifted(): lax.ppermute(x, axis, [(i, (i + by) % devices) for i in range(devices)])  23 us
    all_to_all x2, starting transfers between devices, exchange(): return lax.all_to_all(x, 'tile', split_axis=0, concat_axis=0, tiled=True)  17 us
    all_to_all x2, waiting for transfers between devices, exchange(): return lax.all_to_all(x, 'tile', split_axis=0, concat_axis=0, tiled=True)  16.5 us
    pallas_call x1, Pallas kernels, moments_of(): pl.pallas_call(moments_kernel, in_specs=[smem, smem, vmem, vmem, vmem, vm...  10.9 us
    pallas_call x2, Pallas kernels, pair_sums(): pl.pallas_call(functools.partial(pair_kernel, other_first), grid=(count /...  8.48 us
    ppermute x5, starting transfers between devices, shifted(): lax.ppermute(x, axis, [(i, (i + by) % devices) for i in range(devices)])  7.1 us
    pallas_call x1, Pallas kernels, lines_of(): pl.pallas_call(lines_kernel, in_specs=[pl.BlockSpec(memory_space=pl.ANY),...  5.06 us
    convert_element_type x1, other arithmetic, moments_of(): sum((sources[:, :, None] == links[k] for k in range(links.shape[0])))  2.74 us
  transfers between devices with their start and end apart: 7, of which 5 were waited for; matrix products, arithmetic and copies ran while one was open for 7% of the time, Pallas kernels for 11%

profile of v5, /device:TPU:1, one launch (start us, length us, event | category | flops | bytes accessed | tf_op | source)
XLA Modules:
  0.0 99.4 jit_solution(1924236783828008823)
XLA Ops:
  0.6 5.1 %lines.1 = bf16[32,33,16,128]{3,2,1,0:T(8,128)(2,1)} custom-call(bf16[16,256,256]{2,1,0:T(8,128)(2,1)} %bitcast.68, f32[2,16]{1,0:T(2,128)} %bitcast.76, bf16[256,256]{1,0:T(8,128)(2,1)} %constant.68.table_ref), custom_call_target="tpu_custom_call" | custom-call | flops 1073741824 | bytes 6291456 | tf_op jit(solution)/shard_map/lines/pallas_call | solution.py:251
  5.7 9.8 %all-to-all-start = ((bf16[32,33,16,128]{3,2,1,0:T(8,128)(2,1)}), bf16[32,33,16,128]{3,2,1,0:T(8,128)(2,1)}, u32[]{:S(2)}, u32[]{:S(2)}) async-start(bf16[32,33,16,128]{3,2,1,0:T(8,128)(2,1)} %lines.1), calls=%async_computation | async-start | bytes 8650752 | tf_op jit(solution)/shard_map/all_to_all | solution.py:433
  15.6 2.5 %collective-permute-start = (f32[2,16]{1,0:T(2,128)S(1)}, f32[2,16]{1,0:T(2,128)S(1)}, u32[]{:S(2)}, u32[]{:S(2)}) collective-permute-start(f32[2,16]{1,0:T(2,128)S(1)} %bitcast.77), channel_id=1, source_target_pairs={{0,96},{32,0},{64,32},{96,64},{1,97},{33,1},{65,33},{97,65},{2,98}... | collective-permute-start | bytes 392 | tf_op jit(solution)/shard_map/ppermute | solution.py:18
  18.1 1.5 %slice_bitcast_fusion = (bf16[8,256,256]{2,1,0:T(8,128)(2,1)}, bf16[8,256,256]{2,1,0:T(8,128)(2,1)}) fusion(bf16[1,16,256,256]{3,2,1,0:T(8,128)(2,1)S(1)} %copy-done), kind=kLoop, calls=%fused_computation.2 | loop fusion | bytes 4194304 | tf_op jit(solution)/shard_map/slice | solution.py:455
  19.6 0.6 collective-permute-start.1
  20.1 0.9 collective-permute-start.2
  21.1 0.1 constant_dynamic-slice_fusion.2
  21.2 1.0 %fusion.chosen_ref = bf16[512,512]{1,0:T(8,128)(2,1)} fusion(s32[512]{0:T(512)S(1)} %bitcast.70), kind=kLoop, calls=%fused_computation.5 | loop fusion | flops 524288 | bytes 526336 | tf_op jit(solution)/shard_map/convert_element_type | solution.py:403
  22.2 2.7 %add_convert_fusion.counts_ref = bf16[32,128,128]{2,1,0:T(8,128)(2,1)S(1)} fusion(s32[128]{0:T(128)S(1)} %get-tuple-element.37, s32[128]{0:T(128)S(1)} %get-tuple-element.36, s32[128]{0:T(128)S(1)} %get-tuple-element.35, s32[128]{0:T(128)S(1)} %get-tuple-element.34, s32[128]{0:T(128)S(1)} %get-tuple-element.33, s32[128]{0:T(128)S(1)} %get-tuple-element.32, ...), kind=kLoop, calls=%fused_computation.1 | loop fusion | flops 11010048 | bytes 1068544 | tf_op jit(solution)/shard_map/convert_element_type | solution.py:410
  25.0 19.1 %collective-permute-done.1.images_ref = bf16[8,256,256]{2,1,0:T(8,128)(2,1)} collective-permute-done((bf16[8,256,256]{2,1,0:T(8,128)(2,1)}, bf16[8,256,256]{2,1,0:T(8,128)(2,1)}, u32[]{:S(2)}, u32[]{:S(2)}) %collective-permute-start.1) | collective-permute-done | bytes 1048608 | tf_op jit(solution)/shard_map/ppermute | solution.py:18
  44.0 1.4 %collective-permute-done.2.images_ref = bf16[8,256,256]{2,1,0:T(8,128)(2,1)} collective-permute-done((bf16[8,256,256]{2,1,0:T(8,128)(2,1)}, bf16[8,256,256]{2,1,0:T(8,128)(2,1)}, u32[]{:S(2)}, u32[]{:S(2)}) %collective-permute-start.2) | collective-permute-done | bytes 1048608 | tf_op jit(solution)/shard_map/ppermute | solution.py:18
  45.5 2.6 %spectra.1.fields_ref = bf16[16,2,256,256]{3,2,1,0:T(8,128)(2,1)S(1)} custom-call(bf16[16,256,256]{2,1,0:T(8,128)(2,1)S(1)} %bitcast.69, bf16[256,256]{1,0:T(8,128)(2,1)S(1)} %copy-done.2, bf16[512,256]{1,0:T(8,128)(2,1)S(1)} %copy-done.1), custom_call_target="tpu_custom_call" | custom-call | flops 1610612736 | bytes 6291456 | tf_op jit(solution)/shard_map/spectra/pallas_call | solution.py:136
  48.1 0.1 broadcast_in_dim.16.offsets_ref
  48.3 4.2 %pair_sums.3 = f32[8,8,256]{2,1,0:T(8,128)S(1)} custom-call(bf16[8,256,256]{2,1,0:T(8,128)(2,1)} %collective-permute-done.2.images_ref, bf16[16,2,256,256]{3,2,1,0:T(8,128)(2,1)S(1)} %spectra.1.fields_ref, bf16[256,256]{1,0:T(8,128)(2,1)S(1)} %copy-done.2, bf16[512,256]{1,0:T(8,128)(2,1)S(1)} %copy-done.1, bf16[256,256]{1,0:T(8,128)(2,1)S(1)} %copy-done.3, ...), custom_call_target="tpu_custom_call" | custom-call | flops 1610612736 | bytes 3145728 | tf_op jit(solution)/shard_map/pair_sums/pallas_call | solution.py:158
  52.5 4.3 %pair_sums.2 = f32[8,8,256]{2,1,0:T(8,128)S(1)} custom-call(bf16[8,256,256]{2,1,0:T(8,128)(2,1)} %collective-permute-done.1.images_ref, bf16[16,2,256,256]{3,2,1,0:T(8,128)(2,1)S(1)} %spectra.1.fields_ref, bf16[256,256]{1,0:T(8,128)(2,1)S(1)} %copy-done.2, bf16[512,256]{1,0:T(8,128)(2,1)S(1)} %copy-done.1, bf16[256,256]{1,0:T(8,128)(2,1)S(1)} %copy-done.3, ...), custom_call_target="tpu_custom_call" | custom-call | flops 1610612736 | bytes 3145728 | tf_op jit(solution)/shard_map/pair_sums/pallas_call | solution.py:158
  56.8 0.2 slice_reduce_fusion
  56.9 0.1 fusion.2
  57.1 0.6 collective-permute-start.3
  57.7 2.5 %collective-permute-done.3 = f32[2,8]{1,0:T(2,128)S(1)} collective-permute-done((f32[2,8]{1,0:T(2,128)S(1)}, f32[2,8]{1,0:T(2,128)S(1)}, u32[]{:S(2)}, u32[]{:S(2)}) %collective-permute-start.3) | collective-permute-done | bytes 96 | tf_op jit(solution)/shard_map/ppermute | solution.py:18
  60.2 0.1 multiply_add_fusion.1
  60.3 9.0 %all-to-all-done.lines_ref = bf16[32,33,16,128]{3,2,1,0:T(8,128)(2,1)} async-done(((bf16[32,33,16,128]{3,2,1,0:T(8,128)(2,1)}), bf16[32,33,16,128]{3,2,1,0:T(8,128)(2,1)}, u32[]{:S(2)}, u32[]{:S(2)}) %all-to-all-start) | async-done | bytes 4325408 | tf_op jit(solution)/shard_map/all_to_all | solution.py:433
  69.3 10.9 %moments.1 = bf16[32,16,128]{2,1,0:T(8,128)(2,1)} custom-call(s32[512]{0:T(512)S(1)} %bitcast.71, s32[1]{0:T(128)} %bitcast.1.place_ref, bf16[32,33,16,128]{3,2,1,0:T(8,128)(2,1)} %all-to-all-done.lines_ref, bf16[512,512]{1,0:T(8,128)(2,1)S(1)} %copy-done.4, bf16[256,512]{1,0:T(8,128)(2,1)S(1)} %copy-done.5, f32[8,256]{1,0:T(8,128)S(1)} %copy-done.6, ...), custom_call_target="tpu_custom_call" | custom-call | flops 4294967296 | bytes 4325376 | tf_op jit(solution)/shard_map/moments/pallas_call | solution.py:414
  80.3 7.2 %all-to-all-start.1 = ((bf16[32,16,128]{2,1,0:T(8,128)(2,1)}), bf16[32,16,128]{2,1,0:T(8,128)(2,1)S(1)}, u32[]{:S(2)}, u32[]{:S(2)}) async-start(bf16[32,16,128]{2,1,0:T(8,128)(2,1)} %moments.1), calls=%async_computation.1 | async-start | bytes 262144 | tf_op jit(solution)/shard_map/all_to_all | solution.py:433
  87.5 0.1 fusion.22
  87.6 0.1 reshape.212
  87.7 7.5 %all-to-all-done.1.shares_ref = bf16[32,16,128]{2,1,0:T(8,128)(2,1)S(1)} async-done(((bf16[32,16,128]{2,1,0:T(8,128)(2,1)}), bf16[32,16,128]{2,1,0:T(8,128)(2,1)S(1)}, u32[]{:S(2)}, u32[]{:S(2)}) %all-to-all-start.1) | async-done | bytes 131104 | tf_op jit(solution)/shard_map/all_to_all | solution.py:433
  95.2 0.1 copy.25
  95.4 0.1 constant_dynamic-slice_fusion
  95.5 2.5 %collective-permute-start.4 = (f32[2,16]{1,0:T(2,128)S(1)}, f32[2,16]{1,0:T(2,128)S(1)}, u32[]{:S(2)}, u32[]{:S(2)}) collective-permute-start(f32[2,16]{1,0:T(2,128)S(1)} %constant_dynamic-slice_fusion), channel_id=1, source_target_pairs={{0,96},{32,0},{64,32},{96,64},{1,97},{33,1},{65,33},{97,65},{2,98}... | collective-permute-start | bytes 392 | tf_op jit(solution)/shard_map/ppermute | solution.py:18
  98.0 0.6 gather_fusion
  98.6 0.1 copy.26
  98.7 0.6 fusion.9
  (41 shorter events, 0.2 us)
Async XLA Ops:
  5.7 9.8 %copy-start.10 = (f32[2,1,16]{2,1,0:T(1,128)S(1)}, f32[2,1,16]{2,1,0:T(1,128)}, u32[]{:S(2)}) copy-start(f32[2,1,16]{2,1,0:T(1,128)} %param.20) | copy-start | bytes 388
  5.7 12.4 %copy-start = (bf16[1,16,256,256]{3,2,1,0:T(8,128)(2,1)S(1)}, bf16[1,16,256,256]{3,2,1,0:T(8,128)(2,1)}, u32[]{:S(2)}) copy-start(bf16[1,16,256,256]{3,2,1,0:T(8,128)(2,1)} %param.16) | copy-start | bytes 6291460
  5.7 63.6 %all-to-all-start = ((bf16[32,33,16,128]{3,2,1,0:T(8,128)(2,1)}), bf16[32,33,16,128]{3,2,1,0:T(8,128)(2,1)}, u32[]{:S(2)}, u32[]{:S(2)}) async-start(bf16[32,33,16,128]{3,2,1,0:T(8,128)(2,1)} %lines.1), calls=%async_computation | async-start | bytes 8650752 | tf_op jit(solution)/shard_map/all_to_all | solution.py:433
  15.5 5.5 %copy-start.7 = (s32[6,1,16]{2,1,0:T(1,128)S(1)}, s32[6,1,16]{2,1,0:T(1,128)}, u32[]{:S(2)}) copy-start(s32[6,1,16]{2,1,0:T(1,128)} %param.19) | copy-start | bytes 1156
  15.5 5.5 %copy-start.11 = (s32[1,512]{1,0:T(1,128)S(1)}, s32[1,512]{1,0:T(1,128)}, u32[]{:S(2)}) copy-start(s32[1,512]{1,0:T(1,128)} %param.18) | copy-start | bytes 6148
  15.6 5.5 %copy-start.12 = (s32[1,512]{1,0:T(1,128)S(1)}, s32[1,512]{1,0:T(1,128)}, u32[]{:S(2)}) copy-start(s32[1,512]{1,0:T(1,128)} %param.17) | copy-start | bytes 6148
  15.6 29.9 %copy-start.1 = (bf16[512,256]{1,0:T(8,128)(2,1)S(1)}, bf16[512,256]{1,0:T(8,128)(2,1)}, u32[]{:S(2)}) copy-start(bf16[512,256]{1,0:T(8,128)(2,1)} %constant.50.clone.both_ref) | copy-start | bytes 786436
  15.6 29.9 %copy-start.2 = (bf16[256,256]{1,0:T(8,128)(2,1)S(1)}, bf16[256,256]{1,0:T(8,128)(2,1)}, u32[]{:S(2)}) copy-start(bf16[256,256]{1,0:T(8,128)(2,1)} %constant.49.clone.to_half_ref) | copy-start | bytes 393220
  15.6 42.1 %collective-permute-start = (f32[2,16]{1,0:T(2,128)S(1)}, f32[2,16]{1,0:T(2,128)S(1)}, u32[]{:S(2)}, u32[]{:S(2)}) collective-permute-start(f32[2,16]{1,0:T(2,128)S(1)} %bitcast.77), channel_id=1, source_target_pairs={{0,96},{32,0},{64,32},{96,64},{1,97},{33,1},{65,33},{97,65},{2,98}... | collective-permute-start | bytes 392 | tf_op jit(solution)/shard_map/ppermute | solution.py:18
  19.6 24.4 %collective-permute-start.1 = (bf16[8,256,256]{2,1,0:T(8,128)(2,1)}, bf16[8,256,256]{2,1,0:T(8,128)(2,1)}, u32[]{:S(2)}, u32[]{:S(2)}) collective-permute-start(bf16[8,256,256]{2,1,0:T(8,128)(2,1)} %get-tuple-element.26), channel_id=1, source_target_pairs={{0,96},{32,0},{64,32},{96,64},{1,97},{33,1},{65,33},{97,65},{2,98}... | collective-permute-start | bytes 3145736 | tf_op jit(solution)/shard_map/ppermute | solution.py:18
  20.1 25.3 %collective-permute-start.2 = (bf16[8,256,256]{2,1,0:T(8,128)(2,1)}, bf16[8,256,256]{2,1,0:T(8,128)(2,1)}, u32[]{:S(2)}, u32[]{:S(2)}) collective-permute-start(bf16[8,256,256]{2,1,0:T(8,128)(2,1)} %get-tuple-element.25), channel_id=1, source_target_pairs={{0,32},{32,64},{64,96},{96,0},{1,33},{33,65},{65,97},{97,1},{2,34}... | collective-permute-start | bytes 3145736 | tf_op jit(solution)/shard_map/ppermute | solution.py:18
  24.9 23.2 %copy-start.8 = (f32[256]{0:T(256)S(1)}, f32[256]{0:T(256)}, u32[]{:S(2)}) copy-start(f32[256]{0:T(256)} %constant.54.clone) | copy-start | bytes 3076
  25.0 23.3 %copy-start.3 = (bf16[256,256]{1,0:T(8,128)(2,1)S(1)}, bf16[256,256]{1,0:T(8,128)(2,1)}, u32[]{:S(2)}) copy-start(bf16[256,256]{1,0:T(8,128)(2,1)} %constant.51.clone.from_half_ref) | copy-start | bytes 393220
  52.5 16.8 %copy-start.4 = (bf16[512,512]{1,0:T(8,128)(2,1)S(1)}, bf16[512,512]{1,0:T(8,128)(2,1)}, u32[]{:S(2)}) copy-start(bf16[512,512]{1,0:T(8,128)(2,1)} %fusion.chosen_ref) | copy-start | bytes 1572868
  52.5 16.8 %copy-start.5 = (bf16[256,512]{1,0:T(8,128)(2,1)S(1)}, bf16[256,512]{1,0:T(8,128)(2,1)}, u32[]{:S(2)}) copy-start(bf16[256,512]{1,0:T(8,128)(2,1)} %constant.71.both_ref) | copy-start | bytes 786436
  52.5 16.8 %copy-start.6 = (f32[8,256]{1,0:T(8,128)S(1)}, f32[8,256]{1,0:T(8,128)}, u32[]{:S(2)}) copy-start(f32[8,256]{1,0:T(8,128)} %constant.56.clone.weights_ref) | copy-start | bytes 24580
  57.1 3.1 %collective-permute-start.3 = (f32[2,8]{1,0:T(2,128)S(1)}, f32[2,8]{1,0:T(2,128)S(1)}, u32[]{:S(2)}, u32[]{:S(2)}) collective-permute-start(f32[2,8]{1,0:T(2,128)S(1)} %pad_maximum_fusion), channel_id=1, source_target_pairs={{0,96},{32,0},{64,32},{96,64},{1,97},{33,1},{65,33},{97,65},{2,98}... | collective-permute-start | bytes 200 | tf_op jit(solution)/shard_map/ppermute | solution.py:18
  60.3 38.4 %copy-start.9 = (f32[2,16]{1,0:T(2,128)}, f32[2,16]{1,0:T(2,128)S(1)}, u32[]{:S(2)}) copy-start(f32[2,16]{1,0:T(2,128)S(1)} %get-tuple-element.24) | copy-start | bytes 388
  80.3 14.9 %all-to-all-start.1 = ((bf16[32,16,128]{2,1,0:T(8,128)(2,1)}), bf16[32,16,128]{2,1,0:T(8,128)(2,1)S(1)}, u32[]{:S(2)}, u32[]{:S(2)}) async-start(bf16[32,16,128]{2,1,0:T(8,128)(2,1)} %moments.1), calls=%async_computation.1 | async-start | bytes 262144 | tf_op jit(solution)/shard_map/all_to_all | solution.py:433
  95.5 3.2 %collective-permute-start.4 = (f32[2,16]{1,0:T(2,128)S(1)}, f32[2,16]{1,0:T(2,128)S(1)}, u32[]{:S(2)}, u32[]{:S(2)}) collective-permute-start(f32[2,16]{1,0:T(2,128)S(1)} %constant_dynamic-slice_fusion), channel_id=1, source_target_pairs={{0,96},{32,0},{64,32},{96,64},{1,97},{33,1},{65,33},{97,65},{2,98}... | collective-permute-start | bytes 392 | tf_op jit(solution)/shard_map/ppermute | solution.py:18

commit v6 on v5

--- a/solution.py
+++ b/solution.py
@@ -302,7 +302,7 @@
             transform(step * unroll + k)
 
     def surfaces(tile):
-        at = pl.multiple_of(tile * count, count)
+        at = tile * count
         first = jnp.stack([spectra[partner_ref[at + k]] for k in range(count)], 0)
         first = first.astype(jnp.float32)
         second = spectra[pl.ds(at, count)].astype(jnp.float32)
@@ -314,10 +314,8 @@
         imag = mixed[:, :half, length:] + mixed[:, half:, :length]
         profile[pl.ds(at, count), :] = jnp.sum((real * real + imag * imag) * scale, axis=1)
 
-    @pl.loop(0, tiles // unroll)
-    def _(step):
-        for k in range(unroll):
-            surfaces(step * unroll + k)
+    for tile in range(tiles):
+        surfaces(tile)
 
     second = extra[...]
     first = dot(chosen_ref[...], second)
@@ -328,16 +326,16 @@
     imag = dot((b * c - a * d).astype(jnp.bfloat16), both[:, length:])
     last = real - imag
     profile[...] += last * last * on_first.astype(jnp.float32)
-    sums = lax.dot_general(
-        weights_ref[...],
-        profile[...],
-        (((1,), (1,)), ((), ())),
-        precision=lax.Precision.HIGHEST,
-        preferred_element_type=jnp.float32,
-    )
-    linked = jnp.zeros((rows, columns), jnp.float32)
-    for tile in range(tiles):
-        linked += dot(lines_ref[tile, 2 * count], counts_ref[tile])
+    sums = jnp.zeros((weights_ref.shape[0], tiles * count), jnp.float32)
+    rest = profile[...]
+    for _ in range(3):
+        part = rest.astype(jnp.bfloat16)
+        rest = rest - part.astype(jnp.float32)
+        sums += lax.dot_general(
+            weights_ref[...], part, (((1,), (1,)), ((), ())), preferred_element_type=jnp.float32
+        )
+    notes = jnp.concatenate([lines_ref[tile, 2 * count] for tile in range(tiles)], 1)
+    linked = dot(notes, counts_ref[...])
     linked = (linked[4:6] + linked[2:4]) + linked[0:2]
     base = rest_ref[...] + relax_rate * linked
     width = count
@@ -401,13 +399,14 @@
     count, length = slots // 2, 2 * columns
     nodes = tiles * count
     chosen = (partner[:, None] == jnp.arange(nodes)).astype(jnp.bfloat16)
-    weights = np.zeros((8, length), np.float32)
+    weights = np.zeros((16, length), np.float32)
     weights[0] = 1.0
     weights[1] = offsets_of(length)
     lanes = np.arange(columns)
     sources = jnp.asarray(np.where(lanes < count, np.arange(tiles)[:, None] * count + lanes, -1))
     links = jnp.pad(links, ((0, 0), (0, columns - count)), constant_values=nodes)
-    counts = sum(sources[:, :, None] == links[k] for k in range(links.shape[0])).astype(jnp.bfloat16)
+    sources = sources.reshape(-1, 1)
+    counts = sum(sources == links[k] for k in range(links.shape[0])).astype(jnp.bfloat16)
     rest = jnp.pad(rest, ((0, 0), (0, columns - count)))
     vmem = pl.BlockSpec(memory_space=pltpu.VMEM)
     smem = pl.BlockSpec(memory_space=pltpu.SMEM)
@@ -426,7 +425,7 @@
             flops=nodes * rows * 4 * 2 * length**2, bytes_accessed=2 * lines.size, transcendentals=0
         ),
         name="moments",
-    )(partner, place[None], lines, chosen, both, jnp.asarray(weights), counts, rest)
+    )(partner, place[None], lines, chosen, both, jnp.asarray(weights, jnp.bfloat16), counts, rest)
 
 
 def exchange(x):

time: 100 us -> 99.3 us (level)
  Pallas kernels: 27.2 us -> 26.2 us
where the time goes in v6:
time: 99.3 us; the launch traced here: 98.4 us
  waiting for transfers between devices  39.5 us (40%)
  Pallas kernels  26.2 us (26%)
  starting transfers between devices  24.1 us (24%)
  other arithmetic  4.86 us (5%)
  local copies, waits for them, and re-layouts  2.82 us (3%)
    ppermute x5, waiting for transfers between devices, shifted(): lax.ppermute(x, axis, [(i, (i + by) % devices) for i in range(devices)])  23 us
    all_to_all x2, starting transfers between devices, exchange(): return lax.all_to_all(x, 'tile', split_axis=0, concat_axis=0, tiled=True)  17 us
    all_to_all x2, waiting for transfers between devices, exchange(): return lax.all_to_all(x, 'tile', split_axis=0, concat_axis=0, tiled=True)  16.5 us
    pallas_call x1, Pallas kernels, moments_of(): pl.pallas_call(moments_kernel, in_specs=[smem, smem, vmem, vmem, vmem, vm...  9.98 us
    pallas_call x2, Pallas kernels, pair_sums(): pl.pallas_call(functools.partial(pair_kernel, other_first), grid=(count /...  8.48 us
    ppermute x5, starting transfers between devices, shifted(): lax.ppermute(x, axis, [(i, (i + by) % devices) for i in range(devices)])  7.08 us
    pallas_call x1, Pallas kernels, lines_of(): pl.pallas_call(lines_kernel, in_specs=[pl.BlockSpec(memory_space=pl.ANY),...  5.06 us
    convert_element_type x1, other arithmetic, moments_of(): sum((sources == links[k] for k in range(links.shape[0])))  2.75 us
  transfers between devices with their start and end apart: 7, of which 5 were waited for; matrix products, arithmetic and copies ran while one was open for 7% of the time, Pallas kernels for 11%

profile of v6, /device:TPU:1, one launch (start us, length us, event | category | flops | bytes accessed | tf_op | source)
XLA Modules:
  0.0 98.4 jit_solution(7816308022601795656)
XLA Ops:
  0.6 5.1 %lines.1 = bf16[32,33,16,128]{3,2,1,0:T(8,128)(2,1)} custom-call(bf16[16,256,256]{2,1,0:T(8,128)(2,1)} %bitcast.68, f32[2,16]{1,0:T(2,128)} %bitcast.76, bf16[256,256]{1,0:T(8,128)(2,1)} %constant.68.table_ref), custom_call_target="tpu_custom_call" | custom-call | flops 1073741824 | bytes 6291456 | tf_op jit(solution)/shard_map/lines/pallas_call | solution.py:251
  5.7 9.8 %all-to-all-start = ((bf16[32,33,16,128]{3,2,1,0:T(8,128)(2,1)}), bf16[32,33,16,128]{3,2,1,0:T(8,128)(2,1)}, u32[]{:S(2)}, u32[]{:S(2)}) async-start(bf16[32,33,16,128]{3,2,1,0:T(8,128)(2,1)} %lines.1), calls=%async_computation | async-start | bytes 8650752 | tf_op jit(solution)/shard_map/all_to_all | solution.py:432
  15.6 2.5 %collective-permute-start = (f32[2,16]{1,0:T(2,128)S(1)}, f32[2,16]{1,0:T(2,128)S(1)}, u32[]{:S(2)}, u32[]{:S(2)}) collective-permute-start(f32[2,16]{1,0:T(2,128)S(1)} %bitcast.77), channel_id=1, source_target_pairs={{0,96},{32,0},{64,32},{96,64},{1,97},{33,1},{65,33},{97,65},{2,98}... | collective-permute-start | bytes 392 | tf_op jit(solution)/shard_map/ppermute | solution.py:18
  18.1 1.5 %slice_bitcast_fusion = (bf16[8,256,256]{2,1,0:T(8,128)(2,1)}, bf16[8,256,256]{2,1,0:T(8,128)(2,1)}) fusion(bf16[1,16,256,256]{3,2,1,0:T(8,128)(2,1)S(1)} %copy-done), kind=kLoop, calls=%fused_computation.2 | loop fusion | bytes 4194304 | tf_op jit(solution)/shard_map/slice | solution.py:454
  19.6 0.6 collective-permute-start.1
  20.1 0.9 collective-permute-start.2
  21.1 0.1 constant_dynamic-slice_fusion.2
  21.2 1.0 %fusion.chosen_ref = bf16[512,512]{1,0:T(8,128)(2,1)} fusion(s32[512]{0:T(512)S(1)} %bitcast.70), kind=kLoop, calls=%fused_computation.5 | loop fusion | flops 524288 | bytes 526336 | tf_op jit(solution)/shard_map/convert_element_type | solution.py:401
  22.2 2.7 %add_convert_fusion.counts_ref = bf16[4096,128]{1,0:T(8,128)(2,1)S(1)} fusion(s32[128]{0:T(128)S(1)} %get-tuple-element.37, s32[128]{0:T(128)S(1)} %get-tuple-element.36, s32[128]{0:T(128)S(1)} %get-tuple-element.35, s32[128]{0:T(128)S(1)} %get-tuple-element.34, s32[128]{0:T(128)S(1)} %get-tuple-element.33, s32[128]{0:T(128)S(1)} %get-tuple-element.32, ...), kind=kLoop, calls=%fused_computation.1 | loop fusion | flops 11010048 | bytes 1068544 | tf_op jit(solution)/shard_map/convert_element_type | solution.py:409
  25.0 19.1 %collective-permute-done.1.images_ref = bf16[8,256,256]{2,1,0:T(8,128)(2,1)} collective-permute-done((bf16[8,256,256]{2,1,0:T(8,128)(2,1)}, bf16[8,256,256]{2,1,0:T(8,128)(2,1)}, u32[]{:S(2)}, u32[]{:S(2)}) %collective-permute-start.1) | collective-permute-done | bytes 1048608 | tf_op jit(solution)/shard_map/ppermute | solution.py:18
  44.0 1.4 %collective-permute-done.2.images_ref = bf16[8,256,256]{2,1,0:T(8,128)(2,1)} collective-permute-done((bf16[8,256,256]{2,1,0:T(8,128)(2,1)}, bf16[8,256,256]{2,1,0:T(8,128)(2,1)}, u32[]{:S(2)}, u32[]{:S(2)}) %collective-permute-start.2) | collective-permute-done | bytes 1048608 | tf_op jit(solution)/shard_map/ppermute | solution.py:18
  45.5 2.6 %spectra.1.fields_ref = bf16[16,2,256,256]{3,2,1,0:T(8,128)(2,1)S(1)} custom-call(bf16[16,256,256]{2,1,0:T(8,128)(2,1)S(1)} %bitcast.69, bf16[256,256]{1,0:T(8,128)(2,1)S(1)} %copy-done.2, bf16[512,256]{1,0:T(8,128)(2,1)S(1)} %copy-done.1), custom_call_target="tpu_custom_call" | custom-call | flops 1610612736 | bytes 6291456 | tf_op jit(solution)/shard_map/spectra/pallas_call | solution.py:136
  48.1 0.1 broadcast_in_dim.16.offsets_ref
  48.3 4.2 %pair_sums.3 = f32[8,8,256]{2,1,0:T(8,128)S(1)} custom-call(bf16[8,256,256]{2,1,0:T(8,128)(2,1)} %collective-permute-done.2.images_ref, bf16[16,2,256,256]{3,2,1,0:T(8,128)(2,1)S(1)} %spectra.1.fields_ref, bf16[256,256]{1,0:T(8,128)(2,1)S(1)} %copy-done.2, bf16[512,256]{1,0:T(8,128)(2,1)S(1)} %copy-done.1, bf16[256,256]{1,0:T(8,128)(2,1)S(1)} %copy-done.3, ...), custom_call_target="tpu_custom_call" | custom-call | flops 1610612736 | bytes 3145728 | tf_op jit(solution)/shard_map/pair_sums/pallas_call | solution.py:158
  52.5 4.3 %pair_sums.2 = f32[8,8,256]{2,1,0:T(8,128)S(1)} custom-call(bf16[8,256,256]{2,1,0:T(8,128)(2,1)} %collective-permute-done.1.images_ref, bf16[16,2,256,256]{3,2,1,0:T(8,128)(2,1)S(1)} %spectra.1.fields_ref, bf16[256,256]{1,0:T(8,128)(2,1)S(1)} %copy-done.2, bf16[512,256]{1,0:T(8,128)(2,1)S(1)} %copy-done.1, bf16[256,256]{1,0:T(8,128)(2,1)S(1)} %copy-done.3, ...), custom_call_target="tpu_custom_call" | custom-call | flops 1610612736 | bytes 3145728 | tf_op jit(solution)/shard_map/pair_sums/pallas_call | solution.py:158
  56.8 0.2 slice_reduce_fusion
  56.9 0.1 fusion.2
  57.1 0.6 collective-permute-start.3
  57.7 2.5 %collective-permute-done.3 = f32[2,8]{1,0:T(2,128)S(1)} collective-permute-done((f32[2,8]{1,0:T(2,128)S(1)}, f32[2,8]{1,0:T(2,128)S(1)}, u32[]{:S(2)}, u32[]{:S(2)}) %collective-permute-start.3) | collective-permute-done | bytes 96 | tf_op jit(solution)/shard_map/ppermute | solution.py:18
  60.2 0.1 multiply_add_fusion.1
  60.3 9.0 %all-to-all-done.lines_ref = bf16[32,33,16,128]{3,2,1,0:T(8,128)(2,1)} async-done(((bf16[32,33,16,128]{3,2,1,0:T(8,128)(2,1)}), bf16[32,33,16,128]{3,2,1,0:T(8,128)(2,1)}, u32[]{:S(2)}, u32[]{:S(2)}) %all-to-all-start) | async-done | bytes 4325408 | tf_op jit(solution)/shard_map/all_to_all | solution.py:432
  69.3 10.0 %moments.1 = bf16[32,16,128]{2,1,0:T(8,128)(2,1)} custom-call(s32[512]{0:T(512)S(1)} %bitcast.71, s32[1]{0:T(128)} %bitcast.1.place_ref, bf16[32,33,16,128]{3,2,1,0:T(8,128)(2,1)} %all-to-all-done.lines_ref, bf16[512,512]{1,0:T(8,128)(2,1)S(1)} %copy-done.4, bf16[256,512]{1,0:T(8,128)(2,1)S(1)} %copy-done.5, bf16[16,256]{1,0:T(8,128)(2,1)S(1)} %copy-done.6, ...), custom_call_target="tpu_custom_call" | custom-call | flops 4294967296 | bytes 4325376 | tf_op jit(solution)/shard_map/moments/pallas_call | solution.py:413
  79.3 7.2 %all-to-all-start.1 = ((bf16[32,16,128]{2,1,0:T(8,128)(2,1)}), bf16[32,16,128]{2,1,0:T(8,128)(2,1)S(1)}, u32[]{:S(2)}, u32[]{:S(2)}) async-start(bf16[32,16,128]{2,1,0:T(8,128)(2,1)} %moments.1), calls=%async_computation.1 | async-start | bytes 262144 | tf_op jit(solution)/shard_map/all_to_all | solution.py:432
  86.5 0.1 fusion.22
  86.6 0.1 reshape.206
  86.7 7.5 %all-to-all-done.1.shares_ref = bf16[32,16,128]{2,1,0:T(8,128)(2,1)S(1)} async-done(((bf16[32,16,128]{2,1,0:T(8,128)(2,1)}), bf16[32,16,128]{2,1,0:T(8,128)(2,1)S(1)}, u32[]{:S(2)}, u32[]{:S(2)}) %all-to-all-start.1) | async-done | bytes 131104 | tf_op jit(solution)/shard_map/all_to_all | solution.py:432
  94.3 0.1 copy.25
  94.5 0.1 constant_dynamic-slice_fusion
  94.5 2.5 %collective-permute-start.4 = (f32[2,16]{1,0:T(2,128)S(1)}, f32[2,16]{1,0:T(2,128)S(1)}, u32[]{:S(2)}, u32[]{:S(2)}) collective-permute-start(f32[2,16]{1,0:T(2,128)S(1)} %constant_dynamic-slice_fusion), channel_id=1, source_target_pairs={{0,96},{32,0},{64,32},{96,64},{1,97},{33,1},{65,33},{97,65},{2,98}... | collective-permute-start | bytes 392 | tf_op jit(solution)/shard_map/ppermute | solution.py:18
  97.0 0.6 gather_fusion
  97.7 0.1 copy.26
  97.7 0.6 fusion.9
  (41 shorter events, 0.2 us)
Async XLA Ops:
  5.7 9.8 %copy-start.10 = (f32[2,1,16]{2,1,0:T(1,128)S(1)}, f32[2,1,16]{2,1,0:T(1,128)}, u32[]{:S(2)}) copy-start(f32[2,1,16]{2,1,0:T(1,128)} %param.20) | copy-start | bytes 388
  5.7 12.4 %copy-start = (bf16[1,16,256,256]{3,2,1,0:T(8,128)(2,1)S(1)}, bf16[1,16,256,256]{3,2,1,0:T(8,128)(2,1)}, u32[]{:S(2)}) copy-start(bf16[1,16,256,256]{3,2,1,0:T(8,128)(2,1)} %param.16) | copy-start | bytes 6291460
  5.7 63.6 %all-to-all-start = ((bf16[32,33,16,128]{3,2,1,0:T(8,128)(2,1)}), bf16[32,33,16,128]{3,2,1,0:T(8,128)(2,1)}, u32[]{:S(2)}, u32[]{:S(2)}) async-start(bf16[32,33,16,128]{3,2,1,0:T(8,128)(2,1)} %lines.1), calls=%async_computation | async-start | bytes 8650752 | tf_op jit(solution)/shard_map/all_to_all | solution.py:432
  15.5 5.5 %copy-start.7 = (s32[6,1,16]{2,1,0:T(1,128)S(1)}, s32[6,1,16]{2,1,0:T(1,128)}, u32[]{:S(2)}) copy-start(s32[6,1,16]{2,1,0:T(1,128)} %param.19) | copy-start | bytes 1156
  15.5 5.5 %copy-start.11 = (s32[1,512]{1,0:T(1,128)S(1)}, s32[1,512]{1,0:T(1,128)}, u32[]{:S(2)}) copy-start(s32[1,512]{1,0:T(1,128)} %param.18) | copy-start | bytes 6148
  15.6 5.5 %copy-start.12 = (s32[1,512]{1,0:T(1,128)S(1)}, s32[1,512]{1,0:T(1,128)}, u32[]{:S(2)}) copy-start(s32[1,512]{1,0:T(1,128)} %param.17) | copy-start | bytes 6148
  15.6 29.9 %copy-start.1 = (bf16[512,256]{1,0:T(8,128)(2,1)S(1)}, bf16[512,256]{1,0:T(8,128)(2,1)}, u32[]{:S(2)}) copy-start(bf16[512,256]{1,0:T(8,128)(2,1)} %constant.50.clone.both_ref) | copy-start | bytes 786436
  15.6 29.9 %copy-start.2 = (bf16[256,256]{1,0:T(8,128)(2,1)S(1)}, bf16[256,256]{1,0:T(8,128)(2,1)}, u32[]{:S(2)}) copy-start(bf16[256,256]{1,0:T(8,128)(2,1)} %constant.49.clone.to_half_ref) | copy-start | bytes 393220
  15.6 42.1 %collective-permute-start = (f32[2,16]{1,0:T(2,128)S(1)}, f32[2,16]{1,0:T(2,128)S(1)}, u32[]{:S(2)}, u32[]{:S(2)}) collective-permute-start(f32[2,16]{1,0:T(2,128)S(1)} %bitcast.77), channel_id=1, source_target_pairs={{0,96},{32,0},{64,32},{96,64},{1,97},{33,1},{65,33},{97,65},{2,98}... | collective-permute-start | bytes 392 | tf_op jit(solution)/shard_map/ppermute | solution.py:18
  19.6 24.4 %collective-permute-start.1 = (bf16[8,256,256]{2,1,0:T(8,128)(2,1)}, bf16[8,256,256]{2,1,0:T(8,128)(2,1)}, u32[]{:S(2)}, u32[]{:S(2)}) collective-permute-start(bf16[8,256,256]{2,1,0:T(8,128)(2,1)} %get-tuple-element.26), channel_id=1, source_target_pairs={{0,96},{32,0},{64,32},{96,64},{1,97},{33,1},{65,33},{97,65},{2,98}... | collective-permute-start | bytes 3145736 | tf_op jit(solution)/shard_map/ppermute | solution.py:18
  20.1 25.3 %collective-permute-start.2 = (bf16[8,256,256]{2,1,0:T(8,128)(2,1)}, bf16[8,256,256]{2,1,0:T(8,128)(2,1)}, u32[]{:S(2)}, u32[]{:S(2)}) collective-permute-start(bf16[8,256,256]{2,1,0:T(8,128)(2,1)} %get-tuple-element.25), channel_id=1, source_target_pairs={{0,32},{32,64},{64,96},{96,0},{1,33},{33,65},{65,97},{97,1},{2,34}... | collective-permute-start | bytes 3145736 | tf_op jit(solution)/shard_map/ppermute | solution.py:18
  24.9 23.2 %copy-start.8 = (f32[256]{0:T(256)S(1)}, f32[256]{0:T(256)}, u32[]{:S(2)}) copy-start(f32[256]{0:T(256)} %constant.54.clone) | copy-start | bytes 3076
  25.0 23.3 %copy-start.3 = (bf16[256,256]{1,0:T(8,128)(2,1)S(1)}, bf16[256,256]{1,0:T(8,128)(2,1)}, u32[]{:S(2)}) copy-start(bf16[256,256]{1,0:T(8,128)(2,1)} %constant.51.clone.from_half_ref) | copy-start | bytes 393220
  52.5 16.8 %copy-start.4 = (bf16[512,512]{1,0:T(8,128)(2,1)S(1)}, bf16[512,512]{1,0:T(8,128)(2,1)}, u32[]{:S(2)}) copy-start(bf16[512,512]{1,0:T(8,128)(2,1)} %fusion.chosen_ref) | copy-start | bytes 1572868
  52.5 16.8 %copy-start.5 = (bf16[256,512]{1,0:T(8,128)(2,1)S(1)}, bf16[256,512]{1,0:T(8,128)(2,1)}, u32[]{:S(2)}) copy-start(bf16[256,512]{1,0:T(8,128)(2,1)} %constant.71.both_ref) | copy-start | bytes 786436
  52.5 16.8 %copy-start.6 = (bf16[16,256]{1,0:T(8,128)(2,1)S(1)}, bf16[16,256]{1,0:T(8,128)(2,1)}, u32[]{:S(2)}) copy-start(bf16[16,256]{1,0:T(8,128)(2,1)} %constant.56.clone.weights_ref) | copy-start | bytes 24580
  57.1 3.1 %collective-permute-start.3 = (f32[2,8]{1,0:T(2,128)S(1)}, f32[2,8]{1,0:T(2,128)S(1)}, u32[]{:S(2)}, u32[]{:S(2)}) collective-permute-start(f32[2,8]{1,0:T(2,128)S(1)} %pad_maximum_fusion), channel_id=1, source_target_pairs={{0,96},{32,0},{64,32},{96,64},{1,97},{33,1},{65,33},{97,65},{2,98}... | collective-permute-start | bytes 200 | tf_op jit(solution)/shard_map/ppermute | solution.py:18
  60.3 37.5 %copy-start.9 = (f32[2,16]{1,0:T(2,128)}, f32[2,16]{1,0:T(2,128)S(1)}, u32[]{:S(2)}) copy-start(f32[2,16]{1,0:T(2,128)S(1)} %get-tuple-element.24) | copy-start | bytes 388
  79.3 14.9 %all-to-all-start.1 = ((bf16[32,16,128]{2,1,0:T(8,128)(2,1)}), bf16[32,16,128]{2,1,0:T(8,128)(2,1)S(1)}, u32[]{:S(2)}, u32[]{:S(2)}) async-start(bf16[32,16,128]{2,1,0:T(8,128)(2,1)} %moments.1), calls=%async_computation.1 | async-start | bytes 262144 | tf_op jit(solution)/shard_map/all_to_all | solution.py:432
  94.5 3.2 %collective-permute-start.4 = (f32[2,16]{1,0:T(2,128)S(1)}, f32[2,16]{1,0:T(2,128)S(1)}, u32[]{:S(2)}, u32[]{:S(2)}) collective-permute-start(f32[2,16]{1,0:T(2,128)S(1)} %constant_dynamic-slice_fusion), channel_id=1, source_target_pairs={{0,96},{32,0},{64,32},{96,64},{1,97},{33,1},{65,33},{97,65},{2,98}... | collective-permute-start | bytes 392 | tf_op jit(solution)/shard_map/ppermute | solution.py:18

commit v7 on v6

--- a/solution.py
+++ b/solution.py
@@ -301,6 +301,18 @@
         for k in range(unroll):
             transform(step * unroll + k)
 
+    second = extra[...]
+    first = dot(chosen_ref[...], second)
+    second = second.astype(jnp.float32)
+    a, b = first[:, :length], first[:, length:]
+    c, d = second[:, :length], second[:, length:]
+    real = dot((a * c + b * d).astype(jnp.bfloat16), both[:, :length])
+    imag = dot((b * c - a * d).astype(jnp.bfloat16), both[:, length:])
+    last = real - imag
+    profile[...] = last * last * on_first.astype(jnp.float32)
+    notes = jnp.concatenate([lines_ref[tile, 2 * count] for tile in range(tiles)], 1)
+    linked = dot(notes, counts_ref[...])
+
     def surfaces(tile):
         at = tile * count
         first = jnp.stack([spectra[partner_ref[at + k]] for k in range(count)], 0)
@@ -312,20 +324,11 @@
         mixed = dot(cross.reshape(count * rows, length), both).reshape(count, rows, 2 * length)
         real = mixed[:, :half, :length] - mixed[:, half:, length:]
         imag = mixed[:, :half, length:] + mixed[:, half:, :length]
-        profile[pl.ds(at, count), :] = jnp.sum((real * real + imag * imag) * scale, axis=1)
+        profile[pl.ds(at, count), :] += jnp.sum((real * real + imag * imag) * scale, axis=1)
 
     for tile in range(tiles):
         surfaces(tile)
 
-    second = extra[...]
-    first = dot(chosen_ref[...], second)
-    second = second.astype(jnp.float32)
-    a, b = first[:, :length], first[:, length:]
-    c, d = second[:, :length], second[:, length:]
-    real = dot((a * c + b * d).astype(jnp.bfloat16), both[:, :length])
-    imag = dot((b * c - a * d).astype(jnp.bfloat16), both[:, length:])
-    last = real - imag
-    profile[...] += last * last * on_first.astype(jnp.float32)
     sums = jnp.zeros((weights_ref.shape[0], tiles * count), jnp.float32)
     rest = profile[...]
     for _ in range(3):
@@ -334,8 +337,6 @@
         sums += lax.dot_general(
             weights_ref[...], part, (((1,), (1,)), ((), ())), preferred_element_type=jnp.float32
         )
-    notes = jnp.concatenate([lines_ref[tile, 2 * count] for tile in range(tiles)], 1)
-    linked = dot(notes, counts_ref[...])
     linked = (linked[4:6] + linked[2:4]) + linked[0:2]
     base = rest_ref[...] + relax_rate * linked
     width = count

time: 99.3 us -> 99.2 us (level)
  no operation moved by 1% of the time
where the time goes in v7:
time: 99.2 us; the launch traced here: 98.3 us
  waiting for transfers between devices  39.5 us (40%)
  Pallas kernels  26.1 us (26%)
  starting transfers between devices  24.1 us (24%)
  other arithmetic  4.86 us (5%)
  local copies, waits for them, and re-layouts  2.82 us (3%)
    ppermute x5, waiting for transfers between devices, shifted(): lax.ppermute(x, axis, [(i, (i + by) % devices) for i in range(devices)])  23 us
    all_to_all x2, starting transfers between devices, exchange(): return lax.all_to_all(x, 'tile', split_axis=0, concat_axis=0, tiled=True)  17 us
    all_to_all x2, waiting for transfers between devices, exchange(): return lax.all_to_all(x, 'tile', split_axis=0, concat_axis=0, tiled=True)  16.5 us
    pallas_call x1, Pallas kernels, moments_of(): pl.pallas_call(moments_kernel, in_specs=[smem, smem, vmem, vmem, vmem, vm...  9.86 us
    pallas_call x2, Pallas kernels, pair_sums(): pl.pallas_call(functools.partial(pair_kernel, other_first), grid=(count /...  8.48 us
    ppermute x5, starting transfers between devices, shifted(): lax.ppermute(x, axis, [(i, (i + by) % devices) for i in range(devices)])  7.11 us
    pallas_call x1, Pallas kernels, lines_of(): pl.pallas_call(lines_kernel, in_specs=[pl.BlockSpec(memory_space=pl.ANY),...  5.06 us
    convert_element_type x1, other arithmetic, moments_of(): sum((sources == links[k] for k in range(links.shape[0])))  2.75 us
  transfers between devices with their start and end apart: 7, of which 5 were waited for; matrix products, arithmetic and copies ran while one was open for 7% of the time, Pallas kernels for 11%

profile of v7, /device:TPU:1, one launch (start us, length us, event | category | flops | bytes accessed | tf_op | source)
XLA Modules:
  0.0 98.3 jit_solution(8052683391945335757)
XLA Ops:
  0.6 5.1 %lines.1 = bf16[32,33,16,128]{3,2,1,0:T(8,128)(2,1)} custom-call(bf16[16,256,256]{2,1,0:T(8,128)(2,1)} %bitcast.68, f32[2,16]{1,0:T(2,128)} %bitcast.76, bf16[256,256]{1,0:T(8,128)(2,1)} %constant.68.table_ref), custom_call_target="tpu_custom_call" | custom-call | flops 1073741824 | bytes 6291456 | tf_op jit(solution)/shard_map/lines/pallas_call | solution.py:251
  5.7 9.8 %all-to-all-start = ((bf16[32,33,16,128]{3,2,1,0:T(8,128)(2,1)}), bf16[32,33,16,128]{3,2,1,0:T(8,128)(2,1)}, u32[]{:S(2)}, u32[]{:S(2)}) async-start(bf16[32,33,16,128]{3,2,1,0:T(8,128)(2,1)} %lines.1), calls=%async_computation | async-start | bytes 8650752 | tf_op jit(solution)/shard_map/all_to_all | solution.py:433
  15.6 2.5 %collective-permute-start = (f32[2,16]{1,0:T(2,128)S(1)}, f32[2,16]{1,0:T(2,128)S(1)}, u32[]{:S(2)}, u32[]{:S(2)}) collective-permute-start(f32[2,16]{1,0:T(2,128)S(1)} %bitcast.77), channel_id=1, source_target_pairs={{0,96},{32,0},{64,32},{96,64},{1,97},{33,1},{65,33},{97,65},{2,98}... | collective-permute-start | bytes 392 | tf_op jit(solution)/shard_map/ppermute | solution.py:18
  18.1 1.5 %slice_bitcast_fusion = (bf16[8,256,256]{2,1,0:T(8,128)(2,1)}, bf16[8,256,256]{2,1,0:T(8,128)(2,1)}) fusion(bf16[1,16,256,256]{3,2,1,0:T(8,128)(2,1)S(1)} %copy-done), kind=kLoop, calls=%fused_computation.2 | loop fusion | bytes 4194304 | tf_op jit(solution)/shard_map/slice | solution.py:455
  19.6 0.6 collective-permute-start.1
  20.1 0.9 collective-permute-start.2
  21.1 0.1 constant_dynamic-slice_fusion.2
  21.2 1.0 %fusion.chosen_ref = bf16[512,512]{1,0:T(8,128)(2,1)} fusion(s32[512]{0:T(512)S(1)} %bitcast.70), kind=kLoop, calls=%fused_computation.5 | loop fusion | flops 524288 | bytes 526336 | tf_op jit(solution)/shard_map/convert_element_type | solution.py:402
  22.2 2.7 %add_convert_fusion.counts_ref = bf16[4096,128]{1,0:T(8,128)(2,1)S(1)} fusion(s32[128]{0:T(128)S(1)} %get-tuple-element.37, s32[128]{0:T(128)S(1)} %get-tuple-element.36, s32[128]{0:T(128)S(1)} %get-tuple-element.35, s32[128]{0:T(128)S(1)} %get-tuple-element.34, s32[128]{0:T(128)S(1)} %get-tuple-element.33, s32[128]{0:T(128)S(1)} %get-tuple-element.32, ...), kind=kLoop, calls=%fused_computation.1 | loop fusion | flops 11010048 | bytes 1068544 | tf_op jit(solution)/shard_map/convert_element_type | solution.py:410
  25.0 19.1 %collective-permute-done.1.images_ref = bf16[8,256,256]{2,1,0:T(8,128)(2,1)} collective-permute-done((bf16[8,256,256]{2,1,0:T(8,128)(2,1)}, bf16[8,256,256]{2,1,0:T(8,128)(2,1)}, u32[]{:S(2)}, u32[]{:S(2)}) %collective-permute-start.1) | collective-permute-done | bytes 1048608 | tf_op jit(solution)/shard_map/ppermute | solution.py:18
  44.0 1.4 %collective-permute-done.2.images_ref = bf16[8,256,256]{2,1,0:T(8,128)(2,1)} collective-permute-done((bf16[8,256,256]{2,1,0:T(8,128)(2,1)}, bf16[8,256,256]{2,1,0:T(8,128)(2,1)}, u32[]{:S(2)}, u32[]{:S(2)}) %collective-permute-start.2) | collective-permute-done | bytes 1048608 | tf_op jit(solution)/shard_map/ppermute | solution.py:18
  45.5 2.6 %spectra.1.fields_ref = bf16[16,2,256,256]{3,2,1,0:T(8,128)(2,1)S(1)} custom-call(bf16[16,256,256]{2,1,0:T(8,128)(2,1)S(1)} %bitcast.69, bf16[256,256]{1,0:T(8,128)(2,1)S(1)} %copy-done.2, bf16[512,256]{1,0:T(8,128)(2,1)S(1)} %copy-done.1), custom_call_target="tpu_custom_call" | custom-call | flops 1610612736 | bytes 6291456 | tf_op jit(solution)/shard_map/spectra/pallas_call | solution.py:136
  48.1 0.1 broadcast_in_dim.16.offsets_ref
  48.3 4.2 %pair_sums.3 = f32[8,8,256]{2,1,0:T(8,128)S(1)} custom-call(bf16[8,256,256]{2,1,0:T(8,128)(2,1)} %collective-permute-done.2.images_ref, bf16[16,2,256,256]{3,2,1,0:T(8,128)(2,1)S(1)} %spectra.1.fields_ref, bf16[256,256]{1,0:T(8,128)(2,1)S(1)} %copy-done.2, bf16[512,256]{1,0:T(8,128)(2,1)S(1)} %copy-done.1, bf16[256,256]{1,0:T(8,128)(2,1)S(1)} %copy-done.3, ...), custom_call_target="tpu_custom_call" | custom-call | flops 1610612736 | bytes 3145728 | tf_op jit(solution)/shard_map/pair_sums/pallas_call | solution.py:158
  52.5 4.3 %pair_sums.2 = f32[8,8,256]{2,1,0:T(8,128)S(1)} custom-call(bf16[8,256,256]{2,1,0:T(8,128)(2,1)} %collective-permute-done.1.images_ref, bf16[16,2,256,256]{3,2,1,0:T(8,128)(2,1)S(1)} %spectra.1.fields_ref, bf16[256,256]{1,0:T(8,128)(2,1)S(1)} %copy-done.2, bf16[512,256]{1,0:T(8,128)(2,1)S(1)} %copy-done.1, bf16[256,256]{1,0:T(8,128)(2,1)S(1)} %copy-done.3, ...), custom_call_target="tpu_custom_call" | custom-call | flops 1610612736 | bytes 3145728 | tf_op jit(solution)/shard_map/pair_sums/pallas_call | solution.py:158
  56.8 0.2 slice_reduce_fusion
  56.9 0.1 fusion.2
  57.1 0.6 collective-permute-start.3
  57.7 2.5 %collective-permute-done.3 = f32[2,8]{1,0:T(2,128)S(1)} collective-permute-done((f32[2,8]{1,0:T(2,128)S(1)}, f32[2,8]{1,0:T(2,128)S(1)}, u32[]{:S(2)}, u32[]{:S(2)}) %collective-permute-start.3) | collective-permute-done | bytes 96 | tf_op jit(solution)/shard_map/ppermute | solution.py:18
  60.2 0.1 multiply_add_fusion.1
  60.3 9.0 %all-to-all-done.lines_ref = bf16[32,33,16,128]{3,2,1,0:T(8,128)(2,1)} async-done(((bf16[32,33,16,128]{3,2,1,0:T(8,128)(2,1)}), bf16[32,33,16,128]{3,2,1,0:T(8,128)(2,1)}, u32[]{:S(2)}, u32[]{:S(2)}) %all-to-all-start) | async-done | bytes 4325408 | tf_op jit(solution)/shard_map/all_to_all | solution.py:433
  69.3 9.9 %moments.1 = bf16[32,16,128]{2,1,0:T(8,128)(2,1)} custom-call(s32[512]{0:T(512)S(1)} %bitcast.71, s32[1]{0:T(128)} %bitcast.1.place_ref, bf16[32,33,16,128]{3,2,1,0:T(8,128)(2,1)} %all-to-all-done.lines_ref, bf16[512,512]{1,0:T(8,128)(2,1)S(1)} %copy-done.4, bf16[256,512]{1,0:T(8,128)(2,1)S(1)} %copy-done.5, bf16[16,256]{1,0:T(8,128)(2,1)S(1)} %copy-done.6, ...), custom_call_target="tpu_custom_call" | custom-call | flops 4294967296 | bytes 4325376 | tf_op jit(solution)/shard_map/moments/pallas_call | solution.py:414
  79.2 7.2 %all-to-all-start.1 = ((bf16[32,16,128]{2,1,0:T(8,128)(2,1)}), bf16[32,16,128]{2,1,0:T(8,128)(2,1)S(1)}, u32[]{:S(2)}, u32[]{:S(2)}) async-start(bf16[32,16,128]{2,1,0:T(8,128)(2,1)} %moments.1), calls=%async_computation.1 | async-start | bytes 262144 | tf_op jit(solution)/shard_map/all_to_all | solution.py:433
  86.4 0.1 fusion.22
  86.5 0.1 reshape.206
  86.6 7.5 %all-to-all-done.1.shares_ref = bf16[32,16,128]{2,1,0:T(8,128)(2,1)S(1)} async-done(((bf16[32,16,128]{2,1,0:T(8,128)(2,1)}), bf16[32,16,128]{2,1,0:T(8,128)(2,1)S(1)}, u32[]{:S(2)}, u32[]{:S(2)}) %all-to-all-start.1) | async-done | bytes 131104 | tf_op jit(solution)/shard_map/all_to_all | solution.py:433
  94.2 0.1 copy.25
  94.3 0.1 constant_dynamic-slice_fusion
  94.4 2.5 %collective-permute-start.4 = (f32[2,16]{1,0:T(2,128)S(1)}, f32[2,16]{1,0:T(2,128)S(1)}, u32[]{:S(2)}, u32[]{:S(2)}) collective-permute-start(f32[2,16]{1,0:T(2,128)S(1)} %constant_dynamic-slice_fusion), channel_id=1, source_target_pairs={{0,96},{32,0},{64,32},{96,64},{1,97},{33,1},{65,33},{97,65},{2,98}... | collective-permute-start | bytes 392 | tf_op jit(solution)/shard_map/ppermute | solution.py:18
  96.9 0.6 gather_fusion
  97.5 0.1 copy.26
  97.6 0.6 fusion.9
  (41 shorter events, 0.2 us)
Async XLA Ops:
  5.7 9.8 %copy-start.10 = (f32[2,1,16]{2,1,0:T(1,128)S(1)}, f32[2,1,16]{2,1,0:T(1,128)}, u32[]{:S(2)}) copy-start(f32[2,1,16]{2,1,0:T(1,128)} %param.20) | copy-start | bytes 388
  5.7 12.4 %copy-start = (bf16[1,16,256,256]{3,2,1,0:T(8,128)(2,1)S(1)}, bf16[1,16,256,256]{3,2,1,0:T(8,128)(2,1)}, u32[]{:S(2)}) copy-start(bf16[1,16,256,256]{3,2,1,0:T(8,128)(2,1)} %param.16) | copy-start | bytes 6291460
  5.7 63.6 %all-to-all-start = ((bf16[32,33,16,128]{3,2,1,0:T(8,128)(2,1)}), bf16[32,33,16,128]{3,2,1,0:T(8,128)(2,1)}, u32[]{:S(2)}, u32[]{:S(2)}) async-start(bf16[32,33,16,128]{3,2,1,0:T(8,128)(2,1)} %lines.1), calls=%async_computation | async-start | bytes 8650752 | tf_op jit(solution)/shard_map/all_to_all | solution.py:433
  15.5 5.5 %copy-start.7 = (s32[6,1,16]{2,1,0:T(1,128)S(1)}, s32[6,1,16]{2,1,0:T(1,128)}, u32[]{:S(2)}) copy-start(s32[6,1,16]{2,1,0:T(1,128)} %param.19) | copy-start | bytes 1156
  15.5 5.5 %copy-start.11 = (s32[1,512]{1,0:T(1,128)S(1)}, s32[1,512]{1,0:T(1,128)}, u32[]{:S(2)}) copy-start(s32[1,512]{1,0:T(1,128)} %param.18) | copy-start | bytes 6148
  15.6 5.5 %copy-start.12 = (s32[1,512]{1,0:T(1,128)S(1)}, s32[1,512]{1,0:T(1,128)}, u32[]{:S(2)}) copy-start(s32[1,512]{1,0:T(1,128)} %param.17) | copy-start | bytes 6148
  15.6 29.9 %copy-start.1 = (bf16[512,256]{1,0:T(8,128)(2,1)S(1)}, bf16[512,256]{1,0:T(8,128)(2,1)}, u32[]{:S(2)}) copy-start(bf16[512,256]{1,0:T(8,128)(2,1)} %constant.50.clone.both_ref) | copy-start | bytes 786436
  15.6 29.9 %copy-start.2 = (bf16[256,256]{1,0:T(8,128)(2,1)S(1)}, bf16[256,256]{1,0:T(8,128)(2,1)}, u32[]{:S(2)}) copy-start(bf16[256,256]{1,0:T(8,128)(2,1)} %constant.49.clone.to_half_ref) | copy-start | bytes 393220
  15.6 42.1 %collective-permute-start = (f32[2,16]{1,0:T(2,128)S(1)}, f32[2,16]{1,0:T(2,128)S(1)}, u32[]{:S(2)}, u32[]{:S(2)}) collective-permute-start(f32[2,16]{1,0:T(2,128)S(1)} %bitcast.77), channel_id=1, source_target_pairs={{0,96},{32,0},{64,32},{96,64},{1,97},{33,1},{65,33},{97,65},{2,98}... | collective-permute-start | bytes 392 | tf_op jit(solution)/shard_map/ppermute | solution.py:18
  19.6 24.4 %collective-permute-start.1 = (bf16[8,256,256]{2,1,0:T(8,128)(2,1)}, bf16[8,256,256]{2,1,0:T(8,128)(2,1)}, u32[]{:S(2)}, u32[]{:S(2)}) collective-permute-start(bf16[8,256,256]{2,1,0:T(8,128)(2,1)} %get-tuple-element.26), channel_id=1, source_target_pairs={{0,96},{32,0},{64,32},{96,64},{1,97},{33,1},{65,33},{97,65},{2,98}... | collective-permute-start | bytes 3145736 | tf_op jit(solution)/shard_map/ppermute | solution.py:18
  20.1 25.3 %collective-permute-start.2 = (bf16[8,256,256]{2,1,0:T(8,128)(2,1)}, bf16[8,256,256]{2,1,0:T(8,128)(2,1)}, u32[]{:S(2)}, u32[]{:S(2)}) collective-permute-start(bf16[8,256,256]{2,1,0:T(8,128)(2,1)} %get-tuple-element.25), channel_id=1, source_target_pairs={{0,32},{32,64},{64,96},{96,0},{1,33},{33,65},{65,97},{97,1},{2,34}... | collective-permute-start | bytes 3145736 | tf_op jit(solution)/shard_map/ppermute | solution.py:18
  24.9 23.2 %copy-start.8 = (f32[256]{0:T(256)S(1)}, f32[256]{0:T(256)}, u32[]{:S(2)}) copy-start(f32[256]{0:T(256)} %constant.54.clone) | copy-start | bytes 3076
  25.0 23.3 %copy-start.3 = (bf16[256,256]{1,0:T(8,128)(2,1)S(1)}, bf16[256,256]{1,0:T(8,128)(2,1)}, u32[]{:S(2)}) copy-start(bf16[256,256]{1,0:T(8,128)(2,1)} %constant.51.clone.from_half_ref) | copy-start | bytes 393220
  52.5 16.8 %copy-start.4 = (bf16[512,512]{1,0:T(8,128)(2,1)S(1)}, bf16[512,512]{1,0:T(8,128)(2,1)}, u32[]{:S(2)}) copy-start(bf16[512,512]{1,0:T(8,128)(2,1)} %fusion.chosen_ref) | copy-start | bytes 1572868
  52.5 16.8 %copy-start.5 = (bf16[256,512]{1,0:T(8,128)(2,1)S(1)}, bf16[256,512]{1,0:T(8,128)(2,1)}, u32[]{:S(2)}) copy-start(bf16[256,512]{1,0:T(8,128)(2,1)} %constant.71.both_ref) | copy-start | bytes 786436
  52.5 16.8 %copy-start.6 = (bf16[16,256]{1,0:T(8,128)(2,1)S(1)}, bf16[16,256]{1,0:T(8,128)(2,1)}, u32[]{:S(2)}) copy-start(bf16[16,256]{1,0:T(8,128)(2,1)} %constant.56.clone.weights_ref) | copy-start | bytes 24580
  57.1 3.1 %collective-permute-start.3 = (f32[2,8]{1,0:T(2,128)S(1)}, f32[2,8]{1,0:T(2,128)S(1)}, u32[]{:S(2)}, u32[]{:S(2)}) collective-permute-start(f32[2,8]{1,0:T(2,128)S(1)} %pad_maximum_fusion), channel_id=1, source_target_pairs={{0,96},{32,0},{64,32},{96,64},{1,97},{33,1},{65,33},{97,65},{2,98}... | collective-permute-start | bytes 200 | tf_op jit(solution)/shard_map/ppermute | solution.py:18
  60.3 37.4 %copy-start.9 = (f32[2,16]{1,0:T(2,128)}, f32[2,16]{1,0:T(2,128)S(1)}, u32[]{:S(2)}) copy-start(f32[2,16]{1,0:T(2,128)S(1)} %get-tuple-element.24) | copy-start | bytes 388
  79.2 14.9 %all-to-all-start.1 = ((bf16[32,16,128]{2,1,0:T(8,128)(2,1)}), bf16[32,16,128]{2,1,0:T(8,128)(2,1)S(1)}, u32[]{:S(2)}, u32[]{:S(2)}) async-start(bf16[32,16,128]{2,1,0:T(8,128)(2,1)} %moments.1), calls=%async_computation.1 | async-start | bytes 262144 | tf_op jit(solution)/shard_map/all_to_all | solution.py:433
  94.4 3.2 %collective-permute-start.4 = (f32[2,16]{1,0:T(2,128)S(1)}, f32[2,16]{1,0:T(2,128)S(1)}, u32[]{:S(2)}, u32[]{:S(2)}) collective-permute-start(f32[2,16]{1,0:T(2,128)S(1)} %constant_dynamic-slice_fusion), channel_id=1, source_target_pairs={{0,96},{32,0},{64,32},{96,64},{1,97},{33,1},{65,33},{97,65},{2,98}... | collective-permute-start | bytes 392 | tf_op jit(solution)/shard_map/ppermute | solution.py:18
